TPU v7x, 256 devices: a whole 4x4x8 slice. The times are simulated.
256 devices in a mesh: row: 16 (over y, x), col: 16 (over z, core).
Axes of the slice: x: 4, y: 4, z: 8, core: 2. Of those that a mesh axis runs over, the one named last changes fastest.
Arguments:
- external_field: float32 [3, 36, 8192], P(None, None, ('row', 'col')), may hold values from -6 to 6
- jitter: float32 [3, 8192], P(None, ('row', 'col')), may hold values from -0.3 to 0.3
- species: int32 [8192], P(('row', 'col')), may hold values from 0 to 3
- alpha_table: float32 [12, 4], replicated, may hold values from 0.1667 to 0.6667
- block_cell: int32 [256], replicated, may hold values from 0 to 255, as said below
- tile_map: int32 [256, 256], replicated, may hold values from 0 to 2, as said below
Outputs:
- dipoles: float32 [3, 36, 8192], P(None, None, ('row', 'col'))
- residual: float32 [3, 36, 8192], P(None, None, ('row', 'col'))
Inputs may be any that keep to these rules, and one draw needn't show every extreme that they name: block_cell holds each cell number of the block grid exactly once. tile_map[a, b] is 0 where the cells of blocks a and b differ by more than 2 along some grid dimension; otherwise it is 1 where a <= b and 2 where a > b.
All inputs are finite; a program needn't handle non-finite values.
Results may differ from a plain program's by a relative error of at most 0.0003.
Values sent between devices are 32-bit elements; how exact they have to be, the bound alone decides.
No kernel may reach another device: no remote copies, remote signals or barrier semaphores. Data moves between devices by JAX's collectives and lax.ppermute only.
A program may use at most 64 MiB of HBM per device.

v0:
```python
import jax
import jax.numpy as jnp
from jax import lax
from jax.sharding import PartitionSpec as P

FIELDS = 3
ITERS = 2


spacing = 2.0
radius = 2.4
steepness = 6.0


def grid_shape(number):
    exponent = number.bit_length() - 1
    along_x = (exponent + 2) // 3
    remaining = exponent - along_x
    along_y = (remaining + 1) // 2
    return (2**along_x, 2**along_y, 2 ** (remaining - along_y))


def lattice(cell_ids, atom_total, block_total):
    grid_x, grid_y, grid_z = grid_shape(block_total)
    sub_x, sub_y, sub_z = grid_shape(atom_total)
    local_ids = jnp.arange(atom_total, dtype=jnp.int32)[None, :]
    column = cell_ids[:, None]
    coord_x = column // (grid_y * grid_z) * sub_x + local_ids // (sub_y * sub_z)
    coord_y = column // grid_z % grid_y * sub_y + local_ids // sub_z % sub_y
    coord_z = column % grid_z * sub_z + local_ids % sub_z
    return jnp.stack([coord_x, coord_y, coord_z]).astype(jnp.float32) * spacing


def coupling_wide(row_place, col_place, self_mask):
    offset = row_place[:, :, None] - col_place[:, None, :]
    distance2 = jnp.sum(offset * offset, axis=0) + self_mask
    inverse = lax.rsqrt(distance2)
    damping = 1.0 / (1.0 + jnp.exp(-steepness * (distance2 * inverse / radius - 1.0)))
    weight = damping * inverse**5 * (1.0 - self_mask)
    products = offset[:, None] * offset[None, :]
    identity = jnp.eye(3, dtype=jnp.float32)[:, :, None, None]
    return weight * (identity * distance2 - 3.0 * products)


def squares_of(residual):
    return lax.psum(jnp.sum(residual * residual, axis=(0, 2)), ("row", "col"))


def local(external_field, jitter, species, alpha_table, block_cell, tile_map):
    n_row = lax.axis_size("row")
    n_col = lax.axis_size("col")
    atom_total = external_field.shape[2]
    rhs_total = external_field.shape[1]
    block_total = n_row * n_col
    my_row = lax.axis_index("row")
    my_col = lax.axis_index("col")
    own_block = my_row * n_col + my_col
    own_cell = lax.dynamic_slice_in_dim(block_cell, own_block, 1, 0)
    own_sites = lattice(own_cell, atom_total, block_total).reshape(3, atom_total) + jitter
    row_sites = lax.all_gather(own_sites, "col", axis=1, tiled=True)
    col_sites = lax.all_gather(own_sites, "row", axis=1, tiled=True)
    species_ids = jnp.arange(alpha_table.shape[1], dtype=jnp.int32)[:, None]
    onehot = (species[None, :] == species_ids).astype(jnp.float32)
    per_atom = jnp.dot(1.0 / alpha_table, onehot, precision=lax.Precision.HIGHEST)
    inv_diag = jnp.repeat(per_atom, FIELDS, axis=0)
    col_block_ids = jnp.arange(n_row, dtype=jnp.int32) * n_col + my_col
    local_iota = lax.broadcasted_iota(jnp.int32, (atom_total, n_row * atom_total), 0)
    wide_iota = lax.broadcasted_iota(jnp.int32, (atom_total, n_row * atom_total), 1)
    same_atom = local_iota == wide_iota % atom_total
    dipoles = jnp.zeros_like(external_field)
    residual = external_field
    direction = external_field
    squares = squares_of(residual)
    for iteration in range(ITERS):
        row_vecs = lax.all_gather(direction, "col", axis=2, tiled=True)
        col_vecs = lax.all_gather(direction, "row", axis=2, tiled=True)

        def one_row(row_slot, totals):
            row_block = my_row * n_col + row_slot
            row_line = lax.dynamic_slice_in_dim(tile_map, row_block, 1, 0)[0]
            codes = row_line[col_block_ids]
            active = codes == 1

            def accumulate(totals):
                row_total, col_total = totals
                row_place = lax.dynamic_slice_in_dim(
                    row_sites, row_slot * atom_total, atom_total, 1
                )
                column_mask = jnp.repeat(active.astype(jnp.float32), atom_total)
                diagonal_columns = jnp.repeat(
                    (col_block_ids == row_block).astype(jnp.float32), atom_total
                )
                self_mask = same_atom.astype(jnp.float32) * diagonal_columns[None, :]
                tile = coupling_wide(row_place, col_sites, self_mask) * column_mask
                forward = jnp.einsum(
                    "kluv,lrv->kru", tile, col_vecs, precision=lax.Precision.HIGHEST
                )
                row_piece = lax.dynamic_slice_in_dim(
                    row_total, row_slot * atom_total, atom_total, 2
                )
                row_total = lax.dynamic_update_slice_in_dim(
                    row_total, row_piece + forward, row_slot * atom_total, 2
                )
                row_vector = lax.dynamic_slice_in_dim(
                    row_vecs, row_slot * atom_total, atom_total, 2
                )
                mirrored = jnp.einsum(
                    "kluv,kru->lrv", tile, row_vector, precision=lax.Precision.HIGHEST
                ) * (1.0 - diagonal_columns)
                col_total = col_total + mirrored
                return (row_total, col_total)

            def keep(totals):
                return totals

            return lax.cond(jnp.any(active), accumulate, keep, totals)

        zeros_row = jnp.zeros((3, rhs_total, n_col * atom_total), jnp.float32)
        zeros_col = jnp.zeros((3, rhs_total, n_row * atom_total), jnp.float32)
        row_total, col_total = lax.fori_loop(0, n_col, one_row, (zeros_row, zeros_col))
        coupled = lax.psum_scatter(row_total, "col", scatter_dimension=2, tiled=True)
        coupled = coupled + lax.psum_scatter(col_total, "row", scatter_dimension=2, tiled=True)
        mapped = inv_diag[None] * direction + coupled
        curvature = lax.psum(jnp.sum(direction * mapped, axis=(0, 2)), ("row", "col"))
        step_size = squares / curvature
        dipoles = dipoles + step_size[None, :, None] * direction
        residual = residual - step_size[None, :, None] * mapped
        squares_next = squares_of(residual)
        direction = residual + (squares_next / squares)[None, :, None] * direction
        squares = squares_next
    return (dipoles, residual)


def solution(mesh):
    return jax.shard_map(
        local,
        mesh=mesh,
        in_specs=(
            P(None, None, ("row", "col")),
            P(None, ("row", "col")),
            P(("row", "col")),
            P(),
            P(),
            P(),
        ),
        out_specs=(P(None, None, ("row", "col")), P(None, None, ("row", "col"))),
        check_vma=False,
    )
```

profile of v0, /device:TPU:1, one launch (start us, length us, event | category | flops | bytes accessed | tf_op | source)
XLA Modules:
  0.0 794.9 jit_solution(16461431003077570751)
XLA Ops:
  11.9 21.4 %all-gather = f32[16,32,3]{1,2,0:T(4,128)S(1)} all-gather(f32[1,32,3]{1,2,0:T(4,128)S(1)} %fusion.86), channel_id=1, replica_groups=mesh['row'=16,'col'=16] {'col'}, dimensions={0}, use_global_device_ids=true | all-gather | bytes 6528 | tf_op jit(solution)/shard_map/all_gather | solution.py:60
  33.2 18.1 %all-gather.1 = f32[16,32,3]{1,2,0:T(4,128)S(1)} all-gather(f32[1,32,3]{1,2,0:T(4,128)S(1)} %fusion.86), channel_id=1, replica_groups=mesh['row'=16,'col'=16] {'row'}, dimensions={0}, use_global_device_ids=true | all-gather | bytes 6528 | tf_op jit(solution)/shard_map/all_gather | solution.py:61
  51.4 18.5 %all_gather.20 = f32[3,36,512]{1,2,0:T(8,128)S(1)} all-gather(f32[3,36,32]{1,2,0:T(8,128)S(1)} %copy-done.2), channel_id=1, replica_groups=mesh['row'=16,'col'=16] {'row'}, dimensions={2}, use_global_device_ids=true | all-gather | bytes 235008 | tf_op jit(solution)/shard_map/all_gather | solution.py:76
  69.8 27.5 %all_gather.21 = f32[3,36,512]{1,2,0:T(8,128)S(1)} all-gather(f32[3,36,32]{1,2,0:T(8,128)S(1)} %copy-done.2), channel_id=1, replica_groups=mesh['row'=16,'col'=16] {'col'}, dimensions={2}, use_global_device_ids=true | all-gather | bytes 235008 | tf_op jit(solution)/shard_map/all_gather | solution.py:75
  97.9 76.9 %while.36 = (s32[]{:T(128)}, f32[3,36,512]{1,2,0:T(8,128)S(1)}, f32[3,36,512]{2,1,0:T(8,128)S(1)}, s32[]{:T(128)}, s32[256,256]{1,0:T(8,128)}, /*index=5*/f32[3,...) while((s32[]{:T(128)}, f32[3,36,512]{1,2,0:T(8,128)S(1)}, ...), condition=%wide.region_7.8_spmd.clone, body=%wide.region_2.7_spmd.clone.sunk | while | flops 129713248 | bytes 2646895 | solution.py:120
  105.4 2.1 conditional.6
  115.0 2.1 conditional.6
  124.6 2.1 conditional.6
  134.3 2.1 conditional.6
  143.9 2.1 conditional.6
  153.5 2.1 conditional.6
  163.1 2.1 conditional.6
  172.7 2.1 conditional.6
  177.7 69.3 %reduce-scatter.7.cloned.1.call-done = f32[3,36,32]{1,2,0:T(8,128)} async-done(((f32[3,36,512]{1,2,0:T(8,128)}), f32[3,36,32]{1,2,0:T(8,128)}) %reduce-scatter.7.cloned.1.call-update) | async-done | bytes 13840 | tf_op jit(solution)/shard_map/reduce_scatter | solution.py:122
  247.0 57.5 %reduce-scatter.5.cloned.1.call-done = f32[3,36,32]{1,2,0:T(8,128)} async-done(((f32[3,36,512]{1,2,0:T(8,128)}), f32[3,36,32]{1,2,0:T(8,128)}) %reduce-scatter.5.cloned.1.call-update) | async-done | bytes 13840 | tf_op jit(solution)/shard_map/reduce_scatter | solution.py:121
  305.5 80.0 %all-reduce = (f32[36]{0:T(128)S(1)}, f32[36]{0:T(128)S(1)}) all-reduce(f32[36]{0:T(128)S(1)} %get-tuple-element.775, f32[36]{0:T(128)S(1)} %get-tuple-element.774), channel_id=1, replica_groups=mesh['row'=16,'col'=16] {'row','col'}, use_global_device_ids=true, to_apply=%region_1.2 | all-reduce | flops 72 | bytes 576 | tf_op jit(solution)/shard_map/psum | solution.py:46
  385.5 72.4 %psum.30 = f32[36]{0:T(128)S(1)} all-reduce(f32[36]{0:T(128)S(1)} %get-tuple-element.834), channel_id=1, replica_groups=mesh['row'=16,'col'=16] {'row','col'}, use_global_device_ids=true, to_apply=%region_13.14 | all-reduce | flops 36 | bytes 288 | tf_op jit(solution)/shard_map/psum | solution.py:46
  457.9 18.0 %all_gather.22 = f32[3,36,512]{1,2,0:T(8,128)S(1)} all-gather(f32[3,36,32]{1,2,0:T(8,128)S(1)} %multiply_add_fusion.3), channel_id=1, replica_groups=mesh['row'=16,'col'=16] {'row'}, dimensions={2}, use_global_device_ids=true | all-gather | bytes 235008 | tf_op jit(solution)/shard_map/all_gather | solution.py:76
  475.9 24.0 %all_gather.23 = f32[3,36,512]{1,2,0:T(8,128)S(1)} all-gather(f32[3,36,32]{1,2,0:T(8,128)S(1)} %multiply_add_fusion.3), channel_id=1, replica_groups=mesh['row'=16,'col'=16] {'col'}, dimensions={2}, use_global_device_ids=true | all-gather | bytes 235008 | tf_op jit(solution)/shard_map/all_gather | solution.py:75
  500.3 76.9 %while.37 = (s32[]{:T(128)}, f32[3,36,512]{1,2,0:T(8,128)S(1)}, f32[3,36,512]{2,1,0:T(8,128)S(1)}, s32[]{:T(128)}, s32[256,256]{1,0:T(8,128)}, /*index=5*/f32[3,...) while((s32[]{:T(128)}, f32[3,36,512]{1,2,0:T(8,128)S(1)}, ...), condition=%wide.region_19.20_spmd.clone, body=%wide.region_14.19_spmd.clone.sunk | while | flops 129713248 | bytes 2646895 | solution.py:120
  503.0 2.1 conditional.7
  507.8 2.1 conditional.7
  517.4 2.1 conditional.7
  527.0 2.1 conditional.7
  536.6 2.1 conditional.7
  546.2 2.1 conditional.7
  555.8 2.1 conditional.7
  565.4 2.1 conditional.7
  575.0 2.1 conditional.7
  579.0 70.3 %reduce-scatter.11.cloned.1.call-done = f32[3,36,32]{1,2,0:T(8,128)} async-done(((f32[3,36,512]{1,2,0:T(8,128)}), f32[3,36,32]{1,2,0:T(8,128)}) %reduce-scatter.11.cloned.1.call-update) | async-done | bytes 13840 | tf_op jit(solution)/shard_map/reduce_scatter | solution.py:122
  649.2 57.7 %reduce-scatter.9.cloned.1.call-done = f32[3,36,32]{1,2,0:T(8,128)} async-done(((f32[3,36,512]{1,2,0:T(8,128)}), f32[3,36,32]{1,2,0:T(8,128)}) %reduce-scatter.9.cloned.1.call-update) | async-done | bytes 13840 | tf_op jit(solution)/shard_map/reduce_scatter | solution.py:121
  707.8 79.8 %psum.31 = f32[36]{0:T(128)S(1)} all-reduce(f32[36]{0:T(128)S(1)} %multiply_reduce_fusion.2), channel_id=1, replica_groups=mesh['row'=16,'col'=16] {'row','col'}, use_global_device_ids=true, to_apply=%region_23.24 | all-reduce | flops 36 | bytes 288 | tf_op jit(solution)/shard_map/psum | solution.py:124
  (747 shorter events, 170.6 us)
Async XLA Ops:
  7.2 239.9 %reduce-scatter.7.cloned.1.call-start = ((), (), s32[]{:S(2)}) async-start(), calls=%async_computation.5 | async-start | bytes 835584 | tf_op jit(solution)/shard_map/reduce_scatter | solution.py:122
  7.2 0.7 copy-start.9
  11.2 0.7 copy-start.7
  11.2 40.2 %copy-start.2 = (f32[3,36,32]{1,2,0:T(8,128)S(1)}, f32[3,36,32]{1,2,0:T(8,128)}, u32[]{:S(2)}) copy-start(f32[3,36,32]{1,2,0:T(8,128)} %param.14) | copy-start | bytes 41476
  174.8 1.2 copy-start.1
  176.0 128.6 %reduce-scatter.5.cloned.1.call-start = ((), (), s32[]{:S(2)}) async-start(), calls=%async_computation.4 | async-start | bytes 835584 | tf_op jit(solution)/shard_map/reduce_scatter | solution.py:121
  176.1 0.8 copy-start.8
  176.8 0.7 copy-start.10
  176.8 472.4 %reduce-scatter.11.cloned.1.call-start = ((), (), s32[]{:S(2)}) async-start(), calls=%async_computation.7 | async-start | bytes 835584 | tf_op jit(solution)/shard_map/reduce_scatter | solution.py:122
  247.0 138.4 %copy-start.3 = (f32[3,36,32]{1,2,0:T(8,128)S(1)}, f32[3,36,32]{1,2,0:T(8,128)}, u32[]{:S(2)}) copy-start(f32[3,36,32]{1,2,0:T(8,128)} %reduce-scatter.7.cloned.1.call-done) | copy-start | bytes 41476
  304.6 80.9 %copy-start.4 = (f32[3,36,32]{1,2,0:T(8,128)S(1)}, f32[3,36,32]{1,2,0:T(8,128)}, u32[]{:S(2)}) copy-start(f32[3,36,32]{1,2,0:T(8,128)} %reduce-scatter.5.cloned.1.call-done) | copy-start | bytes 41476
  577.1 1.2 copy-start
  578.4 128.5 %reduce-scatter.9.cloned.1.call-start = ((), (), s32[]{:S(2)}) async-start(), calls=%async_computation.6 | async-start | bytes 835584 | tf_op jit(solution)/shard_map/reduce_scatter | solution.py:121
  649.2 138.5 %copy-start.5 = (f32[3,36,32]{1,2,0:T(8,128)S(1)}, f32[3,36,32]{1,2,0:T(8,128)}, u32[]{:S(2)}) copy-start(f32[3,36,32]{1,2,0:T(8,128)} %reduce-scatter.11.cloned.1.call-done) | copy-start | bytes 41476
  706.9 80.8 %copy-start.6 = (f32[3,36,32]{1,2,0:T(8,128)S(1)}, f32[3,36,32]{1,2,0:T(8,128)}, u32[]{:S(2)}) copy-start(f32[3,36,32]{1,2,0:T(8,128)} %reduce-scatter.9.cloned.1.call-done) | copy-start | bytes 41476
Sparse Core Ops, SparseCore 0:
  176.1 70.8 reduce-scatter.6
  249.5 54.9 reduce-scatter.4
  578.5 70.6 reduce-scatter.10
  651.7 55.1 reduce-scatter.8
where the time goes:
time: 798 us; the launch traced here: 795 us
  blocking collectives  360 us (45%)
  waiting for transfers between devices  256 us (32%)
  local copies, waits for them, and re-layouts  62 us (8%)
  matrix products  45.6 us (6%)
  other arithmetic  30.6 us (4%)
  loops' own time  24.2 us (3%)
  between operations  16.6 us (2%)
    psum x2, blocking collectives, squares_of(): return lax.psum(jnp.sum(residual * residual, axis=(0, 2)), ('row', 'col'))  152 us
    reduce_scatter x2, waiting for transfers between devices, local(): lax.psum_scatter(col_total, 'row', scatter_dimension=2, tiled=True)  140 us
    reduce_scatter x2, waiting for transfers between devices, local(): lax.psum_scatter(row_total, 'col', scatter_dimension=2, tiled=True)  115 us
    psum x1, blocking collectives, local(): lax.psum(jnp.sum(direction * mapped, axis=(0, 2)), ('row', 'col'))  79.8 us
    all_gather x2, blocking collectives, local(): row_vecs = lax.all_gather(direction, 'col', axis=2, tiled=True)  51.6 us
    all_gather x2, blocking collectives, local(): col_vecs = lax.all_gather(direction, 'row', axis=2, tiled=True)  36.4 us
    dot_general x32, matrix products, accumulate(): jnp.einsum('kluv,lrv->kru', tile, col_vecs, precision=lax.Precision.HIGHEST)  23.8 us
    dynamic_slice x32, local copies, waits for them, and re-layouts, one_row(): row_line = lax.dynamic_slice_in_dim(tile_map, row_block, 1, 0)[0]  22.6 us
  transfers between devices with their start and end apart: 4, of which 4 were waited for; matrix products, arithmetic and copies ran while one was open for 0% of the time, Pallas kernels for 0%

commit v1 on v0

v1 whole, which is shorter than its diff:
```python
import jax
import jax.numpy as jnp
from jax import lax
from jax.experimental import pallas as pl
from jax.experimental.pallas import tpu as pltpu
from jax.sharding import PartitionSpec as P

COMPS = 3
RHS = 36
ATOMS = 32
GROUP = 16
LANES = 128
SUMS = 8
SITE = 120
WIDE = GROUP * ATOMS
PAIRS = 5
SPACING = 2.0
F32 = jnp.float32
BF16 = jnp.bfloat16

VMEM = pl.BlockSpec(memory_space=pltpu.VMEM)
SMEM = pl.BlockSpec(memory_space=pltpu.SMEM)
PARAMS = pltpu.CompilerParams(vmem_limit_bytes=40 * 1024 * 1024)


def lane_ids(rows):
    return lax.broadcasted_iota(jnp.int32, (rows, LANES), 1)


def component_lanes(rows):
    lanes = lane_ids(rows)
    first = lanes < RHS
    second = (lanes >= RHS) & (lanes < 2 * RHS)
    third = (lanes >= 2 * RHS) & (lanes < COMPS * RHS)
    return first, second, third


def sum_components(value):
    first, second, third = component_lanes(SUMS)
    up = pltpu.roll(value, RHS, 1)
    up2 = pltpu.roll(value, 2 * RHS, 1)
    down = pltpu.roll(value, LANES - RHS, 1)
    down2 = pltpu.roll(value, LANES - 2 * RHS, 1)
    of_first = value + down + down2
    of_second = up + value + down
    of_third = up2 + up + value
    return jnp.where(first, of_first, jnp.where(second, of_second, jnp.where(third, of_third, 1.0)))


def prepare_kernel(ids, block_cell, species, alpha, field, jitter, vec_out, site_out, aux_out, work):
    lane = lax.broadcasted_iota(jnp.int32, (1, LANES), 1)
    rhs_lane = jnp.where(lane >= 2 * RHS, lane - 2 * RHS, jnp.where(lane >= RHS, lane - RHS, lane))
    inverse = []
    for kind in range(4):
        row = jnp.ones((1, LANES), F32)
        for freq in range(12):
            row = jnp.where((rhs_lane >= 3 * freq) & (rhs_lane < 3 * freq + 3), alpha[freq, kind], row)
        inverse.append(1.0 / row)
    shift = 0.25 * ((inverse[0] + inverse[1]) + (inverse[2] + inverse[3]))
    row_iota = lax.broadcasted_iota(jnp.int32, (ATOMS, LANES), 0)
    kinds = jnp.zeros((ATOMS, LANES), jnp.int32)
    for atom in range(ATOMS):
        kinds = jnp.where(row_iota == atom, species[atom], kinds)
    diag = jnp.zeros((ATOMS, LANES), F32)
    for kind in range(4):
        diag = jnp.where(kinds == kind, inverse[kind] - shift, diag)
    aux_out[0:ATOMS, :] = diag
    aux_out[ATOMS : ATOMS + SUMS, :] = jnp.broadcast_to(shift, (SUMS, LANES))

    cell = block_cell[ids[0] * GROUP + ids[1]]
    cell_x = cell // 32
    cell_y = (cell // 4) % 8
    cell_z = cell % 4
    atom = lax.broadcasted_iota(jnp.int32, (1, ATOMS), 1)
    place_x = cell_x * 4 + atom // 8
    place_y = cell_y * 4 + (atom // 2) % 4
    place_z = cell_z * 2 + atom % 2
    work[...] = jnp.zeros_like(work)
    for comp in range(COMPS):
        work[comp * RHS : (comp + 1) * RHS, 0:ATOMS] = field[comp]
    for comp, place in enumerate((place_x, place_y, place_z)):
        work[SITE + comp : SITE + comp + 1, 0:ATOMS] = (
            place.astype(F32) * SPACING + jitter[comp : comp + 1, :]
        )
    turned = work[...].T[0:ATOMS, :]
    sites = work[SITE : SITE + SUMS, :]
    for slot in range(GROUP):
        vec_out[slot] = turned
        site_out[slot] = sites


def right_side(vectors, side):
    first, second, third = component_lanes(WIDE)
    zero = jnp.zeros_like(vectors)
    up = pltpu.roll(vectors, RHS, 1)
    up2 = pltpu.roll(vectors, 2 * RHS, 1)
    down = pltpu.roll(vectors, LANES - RHS, 1)
    down2 = pltpu.roll(vectors, LANES - 2 * RHS, 1)
    parts = (
        jnp.where(first, vectors, jnp.where(third, -vectors, zero)),
        jnp.where(second, vectors, jnp.where(third, -vectors, zero)),
        jnp.where(first, down, jnp.where(second, up, zero)),
        jnp.where(first, down2, jnp.where(third, up2, zero)),
        jnp.where(second, down, jnp.where(third, up, zero)),
    )
    for slot, part in enumerate(parts):
        high = part.astype(BF16)
        low = (part - high.astype(F32)).astype(BF16)
        side[slot * WIDE : (slot + 1) * WIDE, 0:LANES] = high
        side[slot * WIDE : (slot + 1) * WIDE, LANES : 2 * LANES] = low


def product(high, low, side):
    both = jnp.dot(high[...], side[...], preferred_element_type=F32)
    rest = jnp.dot(low[...], side[:, 0:LANES], preferred_element_type=F32)
    return both[:, 0:LANES] + (both[:, LANES:] + rest)


def first_kernel(ids, tile_map, vectors, sites, part_out, high, low, side, column, mask):
    wide = vectors[...].reshape(WIDE, LANES)
    right_side(wide, side)
    across = wide.T[SITE : SITE + SUMS, :]
    across_x, across_y, across_z = across[0:1, :], across[1:2, :], across[2:3, :]
    down = sites[...].reshape(GROUP * SUMS, LANES).T[0:ATOMS, :]
    for block in range(GROUP):
        for comp in range(COMPS):
            lane = block * SUMS + comp
            column[comp, block * ATOMS : (block + 1) * ATOMS, :] = jnp.broadcast_to(
                down[:, lane : lane + 1], (ATOMS, LANES)
            )
    active = jnp.where(tile_map[pl.ds(pl.multiple_of(ids[0] * GROUP, GROUP), GROUP), :] != 0, 1.0, 0.0)
    block_row = lax.broadcasted_iota(jnp.int32, (GROUP * GROUP, WIDE), 0)
    block_col = lax.broadcasted_iota(jnp.int32, (GROUP * GROUP, WIDE), 1) // ATOMS * GROUP + ids[1]
    select = jnp.where(block_row == block_col, 1.0, 0.0).astype(BF16)
    mask[...] = jnp.dot(active.astype(BF16), select, preferred_element_type=F32)

    def build(step, carry):
        rows = pl.ds(pl.multiple_of(step * 16, 16), 16)
        here_x, here_y, here_z = column[0, rows, :], column[1, rows, :], column[2, rows, :]
        keep = mask[pl.ds(step // 2, 1), :]
        for tile in range(WIDE // LANES):
            lanes = slice(tile * LANES, (tile + 1) * LANES)
            dx = here_x - across_x[:, lanes]
            dy = here_y - across_y[:, lanes]
            dz = here_z - across_z[:, lanes]
            xx = dx * dx
            yy = dy * dy
            distance2 = xx + yy + dz * dz
            square = jnp.maximum(distance2, 1.0)
            inverse = lax.rsqrt(square)
            damping = 1.0 / (1.0 + jnp.exp(6.0 - 2.5 * (square * inverse)))
            inverse2 = inverse * inverse
            weight = damping * (inverse2 * inverse2 * inverse) * keep[:, lanes]
            weight = jnp.where(distance2 > 0.5, weight, 0.0)
            radial = weight * square
            minus3 = -3.0 * weight
            along_x = minus3 * dx
            along_y = minus3 * dy
            entries = (
                radial + minus3 * xx,
                radial + minus3 * yy,
                along_x * dy,
                along_x * dz,
                along_y * dz,
            )
            for slot, entry in enumerate(entries):
                top = entry.astype(BF16)
                at = slice(slot * WIDE + tile * LANES, slot * WIDE + (tile + 1) * LANES)
                high[rows, at] = top
                low[rows, at] = (entry - top.astype(F32)).astype(BF16)
        return carry

    lax.fori_loop(0, WIDE // 16, build, 0)
    part_out[...] = product(high, low, side).reshape(GROUP, ATOMS, LANES)


def shifted_kernel(parts, own, aux, out):
    coupled = jnp.sum(parts[...], axis=0)
    vector = jnp.where(lane_ids(ATOMS) < COMPS * RHS, own[0], 0.0)
    mapped = aux[0:ATOMS, :] * vector + coupled
    out_rows = jnp.zeros((SUMS, LANES), F32)
    row = lax.broadcasted_iota(jnp.int32, (SUMS, LANES), 0)
    for slot, terms in enumerate((vector * vector, vector * mapped, mapped * mapped)):
        out_rows = jnp.where(row == slot, jnp.sum(terms, axis=0, keepdims=True), out_rows)
    for slot in range(GROUP):
        out[slot, 0:ATOMS, :] = mapped
        out[slot, ATOMS:, :] = out_rows


def second_kernel(gathered, high, low, part_out, side):
    right_side(gathered[:, 0:ATOMS, :].reshape(WIDE, LANES), side)
    part_out[:, 0:ATOMS, :] = product(high, low, side).reshape(GROUP, ATOMS, LANES)
    sums = jnp.sum(gathered[:, ATOMS:, :], axis=0)
    for slot in range(GROUP):
        part_out[slot, ATOMS:, :] = sums


def step_kernel(parts, own, shifted, aux, sums_out, state):
    total = jnp.sum(parts[...], axis=0)
    inside = lane_ids(ATOMS) < COMPS * RHS
    vector = jnp.where(inside, own[0], 0.0)
    mapped = shifted[0, 0:ATOMS, :]
    twice = aux[0:ATOMS, :] * mapped + total[0:ATOMS, :]
    sums = sum_components(total[ATOMS:, :])
    bb, be, ee = sums[0:1, :], sums[1:2, :], sums[2:3, :]
    shift = aux[ATOMS : ATOMS + 1, :]
    bm = shift * bb + be
    step = bb / bm
    kept = be / bm
    beta = (bb * ee - be * be) / (bm * bm)
    residual = kept * vector - step * mapped
    direction = residual + beta * vector
    image = shift * direction + ((kept + beta) * mapped - step * twice)
    row = lax.broadcasted_iota(jnp.int32, (SUMS, LANES), 0)
    squares = jnp.sum(residual * residual, axis=0, keepdims=True)
    curvature = jnp.sum(direction * image, axis=0, keepdims=True)
    both = sum_components(jnp.where(row == 0, squares, jnp.where(row == 1, curvature, 0.0)))
    lane = lax.broadcasted_iota(jnp.int32, (1, LANES), 1)
    packed = jnp.where(lane < RHS, both[0:1, :], jnp.where(lane < 2 * RHS, both[1:2, :], 0.0))
    sums_out[...] = jnp.broadcast_to(packed.reshape(1, 1, LANES), sums_out.shape)
    state[0] = step * vector
    state[1] = direction
    state[2] = residual
    state[3] = image


def finish_kernel(gathered, state, dipoles, residual, work):
    total = jnp.broadcast_to(jnp.sum(gathered[...], axis=0), (SUMS, LANES))
    first, second, third = component_lanes(SUMS)
    up = pltpu.roll(total, RHS, 1)
    up2 = pltpu.roll(total, 2 * RHS, 1)
    down = pltpu.roll(total, LANES - RHS, 1)
    squares = jnp.where(first, total, jnp.where(second, up, up2))
    curvature = jnp.where(first, down, jnp.where(second, total, jnp.where(third, up, 1.0)))
    step = (squares / curvature)[0:1, :]
    for out, value in (
        (dipoles, state[0] + step * state[1]),
        (residual, state[2] - step * state[3]),
    ):
        work[0:ATOMS, :] = value
        turned = work[...].T
        for comp in range(COMPS):
            out[comp] = turned[comp * RHS : (comp + 1) * RHS, 0:ATOMS]


def shape(*dims, dtype=F32):
    return jax.ShapeDtypeStruct(dims, dtype)


def local(external_field, jitter, species, alpha_table, block_cell, tile_map):
    ids = jnp.stack([lax.axis_index("row"), lax.axis_index("col")]).astype(jnp.int32)
    vec, site, aux = pl.pallas_call(
        prepare_kernel,
        out_shape=(shape(GROUP, ATOMS, LANES), shape(GROUP, SUMS, LANES), shape(ATOMS + SUMS, LANES)),
        in_specs=[SMEM, SMEM, SMEM, SMEM, VMEM, VMEM],
        out_specs=(VMEM, VMEM, VMEM),
        scratch_shapes=[pltpu.VMEM((LANES, LANES), F32)],
        compiler_params=PARAMS,
        name="prepare",
    )(ids, block_cell, species, alpha_table, external_field, jitter)
    sites = lax.all_to_all(site, "col", 0, 0)
    vectors = lax.all_to_all(vec, "row", 0, 0)
    own_spec = pl.BlockSpec((1, ATOMS, LANES), lambda i: (0, 0, 0))

    def whole(*dims):
        return pl.BlockSpec(dims, lambda i: (0,) * len(dims))

    part, high, low = pl.pallas_call(
        first_kernel,
        out_shape=(
            shape(GROUP, ATOMS, LANES),
            shape(WIDE, PAIRS * WIDE, dtype=BF16),
            shape(WIDE, PAIRS * WIDE, dtype=BF16),
        ),
        in_specs=[SMEM, VMEM, VMEM, VMEM],
        out_specs=(VMEM, VMEM, VMEM),
        scratch_shapes=[
            pltpu.VMEM((PAIRS * WIDE, 2 * LANES), BF16),
            pltpu.VMEM((COMPS, WIDE, LANES), F32),
            pltpu.VMEM((GROUP, WIDE), F32),
        ],
        compiler_params=PARAMS,
        name="first",
    )(ids, tile_map, vectors, sites)
    parts = lax.all_to_all(part, "col", 0, 0)
    shifted = pl.pallas_call(
        shifted_kernel,
        grid=(1,),
        out_shape=shape(GROUP, ATOMS + SUMS, LANES),
        in_specs=[whole(GROUP, ATOMS, LANES), own_spec, whole(ATOMS + SUMS, LANES)],
        out_specs=whole(GROUP, ATOMS + SUMS, LANES),
        compiler_params=PARAMS,
        name="shifted",
    )(parts, vec, aux)
    gathered = lax.all_to_all(shifted, "row", 0, 0)
    part2 = pl.pallas_call(
        second_kernel,
        out_shape=shape(GROUP, ATOMS + SUMS, LANES),
        in_specs=[VMEM, VMEM, VMEM],
        out_specs=VMEM,
        scratch_shapes=[pltpu.VMEM((PAIRS * WIDE, 2 * LANES), BF16)],
        compiler_params=PARAMS,
        name="second",
    )(gathered, high, low)
    parts2 = lax.all_to_all(part2, "col", 0, 0)
    sums, state = pl.pallas_call(
        step_kernel,
        grid=(1,),
        out_shape=(shape(GROUP * GROUP, 1, LANES), shape(4, ATOMS, LANES)),
        in_specs=[
            whole(GROUP, ATOMS + SUMS, LANES),
            own_spec,
            pl.BlockSpec((1, ATOMS + SUMS, LANES), lambda i: (0, 0, 0)),
            whole(ATOMS + SUMS, LANES),
        ],
        out_specs=(whole(GROUP * GROUP, 1, LANES), whole(4, ATOMS, LANES)),
        compiler_params=PARAMS,
        name="step",
    )(parts2, vec, shifted, aux)
    all_sums = lax.all_to_all(sums, ("row", "col"), 0, 0)
    return pl.pallas_call(
        finish_kernel,
        out_shape=(shape(COMPS, RHS, ATOMS), shape(COMPS, RHS, ATOMS)),
        in_specs=[VMEM, VMEM],
        out_specs=(VMEM, VMEM),
        scratch_shapes=[pltpu.VMEM((LANES, LANES), F32)],
        compiler_params=PARAMS,
        name="finish",
    )(all_sums, state)


def solution(mesh):
    return jax.shard_map(
        local,
        mesh=mesh,
        in_specs=(
            P(None, None, ("row", "col")),
            P(None, ("row", "col")),
            P(("row", "col")),
            P(),
            P(),
            P(),
        ),
        out_specs=(P(None, None, ("row", "col")), P(None, None, ("row", "col"))),
        check_vma=False,
    )
```

time: 798 us -> 110 us (0.14)
  blocking collectives: 360 us -> 94.1 us
  waiting for transfers between devices: 256 us -> 0 us
  local copies, waits for them, and re-layouts: 62 us -> 6.06 us
  matrix products: 45.6 us -> 0 us
  other arithmetic: 30.6 us -> 0.08 us
  loops' own time: 24.2 us -> 0 us
  between operations: 16.6 us -> 0.68 us
  Pallas kernels: 0 us -> 8.61 us
    reduce_scatter x4 -> x0, waiting for transfers between devices: 255 us -> none  [the longest x2 140 us: local(): lax.psum_scatter(col_total, 'row', scatter_dimension=2, tiled=True)]
    psum x3 -> x0, blocking collectives: 232 us -> none  [the longest x2 152 us: squares_of(): return lax.psum(jnp.sum(residual * residual, axis=(0, 2)), ('row', 'col'))]
    all_gather x6 -> x0, blocking collectives: 127 us -> none  [the longest x2 51.6 us: local(): row_vecs = lax.all_gather(direction, 'col', axis=2, tiled=True)]
    all_to_all x0 -> x6, blocking collectives: none -> 94.1 us  [the longest x1 17.6 us: local(): sites = lax.all_to_all(site, 'col', 0, 0)]
    dot_general x65 -> x0, matrix products: 45.6 us -> none  [the longest x32 23.8 us: accumulate(): jnp.einsum('kluv,lrv->kru', tile, col_vecs, precision=lax.Precision.HIGHEST)]
    dynamic_slice x65 -> x0, local copies, waits for them, and re-layouts: 25.6 us -> none  [the longest x32 22.6 us: one_row(): row_line = lax.dynamic_slice_in_dim(tile_map, row_block, 1, 0)[0]]
    another operation x34 -> x0, loops' own time: 24.2 us -> none  [the longest x2 21.6 us: local(): lax.fori_loop(0, n_col, one_row, (zeros_row, zeros_col))]
    eq x32 -> x0, other arithmetic: 21.4 us -> none  [one_row(): active = codes == 1]
  transfers between devices with their start and end apart: 4 -> 0, of which waited for: 4 -> 0; matrix products, arithmetic and copies ran while one was open for 0% -> 0% of each run, Pallas kernels for 0% -> 0%
where the time goes in v1:
time: 110 us
  blocking collectives  94.1 us (86%)
  Pallas kernels  8.61 us (8%)
  local copies, waits for them, and re-layouts  6.06 us (6%)
    all_to_all x1, blocking collectives, local(): sites = lax.all_to_all(site, 'col', 0, 0)  17.6 us
    all_to_all x1, blocking collectives, local(): all_sums = lax.all_to_all(sums, ('row', 'col'), 0, 0)  17.6 us
    all_to_all x1, blocking collectives, local(): parts2 = lax.all_to_all(part2, 'col', 0, 0)  16 us
    all_to_all x1, blocking collectives, local(): parts = lax.all_to_all(part, 'col', 0, 0)  15.6 us
    all_to_all x1, blocking collectives, local(): vectors = lax.all_to_all(vec, 'row', 0, 0)  14.9 us
    all_to_all x1, blocking collectives, local(): gathered = lax.all_to_all(shifted, 'row', 0, 0)  12.5 us
    pallas_call x1, Pallas kernels, local(): pl.pallas_call(first_kernel, out_shape=(shape(GROUP, ATOMS, LANES), shape...  5.44 us
    unnamed x10, local copies, waits for them, and re-layouts  4.63 us

profile of v1, /device:TPU:1, one launch (start us, length us, event | category | flops | bytes accessed | tf_op | source)
XLA Modules:
  0.0 109.5 jit_solution(12715049849961097752)
XLA Ops:
  0.6 0.8 copy.8.alpha
  1.4 0.9 copy.9.field
  2.3 0.1 pad_add_fusion.ids
  2.4 0.0 copy-start.1
  2.4 0.7 copy-done.1
  3.1 0.0 copy-start.2
  3.1 0.7 copy-done.2
  3.7 0.0 copy-start.3
  3.7 0.7 copy-done.3
  4.4 0.8 prepare.1
  5.2 17.6 %all_to_all.30.sites = f32[16,8,128]{2,1,0:T(8,128)S(1)} all-to-all(f32[16,8,128]{2,1,0:T(8,128)S(1)} %get-tuple-element.11), channel_id=1, replica_groups=mesh['row'=16,'col'=16] {'col'}, dimensions={0} | all-to-all | bytes 131072 | tf_op jit(solution)/shard_map/all_to_all | solution.py:261
  22.8 14.9 %all_to_all.31.vectors = f32[16,32,128]{2,1,0:T(8,128)S(1)} all-to-all(f32[16,32,128]{2,1,0:T(8,128)S(1)} %get-tuple-element.10.own), channel_id=1, replica_groups=mesh['row'=16,'col'=16] {'row'}, dimensions={0} | all-to-all | bytes 524288 | tf_op jit(solution)/shard_map/all_to_all | solution.py:262
  37.7 0.0 copy-start
  37.7 0.9 copy-done
  38.6 5.4 %first.1 = (f32[16,32,128]{2,1,0:T(8,128)S(1)}, bf16[512,2560]{1,0:T(8,128)(2,1)S(1)}, bf16[512,2560]{1,0:T(8,128)(2,1)S(1)}) custom-call(s32[2]{0:T(128)S(1)} %pad_add_fusion.ids, s32[256,256]{1,0:T(8,128)S(1)} %copy-done, f32[16,32,128]{2,1,0:T(8,128)S(1)} %all_to_all.31.vectors, f32[16,8,128]{2,1,0:T(8,128)S(1)} %all_to_all.30.sites), custom_call_target="tpu_custom_call" | custom-call | tf_op jit(solution)/shard_map/first/pallas_call | solution.py:268
  44.1 15.6 %all_to_all.32.parts = f32[16,32,128]{2,1,0:T(8,128)S(1)} all-to-all(f32[16,32,128]{2,1,0:T(8,128)S(1)} %get-tuple-element.12), channel_id=1, replica_groups=mesh['row'=16,'col'=16] {'col'}, dimensions={0} | all-to-all | bytes 524288 | tf_op jit(solution)/shard_map/all_to_all | solution.py:285
  59.7 12.5 %all_to_all.33.gathered = f32[16,40,128]{2,1,0:T(8,128)S(1)} all-to-all(f32[16,40,128]{2,1,0:T(8,128)S(1)} %shifted.1), channel_id=1, replica_groups=mesh['row'=16,'col'=16] {'row'}, dimensions={0} | all-to-all | bytes 655360 | tf_op jit(solution)/shard_map/all_to_all | solution.py:295
  72.2 1.6 %second.1 = f32[16,40,128]{2,1,0:T(8,128)S(1)} custom-call(f32[16,40,128]{2,1,0:T(8,128)S(1)} %all_to_all.33.gathered, bf16[512,2560]{1,0:T(8,128)(2,1)S(1)} %get-tuple-element.14.high, bf16[512,2560]{1,0:T(8,128)(2,1)S(1)} %get-tuple-element.15.low), custom_call_target="tpu_custom_call" | custom-call | tf_op jit(solution)/shard_map/second/pallas_call | solution.py:296
  73.8 16.0 %all_to_all.34.parts = f32[16,40,128]{2,1,0:T(8,128)S(1)} all-to-all(f32[16,40,128]{2,1,0:T(8,128)S(1)} %second.1), channel_id=1, replica_groups=mesh['row'=16,'col'=16] {'col'}, dimensions={0} | all-to-all | bytes 655360 | tf_op jit(solution)/shard_map/all_to_all | solution.py:305
  89.8 0.3 step.1
  90.1 17.6 %all_to_all.35.gathered = f32[256,1,128]{2,1,0:T(1,128)S(1)} all-to-all(f32[256,1,128]{2,1,0:T(1,128)S(1)} %get-tuple-element.16), channel_id=1, replica_groups=mesh['row'=16,'col'=16] {'row','col'}, dimensions={0} | all-to-all | bytes 262144 | tf_op jit(solution)/shard_map/all_to_all | solution.py:320
  107.6 0.4 finish.1
  108.1 0.7 copy.10
  108.8 0.7 copy.11
  (1 shorter events, 0.0 us)
Async XLA Ops:
  2.4 0.7 copy-start.1
  3.1 0.7 copy-start.2
  3.7 0.7 copy-start.3
  37.7 1.0 copy-start

commit v2 on v1

v2 whole, which is shorter than its diff:
```python
import jax
import jax.numpy as jnp
from jax import lax
from jax.experimental import pallas as pl
from jax.experimental.pallas import tpu as pltpu
from jax.sharding import PartitionSpec as P

COMPS = 3
RHS = 36
ATOMS = 32
GROUP = 16
HALF = 8
LANES = 128
SUMS = 8
SITE = 120
SUM_ROW = 104
WIDE = GROUP * ATOMS
NARROW = HALF * ATOMS
PAIRS = 5
SPACING = 2.0
F32 = jnp.float32
BF16 = jnp.bfloat16

VMEM = pl.BlockSpec(memory_space=pltpu.VMEM)
SMEM = pl.BlockSpec(memory_space=pltpu.SMEM)
HBM = pl.BlockSpec(memory_space=pltpu.HBM)
SQUARE = pltpu.VMEM((LANES, LANES), F32)
PARAMS = pltpu.CompilerParams(vmem_limit_bytes=40 * 1024 * 1024)


def lane_ids(rows):
    return lax.broadcasted_iota(jnp.int32, (rows, LANES), 1)


def component_lanes(rows):
    lanes = lane_ids(rows)
    first = lanes < RHS
    second = (lanes >= RHS) & (lanes < 2 * RHS)
    third = (lanes >= 2 * RHS) & (lanes < COMPS * RHS)
    return first, second, third


def sum_components(value):
    first, second, third = component_lanes(SUMS)
    up = pltpu.roll(value, RHS, 1)
    up2 = pltpu.roll(value, 2 * RHS, 1)
    down = pltpu.roll(value, LANES - RHS, 1)
    down2 = pltpu.roll(value, LANES - 2 * RHS, 1)
    of_first = value + down + down2
    of_second = up + value + down
    of_third = up2 + up + value
    return jnp.where(first, of_first, jnp.where(second, of_second, jnp.where(third, of_third, 1.0)))


def fetch(pairs, sems):
    copies = [pltpu.make_async_copy(source, target, sems.at[i]) for i, (source, target) in enumerate(pairs)]
    for copy in copies:
        copy.start()
    for copy in copies:
        copy.wait()


def prepare_kernel(ids, cells_hbm, field_hbm, jitter_hbm, vec_out, cells, field, jitter, work, wide, sems):
    fetch(((cells_hbm, cells), (field_hbm, field), (jitter_hbm, jitter)), sems)
    cell = cells[ids[0] * GROUP + ids[1]]
    work[...] = jnp.zeros_like(work)
    work[SITE : SITE + COMPS, 0:ATOMS] = block_sites(cell, jitter[...])
    wide[...] = work[...].T[0:ATOMS, :]
    for comp in range(COMPS):
        wide[:, comp * RHS : (comp + 1) * RHS] = field[comp]
    turned = wide[...]
    for slot in range(HALF):
        vec_out[slot] = turned


def block_sites(cell, jitter):
    comp = lax.broadcasted_iota(jnp.int32, (COMPS, ATOMS), 0)
    atom = lax.broadcasted_iota(jnp.int32, (COMPS, ATOMS), 1)
    inner = jnp.where(comp == 0, atom // 8, jnp.where(comp == 1, (atom // 2) % 4, atom % 2))
    corner = jnp.where(comp == 0, cell // 32 * 4, jnp.where(comp == 1, (cell // 4) % 8 * 4, cell % 4 * 2))
    return (corner + inner).astype(F32) * SPACING + jitter


def side_kernel(
    ids, species_hbm, alpha_hbm, tile_map_hbm, cells_hbm, jitters,
    aux_out, mask_out, column, species, alpha, tile_map, cells, work, sems
):
    fetch(
        ((species_hbm, species), (alpha_hbm, alpha), (tile_map_hbm, tile_map), (cells_hbm, cells)), sems
    )
    lane = lax.broadcasted_iota(jnp.int32, (4, LANES), 1)
    rhs_lane = jnp.where(lane >= 2 * RHS, lane - 2 * RHS, jnp.where(lane >= RHS, lane - RHS, lane))
    table = jnp.ones((4, LANES), F32)
    for freq in range(12):
        table = jnp.where(
            (rhs_lane >= 3 * freq) & (rhs_lane < 3 * freq + 3),
            jnp.broadcast_to(alpha[:, freq : freq + 1], (4, LANES)),
            table,
        )
    inverse = 1.0 / table
    shift = 0.25 * ((inverse[0:1] + inverse[1:2]) + (inverse[2:3] + inverse[3:4]))
    work[...] = jnp.zeros_like(work)
    work[0:1, 0:ATOMS] = species[...].astype(F32).reshape(1, ATOMS)
    kinds = jnp.broadcast_to(work[...].T[0:ATOMS, 0:1], (ATOMS, LANES))
    diag = jnp.zeros((ATOMS, LANES), F32)
    for kind in range(4):
        diag = jnp.where(kinds == float(kind), inverse[kind : kind + 1] - shift, diag)
    aux_out[0:ATOMS, :] = diag
    aux_out[ATOMS : ATOMS + SUMS, :] = jnp.broadcast_to(shift, (SUMS, LANES))

    blocks = GROUP * GROUP
    active = jnp.where(tile_map[...] != 0, 1.0, 0.0).astype(BF16)
    place = lax.broadcasted_iota(jnp.int32, (GROUP, blocks), 1)
    wanted = lax.broadcasted_iota(jnp.int32, (GROUP, blocks), 0) * GROUP + ids[1]
    pick = jnp.where(place == wanted, 1.0, 0.0).astype(BF16)
    lines = jnp.dot(pick, active, preferred_element_type=F32).astype(BF16)
    slot = lax.broadcasted_iota(jnp.int32, (blocks, WIDE), 1) // ATOMS
    wanted = ids[0] * GROUP + (slot % HALF) * 2 + ((ids[1] % 2) ^ (slot // HALF))
    place = lax.broadcasted_iota(jnp.int32, (blocks, WIDE), 0)
    spread = jnp.where(place == wanted, 1.0, 0.0).astype(BF16)
    mask_out[...] = 0.5 * jnp.dot(lines, spread, preferred_element_type=F32)

    work[...] = jnp.zeros_like(work)
    for slot in range(GROUP):
        cell = cells[slot * GROUP + ids[1]]
        work[slot * SUMS : slot * SUMS + COMPS, 0:ATOMS] = block_sites(cell, jitters[slot])
    down = work[...].T[0:ATOMS, :]
    for slot in range(GROUP):
        rows = slice(slot * ATOMS, (slot + 1) * ATOMS)
        for comp in range(COMPS):
            lane = slot * SUMS + comp
            column[comp, rows, :] = jnp.broadcast_to(down[:, lane : lane + 1], (ATOMS, LANES))


def right_side(vectors, side):
    first, second, third = component_lanes(NARROW)
    zero = jnp.zeros_like(vectors)
    up = pltpu.roll(vectors, RHS, 1)
    up2 = pltpu.roll(vectors, 2 * RHS, 1)
    down = pltpu.roll(vectors, LANES - RHS, 1)
    down2 = pltpu.roll(vectors, LANES - 2 * RHS, 1)
    parts = (
        jnp.where(first, vectors, jnp.where(third, -vectors, zero)),
        jnp.where(second, vectors, jnp.where(third, -vectors, zero)),
        jnp.where(first, down, jnp.where(second, up, zero)),
        jnp.where(first, down2, jnp.where(third, up2, zero)),
        jnp.where(second, down, jnp.where(third, up, zero)),
    )
    for slot, part in enumerate(parts):
        high = part.astype(BF16)
        low = (part - high.astype(F32)).astype(BF16)
        side[slot * NARROW : (slot + 1) * NARROW, 0:LANES] = high
        side[slot * NARROW : (slot + 1) * NARROW, LANES : 2 * LANES] = low


def product(high, low, side):
    both = jnp.dot(high[...], side[...], preferred_element_type=F32)
    rest = jnp.dot(low[...], side[:, 0:LANES], preferred_element_type=F32)
    return both[:, 0:LANES] + (both[:, LANES:] + rest)


def build(mask, vectors, column, high, low, first_lane):
    across = vectors.T[SITE : SITE + SUMS, :]
    across_x, across_y, across_z = across[0:1, :], across[1:2, :], across[2:3, :]

    def rows16(step, carry):
        rows = pl.ds(pl.multiple_of(step * 16, 16), 16)
        here_x, here_y, here_z = column[0, rows, :], column[1, rows, :], column[2, rows, :]
        keep = mask[pl.ds(step // 2, 1), :]
        for tile in range(NARROW // LANES):
            lanes = slice(tile * LANES, (tile + 1) * LANES)
            dx = here_x - across_x[:, lanes]
            dy = here_y - across_y[:, lanes]
            dz = here_z - across_z[:, lanes]
            xx = dx * dx
            yy = dy * dy
            distance2 = xx + yy + dz * dz
            square = jnp.maximum(distance2, 1.0)
            inverse = lax.rsqrt(square)
            damping = 1.0 + jnp.tanh(1.25 * (square * inverse) - 3.0)
            inverse2 = inverse * inverse
            kept = keep[:, first_lane + tile * LANES : first_lane + (tile + 1) * LANES]
            weight = damping * (inverse2 * inverse2 * inverse) * kept
            radial = weight * distance2
            minus3 = -3.0 * weight
            along_x = minus3 * dx
            along_y = minus3 * dy
            entries = (
                radial + minus3 * xx,
                radial + minus3 * yy,
                along_x * dy,
                along_x * dz,
                along_y * dz,
            )
            for slot, entry in enumerate(entries):
                top = entry.astype(BF16)
                at = slice(slot * NARROW + tile * LANES, slot * NARROW + (tile + 1) * LANES)
                high[rows, at] = top
                low[rows, at] = (entry - top.astype(F32)).astype(BF16)
        return carry

    lax.fori_loop(0, WIDE // 16, rows16, 0, unroll=4)


def first_own_kernel(mask, column, gathered, total, high, low, side):
    vectors = gathered[...].reshape(NARROW, LANES)
    right_side(vectors, side)
    build(mask, vectors, column, high, low, 0)
    total[...] = product(high, low, side)


def first_other_kernel(mask, column, gathered, total, part_out, high, low, side):
    vectors = gathered[...].reshape(NARROW, LANES)
    right_side(vectors, side)
    build(mask, vectors, column, high, low, NARROW)
    part_out[...] = (total[...] + product(high, low, side)).reshape(GROUP, ATOMS, LANES)


def spare_sums(vectors):
    return jnp.where(lane_ids(ATOMS) < COMPS * RHS, 0.0, jnp.sum(vectors, axis=0))


def second_own_kernel(gathered, high, low, total, side):
    vectors = gathered[...]
    right_side(vectors.reshape(NARROW, LANES), side)
    out = product(high, low, side).reshape(GROUP, ATOMS, LANES) + spare_sums(vectors)[None]
    total[...] = out


def second_other_kernel(gathered, high, low, total, part_out, side):
    vectors = gathered[...]
    right_side(vectors.reshape(NARROW, LANES), side)
    out = product(high, low, side).reshape(GROUP, ATOMS, LANES) + spare_sums(vectors)[None]
    part_out[...] = total[...] + out


def shifted_kernel(parts, own, aux, out, work):
    coupled = jnp.sum(parts[...], axis=0)
    inside = lane_ids(ATOMS) < COMPS * RHS
    vector = jnp.where(inside, own[0], 0.0)
    mapped = aux[0:ATOMS, :] * vector + coupled
    sums = jnp.zeros((SUMS, LANES), F32)
    row = lax.broadcasted_iota(jnp.int32, (SUMS, LANES), 0)
    for slot, terms in enumerate((vector * vector, vector * mapped, mapped * mapped)):
        sums = jnp.where(row == slot, jnp.sum(terms, axis=0, keepdims=True), sums)
    sums = sum_components(sums)
    work[...] = jnp.zeros_like(work)
    work[SUM_ROW : SUM_ROW + SUMS, :] = pltpu.roll(sums, 4, 0)
    work[SUM_ROW + SUMS : SUM_ROW + 2 * SUMS, :] = pltpu.roll(sums, LANES - ATOMS, 1)
    payload = jnp.where(inside, mapped, work[...].T[0:ATOMS, :])
    for slot in range(HALF):
        out[slot] = payload


def second_kernel(gathered, high, low, part_out, side):
    vectors = gathered[...]
    right_side(vectors.reshape(WIDE, LANES), side)
    sums = jnp.where(lane_ids(ATOMS) < COMPS * RHS, 0.0, jnp.sum(vectors, axis=0))
    part_out[...] = product(high, low, side).reshape(GROUP, ATOMS, LANES) + sums[None]


def step_kernel(parts, own, shifted, aux, sums_out, state, work):
    total = jnp.sum(parts[...], axis=0)
    vector = own[0]
    mapped = shifted[0]
    twice = aux[0:ATOMS, :] * mapped + total
    work[...] = jnp.zeros_like(work)
    work[0:ATOMS, :] = total
    turned = work[...].T
    lane8 = lane_ids(SUMS)
    head = pltpu.roll(turned[SUM_ROW : SUM_ROW + SUMS, :], 4, 0)
    tail = pltpu.roll(turned[SUM_ROW + SUMS : SUM_ROW + 2 * SUMS, :], ATOMS, 1)
    sums = jnp.where(lane8 < ATOMS, head, jnp.where(lane8 < RHS, tail, 0.0))
    sums = sums + pltpu.roll(sums, RHS, 1) + pltpu.roll(sums, 2 * RHS, 1)
    bb, be, ee = sums[0:1, :], sums[1:2, :], sums[2:3, :]
    shift = aux[ATOMS : ATOMS + 1, :]
    bm = shift * bb + be
    step = bb / bm
    kept = be / bm
    beta = (bb * ee - be * be) / (bm * bm)
    residual = kept * vector - step * mapped
    direction = residual + beta * vector
    image = shift * direction + ((kept + beta) * mapped - step * twice)
    row = lax.broadcasted_iota(jnp.int32, (SUMS, LANES), 0)
    squares = jnp.sum(residual * residual, axis=0, keepdims=True)
    curvature = jnp.sum(direction * image, axis=0, keepdims=True)
    both = sum_components(jnp.where(row == 0, squares, jnp.where(row == 1, curvature, 0.0)))
    lane = lax.broadcasted_iota(jnp.int32, (1, LANES), 1)
    packed = jnp.where(lane < RHS, both[0:1, :], jnp.where(lane < 2 * RHS, both[1:2, :], 0.0))
    sums_out[...] = jnp.broadcast_to(packed.reshape(1, 1, LANES), sums_out.shape)
    state[0] = step * vector
    state[1] = direction
    state[2] = residual
    state[3] = image


def finish_kernel(gathered, state, dipoles, residual):
    total = jnp.broadcast_to(jnp.sum(gathered[...], axis=0), (SUMS, LANES))
    first, second, third = component_lanes(SUMS)
    up = pltpu.roll(total, RHS, 1)
    up2 = pltpu.roll(total, 2 * RHS, 1)
    down = pltpu.roll(total, LANES - RHS, 1)
    squares = jnp.where(first, total, jnp.where(second, up, up2))
    curvature = jnp.where(first, down, jnp.where(second, total, jnp.where(third, up, 1.0)))
    step = (squares / curvature)[0:1, :]
    for out, value in (
        (dipoles, state[0] + step * state[1]),
        (residual, state[2] - step * state[3]),
    ):
        for comp in range(COMPS):
            out[comp] = value[:, comp * RHS : (comp + 1) * RHS]


def shape(*dims, dtype=F32):
    return jax.ShapeDtypeStruct(dims, dtype)


def whole(*dims):
    return pl.BlockSpec(dims, lambda i: (0,) * len(dims))


def core_swap(value):
    return lax.ppermute(value, "col", [(slot, slot ^ 1) for slot in range(GROUP)])


def gather_own(value):
    groups = [list(range(core, GROUP, 2)) for core in range(2)]
    return lax.all_to_all(value, "col", 0, 0, axis_index_groups=groups)


def local(external_field, jitter, species, alpha_table, block_cell, tile_map):
    ids = jnp.stack([lax.axis_index("row"), lax.axis_index("col")]).astype(jnp.int32)
    jitters = lax.all_to_all(jnp.broadcast_to(jitter, (GROUP, COMPS, ATOMS)), "row", 0, 0)
    vec = pl.pallas_call(
        prepare_kernel,
        out_shape=shape(HALF, ATOMS, LANES),
        in_specs=[SMEM, HBM, HBM, HBM],
        out_specs=VMEM,
        scratch_shapes=[
            pltpu.SMEM((GROUP * GROUP,), jnp.int32),
            pltpu.VMEM((COMPS, ATOMS, RHS), F32),
            pltpu.VMEM((COMPS, ATOMS), F32),
            SQUARE,
            pltpu.VMEM((ATOMS, LANES), F32),
            pltpu.SemaphoreType.DMA((3,)),
        ],
        compiler_params=PARAMS,
        name="prepare",
    )(ids, block_cell, external_field.transpose(0, 2, 1), jitter)
    ready, jitters = lax.optimization_barrier((vec, jitters))
    aux, mask, column = pl.pallas_call(
        side_kernel,
        out_shape=(shape(ATOMS + SUMS, LANES), shape(GROUP, WIDE), shape(COMPS, WIDE, LANES)),
        in_specs=[SMEM, HBM, HBM, HBM, HBM, VMEM],
        out_specs=(VMEM, VMEM, VMEM),
        scratch_shapes=[
            pltpu.VMEM((ATOMS,), jnp.int32),
            pltpu.VMEM((4, 12), F32),
            pltpu.VMEM((GROUP * GROUP, GROUP * GROUP), jnp.int32),
            pltpu.SMEM((GROUP * GROUP,), jnp.int32),
            SQUARE,
            pltpu.SemaphoreType.DMA((4,)),
        ],
        compiler_params=PARAMS,
        name="side",
    )(ids, species, alpha_table.T, tile_map, block_cell, jitters)
    own = gather_own(ready)
    own, aux, mask, column = lax.optimization_barrier((own, aux, mask, column))
    other = core_swap(own)
    side = pltpu.VMEM((PAIRS * NARROW, 2 * LANES), BF16)
    tile = shape(WIDE, PAIRS * NARROW, dtype=BF16)
    total, high0, low0 = pl.pallas_call(
        first_own_kernel,
        out_shape=(shape(WIDE, LANES), tile, tile),
        in_specs=[VMEM] * 3,
        out_specs=(VMEM, VMEM, VMEM),
        scratch_shapes=[side],
        compiler_params=PARAMS,
        name="first_own",
    )(mask, column, own)
    part, high1, low1 = pl.pallas_call(
        first_other_kernel,
        out_shape=(shape(GROUP, ATOMS, LANES), tile, tile),
        in_specs=[VMEM] * 4,
        out_specs=(VMEM, VMEM, VMEM),
        scratch_shapes=[side],
        compiler_params=PARAMS,
        name="first_other",
    )(mask, column, other, total)
    parts = lax.all_to_all(part, "row", 0, 0)
    blocks = whole(GROUP, ATOMS, LANES)
    block = whole(1, ATOMS, LANES)
    shifted = pl.pallas_call(
        shifted_kernel,
        grid=(1,),
        out_shape=shape(HALF, ATOMS, LANES),
        in_specs=[blocks, block, whole(ATOMS + SUMS, LANES)],
        out_specs=whole(HALF, ATOMS, LANES),
        scratch_shapes=[SQUARE],
        compiler_params=PARAMS,
        name="shifted",
    )(parts, vec, aux)
    own2 = gather_own(shifted)
    other2 = core_swap(own2)
    total2 = pl.pallas_call(
        second_own_kernel,
        out_shape=shape(GROUP, ATOMS, LANES),
        in_specs=[VMEM] * 3,
        out_specs=VMEM,
        scratch_shapes=[side],
        compiler_params=PARAMS,
        name="second_own",
    )(own2, high0, low0)
    part2 = pl.pallas_call(
        second_other_kernel,
        out_shape=shape(GROUP, ATOMS, LANES),
        in_specs=[VMEM] * 4,
        out_specs=VMEM,
        scratch_shapes=[side],
        compiler_params=PARAMS,
        name="second_other",
    )(other2, high1, low1, total2)
    parts2 = lax.all_to_all(part2, "row", 0, 0)
    sums, state = pl.pallas_call(
        step_kernel,
        grid=(1,),
        out_shape=(shape(GROUP * GROUP, 1, LANES), shape(4, ATOMS, LANES)),
        in_specs=[blocks, block, block, whole(ATOMS + SUMS, LANES)],
        out_specs=(whole(GROUP * GROUP, 1, LANES), whole(4, ATOMS, LANES)),
        scratch_shapes=[SQUARE],
        compiler_params=PARAMS,
        name="step",
    )(parts2, vec, shifted, aux)
    all_sums = lax.all_to_all(sums, ("row", "col"), 0, 0)
    dipoles, residual = pl.pallas_call(
        finish_kernel,
        out_shape=(shape(COMPS, ATOMS, RHS), shape(COMPS, ATOMS, RHS)),
        in_specs=[VMEM, VMEM],
        out_specs=(VMEM, VMEM),
        compiler_params=PARAMS,
        name="finish",
    )(all_sums, state)
    return dipoles.transpose(0, 2, 1), residual.transpose(0, 2, 1)


def solution(mesh):
    return jax.shard_map(
        local,
        mesh=mesh,
        in_specs=(
            P(None, None, ("row", "col")),
            P(None, ("row", "col")),
            P(("row", "col")),
            P(),
            P(),
            P(),
        ),
        out_specs=(P(None, None, ("row", "col")), P(None, None, ("row", "col"))),
        check_vma=False,
    )
```

time: 110 us -> 101 us (0.918)
  blocking collectives: 94.1 us -> 52.3 us
  starting transfers between devices: 0 us -> 21.6 us
  waiting for transfers between devices: 0 us -> 5.75 us
  Pallas kernels: 8.61 us -> 13.1 us
    all_to_all x5 -> x3, blocking collectives: 76.5 us -> 33.1 us  [the longest x1 11.8 us: local(): parts = lax.all_to_all(part, 'row', 0, 0)]
    all_to_all x0 -> x2, starting transfers between devices: none -> 15.8 us  [the longest x1 8.19 us: gather_own(): return lax.all_to_all(value, 'col', 0, 0, axis_index_groups=groups)]
    ppermute x0 -> x2, starting transfers between devices: none -> 5.86 us  [core_swap(): lax.ppermute(value, 'col', [(slot, slot ^ 1) for slot in range(GROUP)])]
    all_to_all x0 -> x2, waiting for transfers between devices: none -> 5.65 us  [the longest x1 3.31 us: gather_own(): return lax.all_to_all(value, 'col', 0, 0, axis_index_groups=groups)]
    pallas_call x5 -> x8, Pallas kernels: 8.35 us -> 12 us  [the longest x1 2.31 us: local(): pl.pallas_call(first_other_kernel, out_shape=(shape(GROUP, ATOMS, LANES),...]
    all_to_all x1, blocking collectives: 17.6 us -> 19.2 us  [local(): all_sums = lax.all_to_all(sums, ('row', 'col'), 0, 0)]
    pallas_call x2 -> x0, local copies, waits for them, and re-layouts: 1.43 us -> none  [local(): pl.pallas_call(finish_kernel, out_shape=(shape(COMPS, RHS, ATOMS), shape(...]
    broadcast_in_dim x0 -> x1, local copies, waits for them, and re-layouts: none -> 1.3 us  [local(): jnp.broadcast_to(jitter, (GROUP, COMPS, ATOMS))]
  transfers between devices with their start and end apart: 0 -> 4, of which waited for: 0 -> 3; matrix products, arithmetic and copies ran while one was open for 0% -> 0% of each run, Pallas kernels for 0% -> 7%
where the time goes in v2:
time: 101 us; the launch traced here: 100 us
  blocking collectives  52.3 us (52%)
  starting transfers between devices  21.6 us (21%)
  Pallas kernels  13.1 us (13%)
  local copies, waits for them, and re-layouts  6.42 us (6%)
  waiting for transfers between devices  5.75 us (6%)
    all_to_all x1, blocking collectives, local(): all_sums = lax.all_to_all(sums, ('row', 'col'), 0, 0)  19.2 us
    all_to_all x1, blocking collectives, local(): parts = lax.all_to_all(part, 'row', 0, 0)  11.8 us
    all_to_all x1, blocking collectives, local(): parts2 = lax.all_to_all(part2, 'row', 0, 0)  10.7 us
    all_to_all x1, blocking collectives, gather_own(): return lax.all_to_all(value, 'col', 0, 0, axis_index_groups=groups)  10.5 us
    all_to_all x1, starting transfers between devices, gather_own(): return lax.all_to_all(value, 'col', 0, 0, axis_index_groups=groups)  8.19 us
    all_to_all x1, starting transfers between devices, local(): lax.all_to_all(jnp.broadcast_to(jitter, (GROUP, COMPS, ATOMS)), 'row', 0, 0)  7.58 us
    ppermute x2, starting transfers between devices, core_swap(): lax.ppermute(value, 'col', [(slot, slot ^ 1) for slot in range(GROUP)])  5.86 us
    unnamed x14, local copies, waits for them, and re-layouts  5.12 us
  transfers between devices with their start and end apart: 4, of which 3 were waited for; matrix products, arithmetic and copies ran while one was open for 0% of the time, Pallas kernels for 7%

profile of v2, /device:TPU:1, one launch (start us, length us, event | category | flops | bytes accessed | tf_op | source)
XLA Modules:
  0.0 100.0 jit_solution(10684168439428086500)
XLA Ops:
  0.6 1.3 %broadcast_in_dim.3 = f32[16,3,32]{2,1,0:T(4,128)} broadcast(f32[3,32]{1,0:T(4,128)} %jitter_hbm.1), dimensions={1,2} | broadcast | bytes 6528 | tf_op jit(solution)/shard_map/broadcast_in_dim | solution.py:333
  1.9 7.6 %all-to-all-start = ((f32[16,3,32]{2,1,0:T(4,128)}), f32[16,3,32]{2,1,0:T(4,128)S(1)}, u32[]{:S(2)}, u32[]{:S(2)}) async-start(f32[16,3,32]{2,1,0:T(4,128)} %broadcast_in_dim.3), calls=%async_computation | async-start | bytes 65536 | tf_op jit(solution)/shard_map/all_to_all | solution.py:333
  9.5 0.1 pad_add_fusion.ids
  9.6 0.0 copy-start.1
  9.6 0.8 copy-done.1
  10.4 0.0 copy-start.2
  10.4 0.7 copy-done.2
  11.1 0.7 copy-done.3
  11.8 1.9 %prepare.1.own = f32[8,32,128]{2,1,0:T(8,128)} custom-call(s32[2]{0:T(128)S(1)} %pad_add_fusion.ids, s32[256]{0:T(256)S(1)} %copy-done.3, f32[3,32,36]{2,1,0:T(8,128)S(1)} %bitcast.6, f32[3,32]{1,0:T(4,128)S(1)} %copy-done.2), custom_call_target="tpu_custom_call" | custom-call | tf_op jit(solution)/shard_map/prepare/pallas_call | solution.py:334
  13.7 2.3 %all-to-all-done.jitters = f32[16,3,32]{2,1,0:T(4,128)S(1)} async-done(((f32[16,3,32]{2,1,0:T(4,128)}), f32[16,3,32]{2,1,0:T(4,128)S(1)}, u32[]{:S(2)}, u32[]{:S(2)}) %all-to-all-start) | async-done | bytes 6176 | tf_op jit(solution)/shard_map/all_to_all | solution.py:333
  16.0 8.2 %all-to-all-start.1 = ((f32[8,32,128]{2,1,0:T(8,128)}), f32[8,32,128]{2,1,0:T(8,128)S(1)}, u32[]{:S(2)}, u32[]{:S(2)}) async-start(f32[8,32,128]{2,1,0:T(8,128)} %prepare.1.own), calls=%async_computation.1 | async-start | bytes 262144 | tf_op jit(solution)/shard_map/all_to_all | solution.py:328
  24.2 0.9 copy-done
  25.1 0.7 copy-done.4
  25.8 0.7 copy-done.5
  26.5 0.7 copy-done.6
  27.1 1.7 %side.1 = (f32[40,128]{1,0:T(8,128)S(1)}, f32[16,512]{1,0:T(8,128)S(1)}, f32[3,512,128]{2,1,0:T(8,128)S(1)}) custom-call(s32[2]{0:T(128)S(1)} %pad_add_fusion.ids, s32[32]{0:T(128)S(1)} %copy-done.6, f32[4,12]{1,0:T(4,128)S(1)} %bitcast.7, s32[256,256]{1,0:T(8,128)S(1)} %copy-done, s32[256]{0:T(256)S(1)} %copy-done.4, f32[16,3,32]{2,1,0:T(4,128)S(1)} %all-to-all-done.jitters), custom_call_target="tpu_custom_call" | custom-call | tf_op jit(solution)/shard_map/side/pallas_call | solution.py:351
  28.9 3.3 %all-to-all-done.1.gathered = f32[8,32,128]{2,1,0:T(8,128)S(1)} async-done(((f32[8,32,128]{2,1,0:T(8,128)}), f32[8,32,128]{2,1,0:T(8,128)S(1)}, u32[]{:S(2)}, u32[]{:S(2)}) %all-to-all-start.1) | async-done | bytes 131104 | tf_op jit(solution)/shard_map/all_to_all | solution.py:328
  32.2 3.4 %collective-permute-start = (f32[8,32,128]{2,1,0:T(8,128)S(1)}, f32[8,32,128]{2,1,0:T(8,128)S(1)}, u32[]{:S(2)}, u32[]{:S(2)}) collective-permute-start(f32[8,32,128]{2,1,0:T(8,128)S(1)} %all-to-all-done.1.gathered), channel_id=1, source_target_pairs={{0,1},{1,0},{2,3},{3,2},{4,5},{5,4},{6,7},{7,6},{8,9},{9,8},{10,11... | collective-permute-start | bytes 393224 | tf_op jit(solution)/shard_map/ppermute | solution.py:323
  35.6 2.3 %first_own.1 = (f32[512,128]{1,0:T(8,128)S(1)}, bf16[512,1280]{1,0:T(8,128)(2,1)S(1)}, bf16[512,1280]{1,0:T(8,128)(2,1)S(1)}) custom-call(f32[16,512]{1,0:T(8,128)S(1)} %get-tuple-element.26.mask, f32[3,512,128]{2,1,0:T(8,128)S(1)} %get-tuple-element.27.column, f32[8,32,128]{2,1,0:T(8,128)S(1)} %all-to-all-done.1.gathered), custom_call_target="tpu_custom_call" | custom-call | tf_op jit(solution)/shard_map/first_own/pallas_call | solution.py:372
  37.9 0.0 collective-permute-done.gathered
  38.0 2.3 %first_other.1 = (f32[16,32,128]{2,1,0:T(8,128)S(1)}, bf16[512,1280]{1,0:T(8,128)(2,1)S(1)}, bf16[512,1280]{1,0:T(8,128)(2,1)S(1)}) custom-call(f32[16,512]{1,0:T(8,128)S(1)} %get-tuple-element.26.mask, f32[3,512,128]{2,1,0:T(8,128)S(1)} %get-tuple-element.27.column, f32[8,32,128]{2,1,0:T(8,128)S(1)} %collective-permute-done.gathered, ...), custom_call_target="tpu_custom_call" | custom-call | tf_op jit(solution)/shard_map/first_other/pallas_call | solution.py:381
  40.3 11.8 %all_to_all.30.parts = f32[16,32,128]{2,1,0:T(8,128)S(1)} all-to-all(f32[16,32,128]{2,1,0:T(8,128)S(1)} %get-tuple-element.30), channel_id=1, replica_groups=mesh['row'=16,'col'=16] {'row'}, dimensions={0} | all-to-all | bytes 524288 | tf_op jit(solution)/shard_map/all_to_all | solution.py:390
  52.1 0.9 shifted.1
  53.0 10.5 %all_to_all.31.gathered = f32[8,32,128]{2,1,0:T(8,128)S(1)} all-to-all(f32[8,32,128]{2,1,0:T(8,128)S(1)} %shifted.1), channel_id=1, replica_groups={{0,2,4,6,8,10,12,14},{1,3,5,7,9,11,13,15},{16,18,20,22,24,26,28,30},{17..., dimensions={0} | all-to-all | bytes 262144 | tf_op jit(solution)/shard_map/all_to_all | solution.py:328
  63.5 2.4 %collective-permute-start.1 = (f32[8,32,128]{2,1,0:T(8,128)S(1)}, f32[8,32,128]{2,1,0:T(8,128)S(1)}, u32[]{:S(2)}, u32[]{:S(2)}) collective-permute-start(f32[8,32,128]{2,1,0:T(8,128)S(1)} %all_to_all.31.gathered), channel_id=1, source_target_pairs={{0,1},{1,0},{2,3},{3,2},{4,5},{5,4},{6,7},{7,6},{8,9},{9,8},{10,11... | collective-permute-start | bytes 393224 | tf_op jit(solution)/shard_map/ppermute | solution.py:323
  66.0 0.9 second_own.1.total
  66.8 0.1 collective-permute-done.1.gathered
  66.9 0.9 second_other.1
  67.8 10.7 %all_to_all.32.parts = f32[16,32,128]{2,1,0:T(8,128)S(1)} all-to-all(f32[16,32,128]{2,1,0:T(8,128)S(1)} %second_other.1), channel_id=1, replica_groups=mesh['row'=16,'col'=16] {'row'}, dimensions={0} | all-to-all | bytes 524288 | tf_op jit(solution)/shard_map/all_to_all | solution.py:423
  78.6 1.1 %step.1 = (f32[256,1,128]{2,1,0:T(1,128)S(1)}, f32[4,32,128]{2,1,0:T(8,128)S(1)}) custom-call(f32[16,32,128]{2,1,0:T(8,128)S(1)} %all_to_all.32.parts, f32[8,32,128]{2,1,0:T(8,128)} %prepare.1.own, f32[8,32,128]{2,1,0:T(8,128)S(1)} %shifted.1, f32[40,128]{1,0:T(8,128)S(1)} %get-tuple-element.31.aux), custom_call_target="tpu_custom_call" | custom-call | tf_op jit(solution)/shard_map/step/pallas_call | solution.py:424
  79.7 19.2 %all_to_all.33.gathered = f32[256,1,128]{2,1,0:T(1,128)S(1)} all-to-all(f32[256,1,128]{2,1,0:T(1,128)S(1)} %get-tuple-element.36), channel_id=1, replica_groups=mesh['row'=16,'col'=16] {'row','col'}, dimensions={0} | all-to-all | bytes 262144 | tf_op jit(solution)/shard_map/all_to_all | solution.py:434
  99.0 1.1 %finish.1 = (f32[3,32,36]{2,1,0:T(8,128)}, f32[3,32,36]{2,1,0:T(8,128)}) custom-call(f32[256,1,128]{2,1,0:T(1,128)S(1)} %all_to_all.33.gathered, f32[4,32,128]{2,1,0:T(8,128)S(1)} %get-tuple-element.37.state), custom_call_target="tpu_custom_call" | custom-call | tf_op jit(solution)/shard_map/finish/pallas_call | solution.py:435
  (5 shorter events, 0.0 us)
Async XLA Ops:
  1.9 14.1 %all-to-all-start = ((f32[16,3,32]{2,1,0:T(4,128)}), f32[16,3,32]{2,1,0:T(4,128)S(1)}, u32[]{:S(2)}, u32[]{:S(2)}) async-start(f32[16,3,32]{2,1,0:T(4,128)} %broadcast_in_dim.3), calls=%async_computation | async-start | bytes 65536 | tf_op jit(solution)/shard_map/all_to_all | solution.py:333
  9.6 0.8 copy-start.1
  10.4 0.7 copy-start.2
  11.1 0.7 copy-start.3
  16.0 16.2 %all-to-all-start.1 = ((f32[8,32,128]{2,1,0:T(8,128)}), f32[8,32,128]{2,1,0:T(8,128)S(1)}, u32[]{:S(2)}, u32[]{:S(2)}) async-start(f32[8,32,128]{2,1,0:T(8,128)} %prepare.1.own), calls=%async_computation.1 | async-start | bytes 262144 | tf_op jit(solution)/shard_map/all_to_all | solution.py:328
  24.2 0.9 copy-start
  25.1 0.7 copy-start.4
  25.8 0.7 copy-start.5
  26.5 0.7 copy-start.6
  32.2 5.7 %collective-permute-start = (f32[8,32,128]{2,1,0:T(8,128)S(1)}, f32[8,32,128]{2,1,0:T(8,128)S(1)}, u32[]{:S(2)}, u32[]{:S(2)}) collective-permute-start(f32[8,32,128]{2,1,0:T(8,128)S(1)} %all-to-all-done.1.gathered), channel_id=1, source_target_pairs={{0,1},{1,0},{2,3},{3,2},{4,5},{5,4},{6,7},{7,6},{8,9},{9,8},{10,11... | collective-permute-start | bytes 393224 | tf_op jit(solution)/shard_map/ppermute | solution.py:323
  63.5 3.4 %collective-permute-start.1 = (f32[8,32,128]{2,1,0:T(8,128)S(1)}, f32[8,32,128]{2,1,0:T(8,128)S(1)}, u32[]{:S(2)}, u32[]{:S(2)}) collective-permute-start(f32[8,32,128]{2,1,0:T(8,128)S(1)} %all_to_all.31.gathered), channel_id=1, source_target_pairs={{0,1},{1,0},{2,3},{3,2},{4,5},{5,4},{6,7},{7,6},{8,9},{9,8},{10,11... | collective-permute-start | bytes 393224 | tf_op jit(solution)/shard_map/ppermute | solution.py:323

commit v3 on v2

--- a/solution.py
+++ b/solution.py
@@ -3,7 +3,7 @@
 from jax import lax
 from jax.experimental import pallas as pl
 from jax.experimental.pallas import tpu as pltpu
-from jax.sharding import PartitionSpec as P
+from jax.sharding import Mesh, PartitionSpec as P
 
 COMPS = 3
 RHS = 36
@@ -16,6 +16,7 @@
 SUM_ROW = 104
 WIDE = GROUP * ATOMS
 NARROW = HALF * ATOMS
+CHUNK = 256
 PAIRS = 5
 SPACING = 2.0
 F32 = jnp.float32
@@ -25,7 +26,7 @@
 SMEM = pl.BlockSpec(memory_space=pltpu.SMEM)
 HBM = pl.BlockSpec(memory_space=pltpu.HBM)
 SQUARE = pltpu.VMEM((LANES, LANES), F32)
-PARAMS = pltpu.CompilerParams(vmem_limit_bytes=40 * 1024 * 1024)
+PARAMS = pltpu.CompilerParams(vmem_limit_bytes=16 * 1024 * 1024)
 
 
 def lane_ids(rows):
@@ -60,7 +61,7 @@
         copy.wait()
 
 
-def prepare_kernel(ids, cells_hbm, field_hbm, jitter_hbm, vec_out, cells, field, jitter, work, wide, sems):
+def prepare_kernel(ids, cells_hbm, field_hbm, jitter_hbm, vec_out, own_out, cells, field, jitter, work, wide, sems):
     fetch(((cells_hbm, cells), (field_hbm, field), (jitter_hbm, jitter)), sems)
     cell = cells[ids[0] * GROUP + ids[1]]
     work[...] = jnp.zeros_like(work)
@@ -69,6 +70,7 @@
     for comp in range(COMPS):
         wide[:, comp * RHS : (comp + 1) * RHS] = field[comp]
     turned = wide[...]
+    own_out[...] = turned
     for slot in range(HALF):
         vec_out[slot] = turned
 
@@ -154,19 +156,19 @@
 
 
 def product(high, low, side):
-    both = jnp.dot(high[...], side[...], preferred_element_type=F32)
-    rest = jnp.dot(low[...], side[:, 0:LANES], preferred_element_type=F32)
+    both = jnp.dot(high, side[...], preferred_element_type=F32)
+    rest = jnp.dot(low, side[:, 0:LANES], preferred_element_type=F32)
     return both[:, 0:LANES] + (both[:, LANES:] + rest)
 
 
-def build(mask, vectors, column, high, low, first_lane):
+def build_and_apply(mask, vectors, column, high, low, side, first_lane):
     across = vectors.T[SITE : SITE + SUMS, :]
     across_x, across_y, across_z = across[0:1, :], across[1:2, :], across[2:3, :]
 
-    def rows16(step, carry):
-        rows = pl.ds(pl.multiple_of(step * 16, 16), 16)
+    def rows16(step):
+        rows = slice(step * 16, (step + 1) * 16)
         here_x, here_y, here_z = column[0, rows, :], column[1, rows, :], column[2, rows, :]
-        keep = mask[pl.ds(step // 2, 1), :]
+        keep = mask[step // 2 : step // 2 + 1, :]
         for tile in range(NARROW // LANES):
             lanes = slice(tile * LANES, (tile + 1) * LANES)
             dx = here_x - across_x[:, lanes]
@@ -197,23 +199,27 @@
                 at = slice(slot * NARROW + tile * LANES, slot * NARROW + (tile + 1) * LANES)
                 high[rows, at] = top
                 low[rows, at] = (entry - top.astype(F32)).astype(BF16)
-        return carry
-
-    lax.fori_loop(0, WIDE // 16, rows16, 0, unroll=4)
+
+    outs = []
+    for chunk in range(0, WIDE, CHUNK):
+        for step in range(chunk // 16, (chunk + CHUNK) // 16):
+            rows16(step)
+        rows = slice(chunk, chunk + CHUNK)
+        outs.append(product(high[rows, :], low[rows, :], side))
+    return jnp.concatenate(outs, axis=0)
 
 
 def first_own_kernel(mask, column, gathered, total, high, low, side):
     vectors = gathered[...].reshape(NARROW, LANES)
     right_side(vectors, side)
-    build(mask, vectors, column, high, low, 0)
-    total[...] = product(high, low, side)
+    total[...] = build_and_apply(mask, vectors, column, high, low, side, 0)
 
 
 def first_other_kernel(mask, column, gathered, total, part_out, high, low, side):
     vectors = gathered[...].reshape(NARROW, LANES)
     right_side(vectors, side)
-    build(mask, vectors, column, high, low, NARROW)
-    part_out[...] = (total[...] + product(high, low, side)).reshape(GROUP, ATOMS, LANES)
+    out = build_and_apply(mask, vectors, column, high, low, side, NARROW)
+    part_out[...] = (total[...] + out).reshape(GROUP, ATOMS, LANES)
 
 
 def spare_sums(vectors):
@@ -223,21 +229,21 @@
 def second_own_kernel(gathered, high, low, total, side):
     vectors = gathered[...]
     right_side(vectors.reshape(NARROW, LANES), side)
-    out = product(high, low, side).reshape(GROUP, ATOMS, LANES) + spare_sums(vectors)[None]
+    out = product(high[...], low[...], side).reshape(GROUP, ATOMS, LANES) + spare_sums(vectors)[None]
     total[...] = out
 
 
 def second_other_kernel(gathered, high, low, total, part_out, side):
     vectors = gathered[...]
     right_side(vectors.reshape(NARROW, LANES), side)
-    out = product(high, low, side).reshape(GROUP, ATOMS, LANES) + spare_sums(vectors)[None]
+    out = product(high[...], low[...], side).reshape(GROUP, ATOMS, LANES) + spare_sums(vectors)[None]
     part_out[...] = total[...] + out
 
 
 def shifted_kernel(parts, own, aux, out, work):
     coupled = jnp.sum(parts[...], axis=0)
     inside = lane_ids(ATOMS) < COMPS * RHS
-    vector = jnp.where(inside, own[0], 0.0)
+    vector = jnp.where(inside, own[...], 0.0)
     mapped = aux[0:ATOMS, :] * vector + coupled
     sums = jnp.zeros((SUMS, LANES), F32)
     row = lax.broadcasted_iota(jnp.int32, (SUMS, LANES), 0)
@@ -256,12 +262,12 @@
     vectors = gathered[...]
     right_side(vectors.reshape(WIDE, LANES), side)
     sums = jnp.where(lane_ids(ATOMS) < COMPS * RHS, 0.0, jnp.sum(vectors, axis=0))
-    part_out[...] = product(high, low, side).reshape(GROUP, ATOMS, LANES) + sums[None]
+    part_out[...] = product(high[...], low[...], side).reshape(GROUP, ATOMS, LANES) + sums[None]
 
 
 def step_kernel(parts, own, shifted, aux, sums_out, state, work):
     total = jnp.sum(parts[...], axis=0)
-    vector = own[0]
+    vector = own[...]
     mapped = shifted[0]
     twice = aux[0:ATOMS, :] * mapped + total
     work[...] = jnp.zeros_like(work)
@@ -287,15 +293,20 @@
     both = sum_components(jnp.where(row == 0, squares, jnp.where(row == 1, curvature, 0.0)))
     lane = lax.broadcasted_iota(jnp.int32, (1, LANES), 1)
     packed = jnp.where(lane < RHS, both[0:1, :], jnp.where(lane < 2 * RHS, both[1:2, :], 0.0))
-    sums_out[...] = jnp.broadcast_to(packed.reshape(1, 1, LANES), sums_out.shape)
+    sums_out[...] = jnp.broadcast_to(packed, sums_out.shape)
     state[0] = step * vector
     state[1] = direction
     state[2] = residual
     state[3] = image
 
 
+def pair_kernel(sums, swapped, out):
+    out[...] = jnp.broadcast_to((sums[...] + swapped[...])[None], out.shape)
+
+
 def finish_kernel(gathered, state, dipoles, residual):
-    total = jnp.broadcast_to(jnp.sum(gathered[...], axis=0), (SUMS, LANES))
+    total = jnp.sum(gathered[...], axis=0)
+    total = jnp.broadcast_to(jnp.sum(total, axis=0, keepdims=True), (SUMS, LANES))
     first, second, third = component_lanes(SUMS)
     up = pltpu.roll(total, RHS, 1)
     up2 = pltpu.roll(total, 2 * RHS, 1)
@@ -320,22 +331,21 @@
 
 
 def core_swap(value):
-    return lax.ppermute(value, "col", [(slot, slot ^ 1) for slot in range(GROUP)])
+    return lax.ppermute(value, "core", [(0, 1), (1, 0)])
 
 
 def gather_own(value):
-    groups = [list(range(core, GROUP, 2)) for core in range(2)]
-    return lax.all_to_all(value, "col", 0, 0, axis_index_groups=groups)
+    return lax.all_to_all(value, "z", 0, 0)
 
 
 def local(external_field, jitter, species, alpha_table, block_cell, tile_map):
-    ids = jnp.stack([lax.axis_index("row"), lax.axis_index("col")]).astype(jnp.int32)
+    ids = jnp.stack([lax.axis_index("row"), lax.axis_index(("z", "core"))]).astype(jnp.int32)
     jitters = lax.all_to_all(jnp.broadcast_to(jitter, (GROUP, COMPS, ATOMS)), "row", 0, 0)
-    vec = pl.pallas_call(
+    vec, vector = pl.pallas_call(
         prepare_kernel,
-        out_shape=shape(HALF, ATOMS, LANES),
+        out_shape=(shape(HALF, ATOMS, LANES), shape(ATOMS, LANES)),
         in_specs=[SMEM, HBM, HBM, HBM],
-        out_specs=VMEM,
+        out_specs=(VMEM, VMEM),
         scratch_shapes=[
             pltpu.SMEM((GROUP * GROUP,), jnp.int32),
             pltpu.VMEM((COMPS, ATOMS, RHS), F32),
@@ -347,7 +357,6 @@
         compiler_params=PARAMS,
         name="prepare",
     )(ids, block_cell, external_field.transpose(0, 2, 1), jitter)
-    ready, jitters = lax.optimization_barrier((vec, jitters))
     aux, mask, column = pl.pallas_call(
         side_kernel,
         out_shape=(shape(ATOMS + SUMS, LANES), shape(GROUP, WIDE), shape(COMPS, WIDE, LANES)),
@@ -364,7 +373,7 @@
         compiler_params=PARAMS,
         name="side",
     )(ids, species, alpha_table.T, tile_map, block_cell, jitters)
-    own = gather_own(ready)
+    own = gather_own(vec)
     own, aux, mask, column = lax.optimization_barrier((own, aux, mask, column))
     other = core_swap(own)
     side = pltpu.VMEM((PAIRS * NARROW, 2 * LANES), BF16)
@@ -394,12 +403,12 @@
         shifted_kernel,
         grid=(1,),
         out_shape=shape(HALF, ATOMS, LANES),
-        in_specs=[blocks, block, whole(ATOMS + SUMS, LANES)],
+        in_specs=[blocks, whole(ATOMS, LANES), whole(ATOMS + SUMS, LANES)],
         out_specs=whole(HALF, ATOMS, LANES),
         scratch_shapes=[SQUARE],
         compiler_params=PARAMS,
         name="shifted",
-    )(parts, vec, aux)
+    )(parts, vector, aux)
     own2 = gather_own(shifted)
     other2 = core_swap(own2)
     total2 = pl.pallas_call(
@@ -424,14 +433,23 @@
     sums, state = pl.pallas_call(
         step_kernel,
         grid=(1,),
-        out_shape=(shape(GROUP * GROUP, 1, LANES), shape(4, ATOMS, LANES)),
-        in_specs=[blocks, block, block, whole(ATOMS + SUMS, LANES)],
-        out_specs=(whole(GROUP * GROUP, 1, LANES), whole(4, ATOMS, LANES)),
+        out_shape=(shape(SUMS, LANES), shape(4, ATOMS, LANES)),
+        in_specs=[blocks, whole(ATOMS, LANES), block, whole(ATOMS + SUMS, LANES)],
+        out_specs=(whole(SUMS, LANES), whole(4, ATOMS, LANES)),
         scratch_shapes=[SQUARE],
         compiler_params=PARAMS,
         name="step",
-    )(parts2, vec, shifted, aux)
-    all_sums = lax.all_to_all(sums, ("row", "col"), 0, 0)
+    )(parts2, vector, shifted, aux)
+    pair = pl.pallas_call(
+        pair_kernel,
+        out_shape=shape(GROUP, SUMS, LANES),
+        in_specs=[VMEM, VMEM],
+        out_specs=VMEM,
+        compiler_params=PARAMS,
+        name="pair",
+    )(sums, core_swap(sums))
+    pair = pair.reshape(GROUP * HALF, 1, LANES)
+    all_sums = lax.all_to_all(pair, ("row", "z"), 0, 0).reshape(GROUP, SUMS, LANES)
     dipoles, residual = pl.pallas_call(
         finish_kernel,
         out_shape=(shape(COMPS, ATOMS, RHS), shape(COMPS, ATOMS, RHS)),
@@ -444,17 +462,12 @@
 
 
 def solution(mesh):
+    split = Mesh(mesh.devices.reshape(GROUP, HALF, 2), ("row", "z", "core"))
+    every = ("row", "z", "core")
     return jax.shard_map(
         local,
-        mesh=mesh,
-        in_specs=(
-            P(None, None, ("row", "col")),
-            P(None, ("row", "col")),
-            P(("row", "col")),
-            P(),
-            P(),
-            P(),
-        ),
-        out_specs=(P(None, None, ("row", "col")), P(None, None, ("row", "col"))),
+        mesh=split,
+        in_specs=(P(None, None, every), P(None, every), P(every), P(), P(), P()),
+        out_specs=(P(None, None, every), P(None, None, every)),
         check_vma=False,
     )

time: 101 us -> 96.9 us (0.959)
  blocking collectives: 52.3 us -> 49.2 us
  Pallas kernels: 13.1 us -> 10.1 us
  starting transfers between devices: 21.6 us -> 23.2 us
    all_to_all x2, blocking collectives: 29.7 us -> 26.6 us  [the longest x1 16.1 us: local(): lax.all_to_all(pair, ('row', 'z'), 0, 0).reshape(GROUP, SUMS, LANES)]
    ppermute x2 -> x3, starting transfers between devices: 5.86 us -> 7.41 us  [core_swap(): return lax.ppermute(value, 'core', [(0, 1), (1, 0)])]
    pallas_call x2 -> x3, Pallas kernels: 3.02 us -> 2.24 us  [the longest x1 1.89 us: local(): pl.pallas_call(prepare_kernel, out_shape=(shape(HALF, ATOMS, LANES), shap...]
  transfers between devices with their start and end apart: 4 -> 5, of which waited for: 3 -> 4; matrix products, arithmetic and copies ran while one was open for 0% -> 0% of each run, Pallas kernels for 7% -> 6%
where the time goes in v3:
time: 96.9 us; the launch traced here: 96.3 us
  blocking collectives  49.2 us (51%)
  starting transfers between devices  23.2 us (24%)
  Pallas kernels  10.1 us (10%)
  waiting for transfers between devices  6.57 us (7%)
  local copies, waits for them, and re-layouts  6.42 us (7%)
    all_to_all x1, blocking collectives, local(): lax.all_to_all(pair, ('row', 'z'), 0, 0).reshape(GROUP, SUMS, LANES)  16.1 us
    all_to_all x1, blocking collectives, local(): parts = lax.all_to_all(part, 'row', 0, 0)  11.8 us
    all_to_all x1, blocking collectives, local(): parts2 = lax.all_to_all(part2, 'row', 0, 0)  10.7 us
    all_to_all x1, blocking collectives, gather_own(): return lax.all_to_all(value, 'z', 0, 0)  10.5 us
    all_to_all x1, starting transfers between devices, gather_own(): return lax.all_to_all(value, 'z', 0, 0)  8.19 us
    all_to_all x1, starting transfers between devices, local(): lax.all_to_all(jnp.broadcast_to(jitter, (GROUP, COMPS, ATOMS)), 'row', 0, 0)  7.58 us
    ppermute x3, starting transfers between devices, core_swap(): return lax.ppermute(value, 'core', [(0, 1), (1, 0)])  7.41 us
    unnamed x14, local copies, waits for them, and re-layouts  5.12 us
  transfers between devices with their start and end apart: 5, of which 4 were waited for; matrix products, arithmetic and copies ran while one was open for 0% of the time, Pallas kernels for 6%

profile of v3, /device:TPU:1, one launch (start us, length us, event | category | flops | bytes accessed | tf_op | source)
XLA Modules:
  0.0 96.3 jit_solution(763792174787712633)
XLA Ops:
  0.6 1.3 %broadcast_in_dim.3 = f32[16,3,32]{2,1,0:T(4,128)} broadcast(f32[3,32]{1,0:T(4,128)} %jitter_hbm.1), dimensions={1,2} | broadcast | bytes 6528 | tf_op jit(solution)/shard_map/broadcast_in_dim | solution.py:343
  1.9 7.6 %all-to-all-start.1 = ((f32[16,3,32]{2,1,0:T(4,128)}), f32[16,3,32]{2,1,0:T(4,128)S(1)}, u32[]{:S(2)}, u32[]{:S(2)}) async-start(f32[16,3,32]{2,1,0:T(4,128)} %broadcast_in_dim.3), calls=%async_computation.1 | async-start | bytes 65536 | tf_op jit(solution)/shard_map/all_to_all | solution.py:343
  9.5 0.1 pad_add_fusion.ids
  9.6 0.8 copy-done.1
  10.4 0.7 copy-done.2
  11.1 0.7 copy-done.3
  11.8 1.9 %prepare.1 = (f32[8,32,128]{2,1,0:T(8,128)}, f32[32,128]{1,0:T(8,128)S(1)}) custom-call(s32[2]{0:T(128)S(1)} %pad_add_fusion.ids, s32[256]{0:T(256)S(1)} %copy-done.3, f32[3,32,36]{2,1,0:T(8,128)S(1)} %bitcast.12, f32[3,32]{1,0:T(4,128)S(1)} %copy-done.2), custom_call_target="tpu_custom_call" | custom-call | tf_op jit(solution)/shard_map/prepare/pallas_call | solution.py:344
  13.7 2.3 %all-to-all-done.1.jitters = f32[16,3,32]{2,1,0:T(4,128)S(1)} async-done(((f32[16,3,32]{2,1,0:T(4,128)}), f32[16,3,32]{2,1,0:T(4,128)S(1)}, u32[]{:S(2)}, u32[]{:S(2)}) %all-to-all-start.1) | async-done | bytes 6176 | tf_op jit(solution)/shard_map/all_to_all | solution.py:343
  16.0 8.2 %all-to-all-start = ((f32[8,32,128]{2,1,0:T(8,128)}), f32[8,32,128]{2,1,0:T(8,128)S(1)}, u32[]{:S(2)}, u32[]{:S(2)}) async-start(f32[8,32,128]{2,1,0:T(8,128)} %get-tuple-element.21), calls=%async_computation | async-start | bytes 262144 | tf_op jit(solution)/shard_map/all_to_all | solution.py:338
  24.2 0.9 copy-done
  25.1 0.7 copy-done.4
  25.8 0.7 copy-done.5
  26.5 0.7 copy-done.6
  27.1 1.7 %side.1 = (f32[40,128]{1,0:T(8,128)S(1)}, f32[16,512]{1,0:T(8,128)S(1)}, f32[3,512,128]{2,1,0:T(8,128)S(1)}) custom-call(s32[2]{0:T(128)S(1)} %pad_add_fusion.ids, s32[32]{0:T(128)S(1)} %copy-done.6, f32[4,12]{1,0:T(4,128)S(1)} %bitcast.13, s32[256,256]{1,0:T(8,128)S(1)} %copy-done, s32[256]{0:T(256)S(1)} %copy-done.4, f32[16,3,32]{2,1,0:T(4,128)S(1)} %all-to-all-done.1.jitters), custom_call_target="tpu_custom_call" | custom-call | tf_op jit(solution)/shard_map/side/pallas_call | solution.py:360
  28.9 3.3 %all-to-all-done.gathered = f32[8,32,128]{2,1,0:T(8,128)S(1)} async-done(((f32[8,32,128]{2,1,0:T(8,128)}), f32[8,32,128]{2,1,0:T(8,128)S(1)}, u32[]{:S(2)}, u32[]{:S(2)}) %all-to-all-start) | async-done | bytes 131104 | tf_op jit(solution)/shard_map/all_to_all | solution.py:338
  32.2 3.4 %collective-permute-start = (f32[8,32,128]{2,1,0:T(8,128)S(1)}, f32[8,32,128]{2,1,0:T(8,128)S(1)}, u32[]{:S(2)}, u32[]{:S(2)}) collective-permute-start(f32[8,32,128]{2,1,0:T(8,128)S(1)} %all-to-all-done.gathered), channel_id=1, source_target_pairs={{0,1},{1,0},{2,3},{3,2},{4,5},{5,4},{6,7},{7,6},{8,9},{9,8},{10,11... | collective-permute-start | bytes 393224 | tf_op jit(solution)/shard_map/ppermute | solution.py:334
  35.6 1.7 %first_own.1 = (f32[512,128]{1,0:T(8,128)S(1)}, bf16[512,1280]{1,0:T(8,128)(2,1)S(1)}, bf16[512,1280]{1,0:T(8,128)(2,1)S(1)}) custom-call(f32[16,512]{1,0:T(8,128)S(1)} %get-tuple-element.25.mask, f32[3,512,128]{2,1,0:T(8,128)S(1)} %get-tuple-element.26.column, f32[8,32,128]{2,1,0:T(8,128)S(1)} %all-to-all-done.gathered), custom_call_target="tpu_custom_call" | custom-call | tf_op jit(solution)/shard_map/first_own/pallas_call | solution.py:381
  37.3 0.0 collective-permute-done.gathered
  37.3 1.7 %first_other.1 = (f32[16,32,128]{2,1,0:T(8,128)S(1)}, bf16[512,1280]{1,0:T(8,128)(2,1)S(1)}, bf16[512,1280]{1,0:T(8,128)(2,1)S(1)}) custom-call(f32[16,512]{1,0:T(8,128)S(1)} %get-tuple-element.25.mask, f32[3,512,128]{2,1,0:T(8,128)S(1)} %get-tuple-element.26.column, f32[8,32,128]{2,1,0:T(8,128)S(1)} %collective-permute-done.gathered, ...), custom_call_target="tpu_custom_call" | custom-call | tf_op jit(solution)/shard_map/first_other/pallas_call | solution.py:390
  39.0 11.8 %all_to_all.30.parts = f32[16,32,128]{2,1,0:T(8,128)S(1)} all-to-all(f32[16,32,128]{2,1,0:T(8,128)S(1)} %get-tuple-element.29), channel_id=1, replica_groups=mesh['row'=16,'z'=8,'core'=2] {'row'}, dimensions={0} | all-to-all | bytes 524288 | tf_op jit(solution)/shard_map/all_to_all | solution.py:399
  50.9 0.2 shifted.1
  51.1 10.5 %all_to_all.31.gathered = f32[8,32,128]{2,1,0:T(8,128)S(1)} all-to-all(f32[8,32,128]{2,1,0:T(8,128)S(1)} %shifted.1), channel_id=1, replica_groups=mesh['row'=16,'z'=8,'core'=2] {'z'}, dimensions={0} | all-to-all | bytes 262144 | tf_op jit(solution)/shard_map/all_to_all | solution.py:338
  61.6 2.4 %collective-permute-start.1 = (f32[8,32,128]{2,1,0:T(8,128)S(1)}, f32[8,32,128]{2,1,0:T(8,128)S(1)}, u32[]{:S(2)}, u32[]{:S(2)}) collective-permute-start(f32[8,32,128]{2,1,0:T(8,128)S(1)} %all_to_all.31.gathered), channel_id=1, source_target_pairs={{0,1},{1,0},{2,3},{3,2},{4,5},{5,4},{6,7},{7,6},{8,9},{9,8},{10,11... | collective-permute-start | bytes 393224 | tf_op jit(solution)/shard_map/ppermute | solution.py:334
  64.0 0.9 second_own.1.total
  64.9 0.1 collective-permute-done.1.gathered
  65.0 0.9 second_other.1
  65.9 10.7 %all_to_all.32.parts = f32[16,32,128]{2,1,0:T(8,128)S(1)} all-to-all(f32[16,32,128]{2,1,0:T(8,128)S(1)} %second_other.1), channel_id=1, replica_groups=mesh['row'=16,'z'=8,'core'=2] {'row'}, dimensions={0} | all-to-all | bytes 524288 | tf_op jit(solution)/shard_map/all_to_all | solution.py:432
  76.6 0.4 step.1
  77.0 1.6 %collective-permute-start.2 = (f32[8,128]{1,0:T(8,128)S(1)}, f32[8,128]{1,0:T(8,128)S(1)}, u32[]{:S(2)}, u32[]{:S(2)}) collective-permute-start(f32[8,128]{1,0:T(8,128)S(1)} %get-tuple-element.36.sums), channel_id=1, source_target_pairs={{0,1},{1,0},{2,3},{3,2},{4,5},{5,4},{6,7},{7,6},{8,9},{9,8},{10,11... | collective-permute-start | bytes 12296 | tf_op jit(solution)/shard_map/ppermute | solution.py:334
  78.5 0.8 collective-permute-done.2.swapped
  79.4 16.1 %all_to_all.33 = f32[128,1,128]{2,1,0:T(1,128)S(1)} all-to-all(f32[128,1,128]{2,1,0:T(1,128)S(1)} %bitcast.11), channel_id=1, replica_groups=mesh['row'=16,'z'=8,'core'=2] {'row','z'}, dimensions={0} | all-to-all | bytes 131072 | tf_op jit(solution)/shard_map/all_to_all | solution.py:452
  95.5 0.8 finish.1
  (8 shorter events, 0.0 us)
Async XLA Ops:
  1.9 14.1 %all-to-all-start.1 = ((f32[16,3,32]{2,1,0:T(4,128)}), f32[16,3,32]{2,1,0:T(4,128)S(1)}, u32[]{:S(2)}, u32[]{:S(2)}) async-start(f32[16,3,32]{2,1,0:T(4,128)} %broadcast_in_dim.3), calls=%async_computation.1 | async-start | bytes 65536 | tf_op jit(solution)/shard_map/all_to_all | solution.py:343
  9.6 0.8 copy-start.1
  10.4 0.7 copy-start.2
  11.1 0.7 copy-start.3
  16.0 16.2 %all-to-all-start = ((f32[8,32,128]{2,1,0:T(8,128)}), f32[8,32,128]{2,1,0:T(8,128)S(1)}, u32[]{:S(2)}, u32[]{:S(2)}) async-start(f32[8,32,128]{2,1,0:T(8,128)} %get-tuple-element.21), calls=%async_computation | async-start | bytes 262144 | tf_op jit(solution)/shard_map/all_to_all | solution.py:338
  24.2 0.9 copy-start
  25.1 0.7 copy-start.4
  25.8 0.7 copy-start.5
  26.5 0.7 copy-start.6
  32.2 5.1 %collective-permute-start = (f32[8,32,128]{2,1,0:T(8,128)S(1)}, f32[8,32,128]{2,1,0:T(8,128)S(1)}, u32[]{:S(2)}, u32[]{:S(2)}) collective-permute-start(f32[8,32,128]{2,1,0:T(8,128)S(1)} %all-to-all-done.gathered), channel_id=1, source_target_pairs={{0,1},{1,0},{2,3},{3,2},{4,5},{5,4},{6,7},{7,6},{8,9},{9,8},{10,11... | collective-permute-start | bytes 393224 | tf_op jit(solution)/shard_map/ppermute | solution.py:334
  61.6 3.4 %collective-permute-start.1 = (f32[8,32,128]{2,1,0:T(8,128)S(1)}, f32[8,32,128]{2,1,0:T(8,128)S(1)}, u32[]{:S(2)}, u32[]{:S(2)}) collective-permute-start(f32[8,32,128]{2,1,0:T(8,128)S(1)} %all_to_all.31.gathered), channel_id=1, source_target_pairs={{0,1},{1,0},{2,3},{3,2},{4,5},{5,4},{6,7},{7,6},{8,9},{9,8},{10,11... | collective-permute-start | bytes 393224 | tf_op jit(solution)/shard_map/ppermute | solution.py:334
  77.0 2.4 %collective-permute-start.2 = (f32[8,128]{1,0:T(8,128)S(1)}, f32[8,128]{1,0:T(8,128)S(1)}, u32[]{:S(2)}, u32[]{:S(2)}) collective-permute-start(f32[8,128]{1,0:T(8,128)S(1)} %get-tuple-element.36.sums), channel_id=1, source_target_pairs={{0,1},{1,0},{2,3},{3,2},{4,5},{5,4},{6,7},{7,6},{8,9},{9,8},{10,11... | collective-permute-start | bytes 12296 | tf_op jit(solution)/shard_map/ppermute | solution.py:334

commit v4 on v3

--- a/solution.py
+++ b/solution.py
@@ -61,7 +61,7 @@
         copy.wait()
 
 
-def prepare_kernel(ids, cells_hbm, field_hbm, jitter_hbm, vec_out, own_out, cells, field, jitter, work, wide, sems):
+def prepare_kernel(ids, cells_hbm, field_hbm, jitter_hbm, vec_out, own_out, cells_out, cells, field, jitter, work, wide, sems):
     fetch(((cells_hbm, cells), (field_hbm, field), (jitter_hbm, jitter)), sems)
     cell = cells[ids[0] * GROUP + ids[1]]
     work[...] = jnp.zeros_like(work)
@@ -71,6 +71,7 @@
         wide[:, comp * RHS : (comp + 1) * RHS] = field[comp]
     turned = wide[...]
     own_out[...] = turned
+    cells_out[...] = cells_hbm[...]
     for slot in range(HALF):
         vec_out[slot] = turned
 
@@ -341,11 +342,15 @@
 def local(external_field, jitter, species, alpha_table, block_cell, tile_map):
     ids = jnp.stack([lax.axis_index("row"), lax.axis_index(("z", "core"))]).astype(jnp.int32)
     jitters = lax.all_to_all(jnp.broadcast_to(jitter, (GROUP, COMPS, ATOMS)), "row", 0, 0)
-    vec, vector = pl.pallas_call(
+    vec, vector, cells = pl.pallas_call(
         prepare_kernel,
-        out_shape=(shape(HALF, ATOMS, LANES), shape(ATOMS, LANES)),
-        in_specs=[SMEM, HBM, HBM, HBM],
-        out_specs=(VMEM, VMEM),
+        out_shape=(
+            shape(HALF, ATOMS, LANES),
+            shape(ATOMS, LANES),
+            shape(GROUP * GROUP, dtype=jnp.int32),
+        ),
+        in_specs=[SMEM, VMEM, HBM, HBM],
+        out_specs=(VMEM, VMEM, VMEM),
         scratch_shapes=[
             pltpu.SMEM((GROUP * GROUP,), jnp.int32),
             pltpu.VMEM((COMPS, ATOMS, RHS), F32),
@@ -360,7 +365,7 @@
     aux, mask, column = pl.pallas_call(
         side_kernel,
         out_shape=(shape(ATOMS + SUMS, LANES), shape(GROUP, WIDE), shape(COMPS, WIDE, LANES)),
-        in_specs=[SMEM, HBM, HBM, HBM, HBM, VMEM],
+        in_specs=[SMEM, HBM, HBM, HBM, VMEM, VMEM],
         out_specs=(VMEM, VMEM, VMEM),
         scratch_shapes=[
             pltpu.VMEM((ATOMS,), jnp.int32),
@@ -372,7 +377,7 @@
         ],
         compiler_params=PARAMS,
         name="side",
-    )(ids, species, alpha_table.T, tile_map, block_cell, jitters)
+    )(ids, species, alpha_table.T, tile_map, cells, jitters)
     own = gather_own(vec)
     own, aux, mask, column = lax.optimization_barrier((own, aux, mask, column))
     other = core_swap(own)

time: 96.9 us -> 96.5 us (level)
    unnamed x14 -> x12, local copies, waits for them, and re-layouts: 5.12 us -> 4.44 us
where the time goes in v4:
time: 96.5 us; the launch traced here: 95.9 us
  blocking collectives  48.8 us (51%)
  starting transfers between devices  23.2 us (24%)
  Pallas kernels  10.2 us (11%)
  waiting for transfers between devices  7.23 us (7%)
  local copies, waits for them, and re-layouts  5.74 us (6%)
    all_to_all x1, blocking collectives, local(): lax.all_to_all(pair, ('row', 'z'), 0, 0).reshape(GROUP, SUMS, LANES)  16.1 us
    all_to_all x1, blocking collectives, local(): parts = lax.all_to_all(part, 'row', 0, 0)  11.8 us
    all_to_all x1, blocking collectives, local(): parts2 = lax.all_to_all(part2, 'row', 0, 0)  10.7 us
    all_to_all x1, blocking collectives, gather_own(): return lax.all_to_all(value, 'z', 0, 0)  10.1 us
    all_to_all x1, starting transfers between devices, gather_own(): return lax.all_to_all(value, 'z', 0, 0)  8.19 us
    all_to_all x1, starting transfers between devices, local(): lax.all_to_all(jnp.broadcast_to(jitter, (GROUP, COMPS, ATOMS)), 'row', 0, 0)  7.58 us
    ppermute x3, starting transfers between devices, core_swap(): return lax.ppermute(value, 'core', [(0, 1), (1, 0)])  7.4 us
    unnamed x12, local copies, waits for them, and re-layouts  4.44 us
  transfers between devices with their start and end apart: 5, of which 4 were waited for; matrix products, arithmetic and copies ran while one was open for 0% of the time, Pallas kernels for 6%

profile of v4, /device:TPU:1, one launch (start us, length us, event | category | flops | bytes accessed | tf_op | source)
XLA Modules:
  0.0 95.9 jit_solution(891719298511444851)
XLA Ops:
  0.6 1.3 %broadcast_in_dim.3 = f32[16,3,32]{2,1,0:T(4,128)} broadcast(f32[3,32]{1,0:T(4,128)} %jitter_hbm.1), dimensions={1,2} | broadcast | bytes 6528 | tf_op jit(solution)/shard_map/broadcast_in_dim | solution.py:344
  1.9 7.6 %all-to-all-start.1 = ((f32[16,3,32]{2,1,0:T(4,128)}), f32[16,3,32]{2,1,0:T(4,128)S(1)}, u32[]{:S(2)}, u32[]{:S(2)}) async-start(f32[16,3,32]{2,1,0:T(4,128)} %broadcast_in_dim.3), calls=%async_computation.1 | async-start | bytes 65536 | tf_op jit(solution)/shard_map/all_to_all | solution.py:344
  9.5 0.1 pad_add_fusion.ids
  9.6 0.0 copy-start.1
  9.6 0.8 copy-done.1
  10.4 0.7 copy-done.2
  11.1 0.7 copy-done.4
  11.8 1.9 %prepare.1 = (f32[8,32,128]{2,1,0:T(8,128)}, f32[32,128]{1,0:T(8,128)S(1)}, s32[256]{0:T(256)S(1)}) custom-call(s32[2]{0:T(128)S(1)} %pad_add_fusion.ids, s32[256]{0:T(256)S(1)} %copy-done.4, f32[3,32,36]{2,1,0:T(8,128)S(1)} %bitcast.12, f32[3,32]{1,0:T(4,128)S(1)} %copy-done.2), custom_call_target="tpu_custom_call" | custom-call | tf_op jit(solution)/shard_map/prepare/pallas_call | solution.py:345
  13.7 2.3 %all-to-all-done.1.jitters = f32[16,3,32]{2,1,0:T(4,128)S(1)} async-done(((f32[16,3,32]{2,1,0:T(4,128)}), f32[16,3,32]{2,1,0:T(4,128)S(1)}, u32[]{:S(2)}, u32[]{:S(2)}) %all-to-all-start.1) | async-done | bytes 6176 | tf_op jit(solution)/shard_map/all_to_all | solution.py:344
  16.0 8.2 %all-to-all-start = ((f32[8,32,128]{2,1,0:T(8,128)}), f32[8,32,128]{2,1,0:T(8,128)S(1)}, u32[]{:S(2)}, u32[]{:S(2)}) async-start(f32[8,32,128]{2,1,0:T(8,128)} %get-tuple-element.22), calls=%async_computation | async-start | bytes 262144 | tf_op jit(solution)/shard_map/all_to_all | solution.py:339
  24.2 0.9 copy-done
  25.1 0.7 copy-done.3
  25.8 0.7 copy-done.5
  26.5 1.7 %side.1 = (f32[40,128]{1,0:T(8,128)S(1)}, f32[16,512]{1,0:T(8,128)S(1)}, f32[3,512,128]{2,1,0:T(8,128)S(1)}) custom-call(s32[2]{0:T(128)S(1)} %pad_add_fusion.ids, s32[32]{0:T(128)S(1)} %copy-done.5, f32[4,12]{1,0:T(4,128)S(1)} %bitcast.13, s32[256,256]{1,0:T(8,128)S(1)} %copy-done, s32[256]{0:T(256)S(1)} %get-tuple-element.23.cells_hbm, ...), custom_call_target="tpu_custom_call" | custom-call | tf_op jit(solution)/shard_map/side/pallas_call | solution.py:365
  28.2 4.0 %all-to-all-done.gathered = f32[8,32,128]{2,1,0:T(8,128)S(1)} async-done(((f32[8,32,128]{2,1,0:T(8,128)}), f32[8,32,128]{2,1,0:T(8,128)S(1)}, u32[]{:S(2)}, u32[]{:S(2)}) %all-to-all-start) | async-done | bytes 131104 | tf_op jit(solution)/shard_map/all_to_all | solution.py:339
  32.2 3.4 %collective-permute-start = (f32[8,32,128]{2,1,0:T(8,128)S(1)}, f32[8,32,128]{2,1,0:T(8,128)S(1)}, u32[]{:S(2)}, u32[]{:S(2)}) collective-permute-start(f32[8,32,128]{2,1,0:T(8,128)S(1)} %all-to-all-done.gathered), channel_id=1, source_target_pairs={{0,1},{1,0},{2,3},{3,2},{4,5},{5,4},{6,7},{7,6},{8,9},{9,8},{10,11... | collective-permute-start | bytes 393224 | tf_op jit(solution)/shard_map/ppermute | solution.py:335
  35.6 1.7 %first_own.1 = (f32[512,128]{1,0:T(8,128)S(1)}, bf16[512,1280]{1,0:T(8,128)(2,1)S(1)}, bf16[512,1280]{1,0:T(8,128)(2,1)S(1)}) custom-call(f32[16,512]{1,0:T(8,128)S(1)} %get-tuple-element.27.mask, f32[3,512,128]{2,1,0:T(8,128)S(1)} %get-tuple-element.28.column, f32[8,32,128]{2,1,0:T(8,128)S(1)} %all-to-all-done.gathered), custom_call_target="tpu_custom_call" | custom-call | tf_op jit(solution)/shard_map/first_own/pallas_call | solution.py:386
  37.3 0.0 collective-permute-done.gathered
  37.3 1.7 %first_other.1 = (f32[16,32,128]{2,1,0:T(8,128)S(1)}, bf16[512,1280]{1,0:T(8,128)(2,1)S(1)}, bf16[512,1280]{1,0:T(8,128)(2,1)S(1)}) custom-call(f32[16,512]{1,0:T(8,128)S(1)} %get-tuple-element.27.mask, f32[3,512,128]{2,1,0:T(8,128)S(1)} %get-tuple-element.28.column, f32[8,32,128]{2,1,0:T(8,128)S(1)} %collective-permute-done.gathered, ...), custom_call_target="tpu_custom_call" | custom-call | tf_op jit(solution)/shard_map/first_other/pallas_call | solution.py:395
  39.0 11.8 %all_to_all.30.parts = f32[16,32,128]{2,1,0:T(8,128)S(1)} all-to-all(f32[16,32,128]{2,1,0:T(8,128)S(1)} %get-tuple-element.31), channel_id=1, replica_groups=mesh['row'=16,'z'=8,'core'=2] {'row'}, dimensions={0} | all-to-all | bytes 524288 | tf_op jit(solution)/shard_map/all_to_all | solution.py:404
  50.9 0.2 shifted.1
  51.1 10.1 %all_to_all.31.gathered = f32[8,32,128]{2,1,0:T(8,128)S(1)} all-to-all(f32[8,32,128]{2,1,0:T(8,128)S(1)} %shifted.1), channel_id=1, replica_groups=mesh['row'=16,'z'=8,'core'=2] {'z'}, dimensions={0} | all-to-all | bytes 262144 | tf_op jit(solution)/shard_map/all_to_all | solution.py:339
  61.2 2.4 %collective-permute-start.1 = (f32[8,32,128]{2,1,0:T(8,128)S(1)}, f32[8,32,128]{2,1,0:T(8,128)S(1)}, u32[]{:S(2)}, u32[]{:S(2)}) collective-permute-start(f32[8,32,128]{2,1,0:T(8,128)S(1)} %all_to_all.31.gathered), channel_id=1, source_target_pairs={{0,1},{1,0},{2,3},{3,2},{4,5},{5,4},{6,7},{7,6},{8,9},{9,8},{10,11... | collective-permute-start | bytes 393224 | tf_op jit(solution)/shard_map/ppermute | solution.py:335
  63.7 0.9 second_own.1.total
  64.6 0.1 collective-permute-done.1.gathered
  64.7 0.9 second_other.1
  65.5 10.7 %all_to_all.32.parts = f32[16,32,128]{2,1,0:T(8,128)S(1)} all-to-all(f32[16,32,128]{2,1,0:T(8,128)S(1)} %second_other.1), channel_id=1, replica_groups=mesh['row'=16,'z'=8,'core'=2] {'row'}, dimensions={0} | all-to-all | bytes 524288 | tf_op jit(solution)/shard_map/all_to_all | solution.py:437
  76.3 0.4 step.1
  76.6 1.6 %collective-permute-start.2 = (f32[8,128]{1,0:T(8,128)S(1)}, f32[8,128]{1,0:T(8,128)S(1)}, u32[]{:S(2)}, u32[]{:S(2)}) collective-permute-start(f32[8,128]{1,0:T(8,128)S(1)} %get-tuple-element.38.sums), channel_id=1, source_target_pairs={{0,1},{1,0},{2,3},{3,2},{4,5},{5,4},{6,7},{7,6},{8,9},{9,8},{10,11... | collective-permute-start | bytes 12296 | tf_op jit(solution)/shard_map/ppermute | solution.py:335
  78.2 0.8 collective-permute-done.2.swapped
  79.0 16.1 %all_to_all.33 = f32[128,1,128]{2,1,0:T(1,128)S(1)} all-to-all(f32[128,1,128]{2,1,0:T(1,128)S(1)} %bitcast.11), channel_id=1, replica_groups=mesh['row'=16,'z'=8,'core'=2] {'row','z'}, dimensions={0} | all-to-all | bytes 131072 | tf_op jit(solution)/shard_map/all_to_all | solution.py:457
  95.1 0.8 finish.1
  (6 shorter events, 0.0 us)
Async XLA Ops:
  1.9 14.1 %all-to-all-start.1 = ((f32[16,3,32]{2,1,0:T(4,128)}), f32[16,3,32]{2,1,0:T(4,128)S(1)}, u32[]{:S(2)}, u32[]{:S(2)}) async-start(f32[16,3,32]{2,1,0:T(4,128)} %broadcast_in_dim.3), calls=%async_computation.1 | async-start | bytes 65536 | tf_op jit(solution)/shard_map/all_to_all | solution.py:344
  9.6 0.8 copy-start.1
  10.4 0.7 copy-start.2
  11.1 0.7 copy-start.4
  16.0 16.2 %all-to-all-start = ((f32[8,32,128]{2,1,0:T(8,128)}), f32[8,32,128]{2,1,0:T(8,128)S(1)}, u32[]{:S(2)}, u32[]{:S(2)}) async-start(f32[8,32,128]{2,1,0:T(8,128)} %get-tuple-element.22), calls=%async_computation | async-start | bytes 262144 | tf_op jit(solution)/shard_map/all_to_all | solution.py:339
  24.2 0.9 copy-start
  25.1 0.7 copy-start.3
  25.8 0.7 copy-start.5
  32.2 5.1 %collective-permute-start = (f32[8,32,128]{2,1,0:T(8,128)S(1)}, f32[8,32,128]{2,1,0:T(8,128)S(1)}, u32[]{:S(2)}, u32[]{:S(2)}) collective-permute-start(f32[8,32,128]{2,1,0:T(8,128)S(1)} %all-to-all-done.gathered), channel_id=1, source_target_pairs={{0,1},{1,0},{2,3},{3,2},{4,5},{5,4},{6,7},{7,6},{8,9},{9,8},{10,11... | collective-permute-start | bytes 393224 | tf_op jit(solution)/shard_map/ppermute | solution.py:335
  61.2 3.4 %collective-permute-start.1 = (f32[8,32,128]{2,1,0:T(8,128)S(1)}, f32[8,32,128]{2,1,0:T(8,128)S(1)}, u32[]{:S(2)}, u32[]{:S(2)}) collective-permute-start(f32[8,32,128]{2,1,0:T(8,128)S(1)} %all_to_all.31.gathered), channel_id=1, source_target_pairs={{0,1},{1,0},{2,3},{3,2},{4,5},{5,4},{6,7},{7,6},{8,9},{9,8},{10,11... | collective-permute-start | bytes 393224 | tf_op jit(solution)/shard_map/ppermute | solution.py:335
  76.6 2.4 %collective-permute-start.2 = (f32[8,128]{1,0:T(8,128)S(1)}, f32[8,128]{1,0:T(8,128)S(1)}, u32[]{:S(2)}, u32[]{:S(2)}) collective-permute-start(f32[8,128]{1,0:T(8,128)S(1)} %get-tuple-element.38.sums), channel_id=1, source_target_pairs={{0,1},{1,0},{2,3},{3,2},{4,5},{5,4},{6,7},{7,6},{8,9},{9,8},{10,11... | collective-permute-start | bytes 12296 | tf_op jit(solution)/shard_map/ppermute | solution.py:335

commit v5 on v3

--- a/solution.py
+++ b/solution.py
@@ -14,6 +14,7 @@
 SUMS = 8
 SITE = 120
 SUM_ROW = 104
+CELL_ROW = 8
 WIDE = GROUP * ATOMS
 NARROW = HALF * ATOMS
 CHUNK = 256
@@ -24,7 +25,6 @@
 
 VMEM = pl.BlockSpec(memory_space=pltpu.VMEM)
 SMEM = pl.BlockSpec(memory_space=pltpu.SMEM)
-HBM = pl.BlockSpec(memory_space=pltpu.HBM)
 SQUARE = pltpu.VMEM((LANES, LANES), F32)
 PARAMS = pltpu.CompilerParams(vmem_limit_bytes=16 * 1024 * 1024)
 
@@ -53,19 +53,14 @@
     return jnp.where(first, of_first, jnp.where(second, of_second, jnp.where(third, of_third, 1.0)))
 
 
-def fetch(pairs, sems):
-    copies = [pltpu.make_async_copy(source, target, sems.at[i]) for i, (source, target) in enumerate(pairs)]
-    for copy in copies:
-        copy.start()
-    for copy in copies:
-        copy.wait()
-
-
-def prepare_kernel(ids, cells_hbm, field_hbm, jitter_hbm, vec_out, own_out, cells, field, jitter, work, wide, sems):
-    fetch(((cells_hbm, cells), (field_hbm, field), (jitter_hbm, jitter)), sems)
-    cell = cells[ids[0] * GROUP + ids[1]]
+def prepare_kernel(ids, pack, field, vec_out, own_out, work, wide):
+    own = ids[0] * GROUP + ids[1]
+    index = lax.broadcasted_iota(jnp.int32, (SUMS, LANES), 0) * LANES + lane_ids(SUMS)
+    found = jnp.where(index == own, pack[CELL_ROW : CELL_ROW + SUMS, :], 0.0)
+    cell = jnp.sum(jnp.sum(found, axis=0, keepdims=True), axis=1, keepdims=True).astype(jnp.int32)
+    comp = lax.broadcasted_iota(jnp.int32, (SUMS, LANES), 0)
     work[...] = jnp.zeros_like(work)
-    work[SITE : SITE + COMPS, 0:ATOMS] = block_sites(cell, jitter[...])
+    work[SITE : SITE + SUMS, :] = lattice(comp, lane_ids(SUMS), cell) + pack[0:SUMS, :]
     wide[...] = work[...].T[0:ATOMS, :]
     for comp in range(COMPS):
         wide[:, comp * RHS : (comp + 1) * RHS] = field[comp]
@@ -75,21 +70,14 @@
         vec_out[slot] = turned
 
 
-def block_sites(cell, jitter):
-    comp = lax.broadcasted_iota(jnp.int32, (COMPS, ATOMS), 0)
-    atom = lax.broadcasted_iota(jnp.int32, (COMPS, ATOMS), 1)
-    inner = jnp.where(comp == 0, atom // 8, jnp.where(comp == 1, (atom // 2) % 4, atom % 2))
-    corner = jnp.where(comp == 0, cell // 32 * 4, jnp.where(comp == 1, (cell // 4) % 8 * 4, cell % 4 * 2))
-    return (corner + inner).astype(F32) * SPACING + jitter
-
-
-def side_kernel(
-    ids, species_hbm, alpha_hbm, tile_map_hbm, cells_hbm, jitters,
-    aux_out, mask_out, column, species, alpha, tile_map, cells, work, sems
-):
-    fetch(
-        ((species_hbm, species), (alpha_hbm, alpha), (tile_map_hbm, tile_map), (cells_hbm, cells)), sems
-    )
+def lattice(comp, atom, cell):
+    inner = jnp.where(comp == 0, atom >> 3, jnp.where(comp == 1, (atom >> 1) & 3, atom & 1))
+    corner = jnp.where(comp == 0, (cell >> 5) * 4, jnp.where(comp == 1, ((cell >> 2) & 7) * 4, (cell & 3) * 2))
+    return (corner + inner).astype(F32) * SPACING
+
+
+def side_kernel(ids, pack, species, tile_map, jitters, aux_out, mask_out, column, work):
+    alpha = species[4:SUMS, :]
     lane = lax.broadcasted_iota(jnp.int32, (4, LANES), 1)
     rhs_lane = jnp.where(lane >= 2 * RHS, lane - 2 * RHS, jnp.where(lane >= RHS, lane - RHS, lane))
     table = jnp.ones((4, LANES), F32)
@@ -101,8 +89,7 @@
         )
     inverse = 1.0 / table
     shift = 0.25 * ((inverse[0:1] + inverse[1:2]) + (inverse[2:3] + inverse[3:4]))
-    work[...] = jnp.zeros_like(work)
-    work[0:1, 0:ATOMS] = species[...].astype(F32).reshape(1, ATOMS)
+    work[0:SUMS, :] = species[...]
     kinds = jnp.broadcast_to(work[...].T[0:ATOMS, 0:1], (ATOMS, LANES))
     diag = jnp.zeros((ATOMS, LANES), F32)
     for kind in range(4):
@@ -122,11 +109,15 @@
     spread = jnp.where(place == wanted, 1.0, 0.0).astype(BF16)
     mask_out[...] = 0.5 * jnp.dot(lines, spread, preferred_element_type=F32)
 
+    cells = jnp.concatenate([pack[CELL_ROW : CELL_ROW + 1, :], pack[CELL_ROW + 1 : CELL_ROW + 2, :]], axis=1)
+    place = lax.broadcasted_iota(jnp.int32, (LANES, blocks), 1)
+    wanted = (lax.broadcasted_iota(jnp.int32, (LANES, blocks), 0) >> 3) * GROUP + ids[1]
+    cell = jnp.sum(jnp.where(place == wanted, cells, 0.0), axis=1, keepdims=True).astype(jnp.int32)
+    comp = lax.broadcasted_iota(jnp.int32, (LANES, LANES), 0) & 7
     work[...] = jnp.zeros_like(work)
     for slot in range(GROUP):
-        cell = cells[slot * GROUP + ids[1]]
-        work[slot * SUMS : slot * SUMS + COMPS, 0:ATOMS] = block_sites(cell, jitters[slot])
-    down = work[...].T[0:ATOMS, :]
+        work[slot * SUMS : slot * SUMS + COMPS, 0:ATOMS] = jitters[slot]
+    down = (lattice(comp, lane_ids(LANES), cell) + work[...]).T[0:ATOMS, :]
     for slot in range(GROUP):
         rows = slice(slot * ATOMS, (slot + 1) * ATOMS)
         for comp in range(COMPS):
@@ -341,38 +332,36 @@
 def local(external_field, jitter, species, alpha_table, block_cell, tile_map):
     ids = jnp.stack([lax.axis_index("row"), lax.axis_index(("z", "core"))]).astype(jnp.int32)
     jitters = lax.all_to_all(jnp.broadcast_to(jitter, (GROUP, COMPS, ATOMS)), "row", 0, 0)
+    pack = jnp.concatenate(
+        [
+            jnp.pad(jitter, ((0, CELL_ROW - COMPS), (0, LANES - ATOMS))),
+            jnp.pad(block_cell.astype(F32).reshape(2, LANES), ((0, 6), (0, 0))),
+        ]
+    )
+    kinds = jnp.concatenate(
+        [
+            jnp.pad(species.astype(F32)[None], ((0, 3), (0, LANES - ATOMS))),
+            jnp.pad(alpha_table.T, ((0, 0), (0, LANES - 12))),
+        ]
+    )
     vec, vector = pl.pallas_call(
         prepare_kernel,
         out_shape=(shape(HALF, ATOMS, LANES), shape(ATOMS, LANES)),
-        in_specs=[SMEM, HBM, HBM, HBM],
+        in_specs=[SMEM, VMEM, VMEM],
         out_specs=(VMEM, VMEM),
-        scratch_shapes=[
-            pltpu.SMEM((GROUP * GROUP,), jnp.int32),
-            pltpu.VMEM((COMPS, ATOMS, RHS), F32),
-            pltpu.VMEM((COMPS, ATOMS), F32),
-            SQUARE,
-            pltpu.VMEM((ATOMS, LANES), F32),
-            pltpu.SemaphoreType.DMA((3,)),
-        ],
+        scratch_shapes=[SQUARE, pltpu.VMEM((ATOMS, LANES), F32)],
         compiler_params=PARAMS,
         name="prepare",
-    )(ids, block_cell, external_field.transpose(0, 2, 1), jitter)
+    )(ids, pack, external_field.transpose(0, 2, 1))
     aux, mask, column = pl.pallas_call(
         side_kernel,
         out_shape=(shape(ATOMS + SUMS, LANES), shape(GROUP, WIDE), shape(COMPS, WIDE, LANES)),
-        in_specs=[SMEM, HBM, HBM, HBM, HBM, VMEM],
+        in_specs=[SMEM, VMEM, VMEM, VMEM, VMEM],
         out_specs=(VMEM, VMEM, VMEM),
-        scratch_shapes=[
-            pltpu.VMEM((ATOMS,), jnp.int32),
-            pltpu.VMEM((4, 12), F32),
-            pltpu.VMEM((GROUP * GROUP, GROUP * GROUP), jnp.int32),
-            pltpu.SMEM((GROUP * GROUP,), jnp.int32),
-            SQUARE,
-            pltpu.SemaphoreType.DMA((4,)),
-        ],
+        scratch_shapes=[SQUARE],
         compiler_params=PARAMS,
         name="side",
-    )(ids, species, alpha_table.T, tile_map, block_cell, jitters)
+    )(ids, pack, kinds, tile_map, jitters)
     own = gather_own(vec)
     own, aux, mask, column = lax.optimization_barrier((own, aux, mask, column))
     other = core_swap(own)

time: 96.9 us -> 96 us (level)
  local copies, waits for them, and re-layouts: 6.42 us -> 3.05 us
  other arithmetic: 0.08 us -> 2.79 us
  waiting for transfers between devices: 6.57 us -> 8.41 us
  Pallas kernels: 10.1 us -> 8.99 us
    unnamed x14 -> x4, local copies, waits for them, and re-layouts: 5.12 us -> 1.75 us
    concatenate x0 -> x2, other arithmetic: none -> 1.38 us  [the longest x1 0.69 us: local(): jnp.concatenate([jnp.pad(species.astype(F32)[None], ((0, 3), (0, LANES -...]
    all_to_all x1, waiting for transfers between devices: 3.31 us -> 4.6 us  [gather_own(): return lax.all_to_all(value, 'z', 0, 0)]
  transfers between devices with their start and end apart: 5 -> 5, of which waited for: 4 -> 4; matrix products, arithmetic and copies ran while one was open for 0% -> 3% of each run, Pallas kernels for 6% -> 5%
where the time goes in v5:
time: 96 us; the launch traced here: 95.4 us
  blocking collectives  48.3 us (50%)
  starting transfers between devices  23.2 us (24%)
  Pallas kernels  8.99 us (9%)
  waiting for transfers between devices  8.41 us (9%)
  local copies, waits for them, and re-layouts  3.05 us (3%)
  other arithmetic  2.79 us (3%)
    all_to_all x1, blocking collectives, local(): lax.all_to_all(pair, ('row', 'z'), 0, 0).reshape(GROUP, SUMS, LANES)  16.1 us
    all_to_all x1, blocking collectives, local(): parts = lax.all_to_all(part, 'row', 0, 0)  11.3 us
    all_to_all x1, blocking collectives, local(): parts2 = lax.all_to_all(part2, 'row', 0, 0)  10.8 us
    all_to_all x1, blocking collectives, gather_own(): return lax.all_to_all(value, 'z', 0, 0)  10.1 us
    all_to_all x1, starting transfers between devices, gather_own(): return lax.all_to_all(value, 'z', 0, 0)  8.19 us
    all_to_all x1, starting transfers between devices, local(): lax.all_to_all(jnp.broadcast_to(jitter, (GROUP, COMPS, ATOMS)), 'row', 0, 0)  7.58 us
    ppermute x3, starting transfers between devices, core_swap(): return lax.ppermute(value, 'core', [(0, 1), (1, 0)])  7.4 us
    all_to_all x1, waiting for transfers between devices, gather_own(): return lax.all_to_all(value, 'z', 0, 0)  4.6 us
  transfers between devices with their start and end apart: 5, of which 4 were waited for; matrix products, arithmetic and copies ran while one was open for 3% of the time, Pallas kernels for 5%

profile of v5, /device:TPU:1, one launch (start us, length us, event | category | flops | bytes accessed | tf_op | source)
XLA Modules:
  0.0 95.4 jit_solution(11549390140606469823)
XLA Ops:
  0.6 1.3 %broadcast_in_dim.7 = f32[16,3,32]{2,1,0:T(4,128)} broadcast(f32[3,32]{1,0:T(4,128)} %param.7), dimensions={1,2} | broadcast | bytes 6528 | tf_op jit(solution)/shard_map/broadcast_in_dim | solution.py:334
  1.9 7.6 %all-to-all-start.1 = ((f32[16,3,32]{2,1,0:T(4,128)}), f32[16,3,32]{2,1,0:T(4,128)S(1)}, u32[]{:S(2)}, u32[]{:S(2)}) async-start(f32[16,3,32]{2,1,0:T(4,128)} %broadcast_in_dim.7), calls=%async_computation.1 | async-start | bytes 65536 | tf_op jit(solution)/shard_map/all_to_all | solution.py:334
  9.5 0.7 convert_bitcast_fusion
  10.2 0.7 select_maximum_fusion.pack
  10.9 0.1 pad_add_fusion.ids
  11.0 0.0 copy-start.1
  11.0 0.8 copy-done.1
  11.8 1.3 %prepare.1 = (f32[8,32,128]{2,1,0:T(8,128)}, f32[32,128]{1,0:T(8,128)S(1)}) custom-call(s32[2]{0:T(128)S(1)} %pad_add_fusion.ids, f32[16,128]{1,0:T(8,128)S(1)} %select_maximum_fusion.pack, f32[3,32,36]{2,1,0:T(8,128)S(1)} %bitcast.16), custom_call_target="tpu_custom_call" | custom-call | tf_op jit(solution)/shard_map/prepare/pallas_call | solution.py:347
  13.1 2.9 %all-to-all-done.1.jitters = f32[16,3,32]{2,1,0:T(4,128)S(1)} async-done(((f32[16,3,32]{2,1,0:T(4,128)}), f32[16,3,32]{2,1,0:T(4,128)S(1)}, u32[]{:S(2)}, u32[]{:S(2)}) %all-to-all-start.1) | async-done | bytes 6176 | tf_op jit(solution)/shard_map/all_to_all | solution.py:334
  16.0 8.2 %all-to-all-start = ((f32[8,32,128]{2,1,0:T(8,128)}), f32[8,32,128]{2,1,0:T(8,128)S(1)}, u32[]{:S(2)}, u32[]{:S(2)}) async-start(f32[8,32,128]{2,1,0:T(8,128)} %get-tuple-element.21), calls=%async_computation | async-start | bytes 262144 | tf_op jit(solution)/shard_map/all_to_all | solution.py:329
  24.2 0.7 convert_bitcast_fusion.1
  24.8 0.7 select_maximum_fusion.1.species
  25.5 0.9 copy-done
  26.5 1.1 %side.1 = (f32[40,128]{1,0:T(8,128)S(1)}, f32[16,512]{1,0:T(8,128)S(1)}, f32[3,512,128]{2,1,0:T(8,128)S(1)}) custom-call(s32[2]{0:T(128)S(1)} %pad_add_fusion.ids, f32[16,128]{1,0:T(8,128)S(1)} %select_maximum_fusion.pack, f32[8,128]{1,0:T(8,128)S(1)} %select_maximum_fusion.1.species, s32[256,256]{1,0:T(8,128)S(1)} %copy-done, ...), custom_call_target="tpu_custom_call" | custom-call | tf_op jit(solution)/shard_map/side/pallas_call | solution.py:356
  27.6 4.6 %all-to-all-done.gathered = f32[8,32,128]{2,1,0:T(8,128)S(1)} async-done(((f32[8,32,128]{2,1,0:T(8,128)}), f32[8,32,128]{2,1,0:T(8,128)S(1)}, u32[]{:S(2)}, u32[]{:S(2)}) %all-to-all-start) | async-done | bytes 131104 | tf_op jit(solution)/shard_map/all_to_all | solution.py:329
  32.2 3.4 %collective-permute-start = (f32[8,32,128]{2,1,0:T(8,128)S(1)}, f32[8,32,128]{2,1,0:T(8,128)S(1)}, u32[]{:S(2)}, u32[]{:S(2)}) collective-permute-start(f32[8,32,128]{2,1,0:T(8,128)S(1)} %all-to-all-done.gathered), channel_id=1, source_target_pairs={{0,1},{1,0},{2,3},{3,2},{4,5},{5,4},{6,7},{7,6},{8,9},{9,8},{10,11... | collective-permute-start | bytes 393224 | tf_op jit(solution)/shard_map/ppermute | solution.py:325
  35.6 1.7 %first_own.1 = (f32[512,128]{1,0:T(8,128)S(1)}, bf16[512,1280]{1,0:T(8,128)(2,1)S(1)}, bf16[512,1280]{1,0:T(8,128)(2,1)S(1)}) custom-call(f32[16,512]{1,0:T(8,128)S(1)} %get-tuple-element.25.mask, f32[3,512,128]{2,1,0:T(8,128)S(1)} %get-tuple-element.26.column, f32[8,32,128]{2,1,0:T(8,128)S(1)} %all-to-all-done.gathered), custom_call_target="tpu_custom_call" | custom-call | tf_op jit(solution)/shard_map/first_own/pallas_call | solution.py:370
  37.3 0.0 collective-permute-done.gathered
  37.3 1.7 %first_other.1 = (f32[16,32,128]{2,1,0:T(8,128)S(1)}, bf16[512,1280]{1,0:T(8,128)(2,1)S(1)}, bf16[512,1280]{1,0:T(8,128)(2,1)S(1)}) custom-call(f32[16,512]{1,0:T(8,128)S(1)} %get-tuple-element.25.mask, f32[3,512,128]{2,1,0:T(8,128)S(1)} %get-tuple-element.26.column, f32[8,32,128]{2,1,0:T(8,128)S(1)} %collective-permute-done.gathered, ...), custom_call_target="tpu_custom_call" | custom-call | tf_op jit(solution)/shard_map/first_other/pallas_call | solution.py:379
  39.0 11.3 %all_to_all.30.parts = f32[16,32,128]{2,1,0:T(8,128)S(1)} all-to-all(f32[16,32,128]{2,1,0:T(8,128)S(1)} %get-tuple-element.29), channel_id=1, replica_groups=mesh['row'=16,'z'=8,'core'=2] {'row'}, dimensions={0} | all-to-all | bytes 524288 | tf_op jit(solution)/shard_map/all_to_all | solution.py:388
  50.4 0.2 shifted.1
  50.6 10.1 %all_to_all.31.gathered = f32[8,32,128]{2,1,0:T(8,128)S(1)} all-to-all(f32[8,32,128]{2,1,0:T(8,128)S(1)} %shifted.1), channel_id=1, replica_groups=mesh['row'=16,'z'=8,'core'=2] {'z'}, dimensions={0} | all-to-all | bytes 262144 | tf_op jit(solution)/shard_map/all_to_all | solution.py:329
  60.7 2.4 %collective-permute-start.1 = (f32[8,32,128]{2,1,0:T(8,128)S(1)}, f32[8,32,128]{2,1,0:T(8,128)S(1)}, u32[]{:S(2)}, u32[]{:S(2)}) collective-permute-start(f32[8,32,128]{2,1,0:T(8,128)S(1)} %all_to_all.31.gathered), channel_id=1, source_target_pairs={{0,1},{1,0},{2,3},{3,2},{4,5},{5,4},{6,7},{7,6},{8,9},{9,8},{10,11... | collective-permute-start | bytes 393224 | tf_op jit(solution)/shard_map/ppermute | solution.py:325
  63.2 0.9 second_own.1.total
  64.0 0.1 collective-permute-done.1.gathered
  64.1 0.9 second_other.1
  65.0 10.8 %all_to_all.32.parts = f32[16,32,128]{2,1,0:T(8,128)S(1)} all-to-all(f32[16,32,128]{2,1,0:T(8,128)S(1)} %second_other.1), channel_id=1, replica_groups=mesh['row'=16,'z'=8,'core'=2] {'row'}, dimensions={0} | all-to-all | bytes 524288 | tf_op jit(solution)/shard_map/all_to_all | solution.py:421
  75.8 0.4 step.1
  76.1 1.6 %collective-permute-start.2 = (f32[8,128]{1,0:T(8,128)S(1)}, f32[8,128]{1,0:T(8,128)S(1)}, u32[]{:S(2)}, u32[]{:S(2)}) collective-permute-start(f32[8,128]{1,0:T(8,128)S(1)} %get-tuple-element.36.sums), channel_id=1, source_target_pairs={{0,1},{1,0},{2,3},{3,2},{4,5},{5,4},{6,7},{7,6},{8,9},{9,8},{10,11... | collective-permute-start | bytes 12296 | tf_op jit(solution)/shard_map/ppermute | solution.py:325
  77.7 0.8 collective-permute-done.2.swapped
  78.5 16.1 %all_to_all.33 = f32[128,1,128]{2,1,0:T(1,128)S(1)} all-to-all(f32[128,1,128]{2,1,0:T(1,128)S(1)} %bitcast.15), channel_id=1, replica_groups=mesh['row'=16,'z'=8,'core'=2] {'row','z'}, dimensions={0} | all-to-all | bytes 131072 | tf_op jit(solution)/shard_map/all_to_all | solution.py:441
  94.6 0.8 finish.1
  (2 shorter events, 0.0 us)
Async XLA Ops:
  1.9 14.1 %all-to-all-start.1 = ((f32[16,3,32]{2,1,0:T(4,128)}), f32[16,3,32]{2,1,0:T(4,128)S(1)}, u32[]{:S(2)}, u32[]{:S(2)}) async-start(f32[16,3,32]{2,1,0:T(4,128)} %broadcast_in_dim.7), calls=%async_computation.1 | async-start | bytes 65536 | tf_op jit(solution)/shard_map/all_to_all | solution.py:334
  11.0 0.8 copy-start.1
  16.0 16.2 %all-to-all-start = ((f32[8,32,128]{2,1,0:T(8,128)}), f32[8,32,128]{2,1,0:T(8,128)S(1)}, u32[]{:S(2)}, u32[]{:S(2)}) async-start(f32[8,32,128]{2,1,0:T(8,128)} %get-tuple-element.21), calls=%async_computation | async-start | bytes 262144 | tf_op jit(solution)/shard_map/all_to_all | solution.py:329
  25.5 0.9 copy-start
  32.2 5.1 %collective-permute-start = (f32[8,32,128]{2,1,0:T(8,128)S(1)}, f32[8,32,128]{2,1,0:T(8,128)S(1)}, u32[]{:S(2)}, u32[]{:S(2)}) collective-permute-start(f32[8,32,128]{2,1,0:T(8,128)S(1)} %all-to-all-done.gathered), channel_id=1, source_target_pairs={{0,1},{1,0},{2,3},{3,2},{4,5},{5,4},{6,7},{7,6},{8,9},{9,8},{10,11... | collective-permute-start | bytes 393224 | tf_op jit(solution)/shard_map/ppermute | solution.py:325
  60.7 3.4 %collective-permute-start.1 = (f32[8,32,128]{2,1,0:T(8,128)S(1)}, f32[8,32,128]{2,1,0:T(8,128)S(1)}, u32[]{:S(2)}, u32[]{:S(2)}) collective-permute-start(f32[8,32,128]{2,1,0:T(8,128)S(1)} %all_to_all.31.gathered), channel_id=1, source_target_pairs={{0,1},{1,0},{2,3},{3,2},{4,5},{5,4},{6,7},{7,6},{8,9},{9,8},{10,11... | collective-permute-start | bytes 393224 | tf_op jit(solution)/shard_map/ppermute | solution.py:325
  76.1 2.4 %collective-permute-start.2 = (f32[8,128]{1,0:T(8,128)S(1)}, f32[8,128]{1,0:T(8,128)S(1)}, u32[]{:S(2)}, u32[]{:S(2)}) collective-permute-start(f32[8,128]{1,0:T(8,128)S(1)} %get-tuple-element.36.sums), channel_id=1, source_target_pairs={{0,1},{1,0},{2,3},{3,2},{4,5},{5,4},{6,7},{7,6},{8,9},{9,8},{10,11... | collective-permute-start | bytes 12296 | tf_op jit(solution)/shard_map/ppermute | solution.py:325

commit v6 on v5

--- a/solution.py
+++ b/solution.py
@@ -14,7 +14,7 @@
 SUMS = 8
 SITE = 120
 SUM_ROW = 104
-CELL_ROW = 8
+CELL_ROW = 16
 WIDE = GROUP * ATOMS
 NARROW = HALF * ATOMS
 CHUNK = 256
@@ -53,21 +53,53 @@
     return jnp.where(first, of_first, jnp.where(second, of_second, jnp.where(third, of_third, 1.0)))
 
 
-def prepare_kernel(ids, pack, field, vec_out, own_out, work, wide):
-    own = ids[0] * GROUP + ids[1]
+def block_rows(own, pack, jitter_row, field, work, wide):
     index = lax.broadcasted_iota(jnp.int32, (SUMS, LANES), 0) * LANES + lane_ids(SUMS)
     found = jnp.where(index == own, pack[CELL_ROW : CELL_ROW + SUMS, :], 0.0)
     cell = jnp.sum(jnp.sum(found, axis=0, keepdims=True), axis=1, keepdims=True).astype(jnp.int32)
     comp = lax.broadcasted_iota(jnp.int32, (SUMS, LANES), 0)
-    work[...] = jnp.zeros_like(work)
-    work[SITE : SITE + SUMS, :] = lattice(comp, lane_ids(SUMS), cell) + pack[0:SUMS, :]
+    work[SITE : SITE + SUMS, :] = lattice(comp, lane_ids(SUMS), cell) + pack[jitter_row : jitter_row + SUMS, :]
     wide[...] = work[...].T[0:ATOMS, :]
     for comp in range(COMPS):
         wide[:, comp * RHS : (comp + 1) * RHS] = field[comp]
-    turned = wide[...]
-    own_out[...] = turned
-    for slot in range(HALF):
-        vec_out[slot] = turned
+    return wide[...]
+
+
+def prepare_kernel(ids, pack, field, partner, vec_out, own_out, work, wide):
+    work[...] = jnp.zeros_like(work)
+    block = ids[0] * GROUP + ids[1]
+    core = ids[1] % 2
+    mine = block_rows(block, pack, 0, field, work, wide)
+    own_out[...] = mine
+    here = pl.ds(pl.multiple_of(core * ATOMS, ATOMS), ATOMS)
+    for slot in range(GROUP):
+        vec_out[slot, here, :] = mine
+    theirs = block_rows(block ^ 1, pack, SUMS, partner, work, wide)
+    there = pl.ds(pl.multiple_of((1 - core) * ATOMS, ATOMS), ATOMS)
+    for slot in range(GROUP):
+        vec_out[slot, there, :] = theirs
+
+
+def pick_kernel(ids, mine, theirs, own, other, column):
+    core = ids[1] % 2
+    line = pl.ds(pl.multiple_of((ids[0] % 2) * HALF, HALF), HALF)
+    here = pl.ds(pl.multiple_of(core * ATOMS, ATOMS), ATOMS)
+    there = pl.ds(pl.multiple_of((1 - core) * ATOMS, ATOMS), ATOMS)
+
+    def take(along_z, along_row):
+        own[...] = along_z[line, here, :]
+        other[...] = along_z[line, there, :]
+        rows = along_row[:, here, :].reshape(WIDE, LANES)
+        for comp in range(COMPS):
+            column[comp] = jnp.broadcast_to(rows[:, SITE + comp : SITE + comp + 1], (WIDE, LANES))
+
+    @pl.when(core == 0)
+    def _():
+        take(theirs, mine)
+
+    @pl.when(core == 1)
+    def _():
+        take(mine, theirs)
 
 
 def lattice(comp, atom, cell):
@@ -76,7 +108,7 @@
     return (corner + inner).astype(F32) * SPACING
 
 
-def side_kernel(ids, pack, species, tile_map, jitters, aux_out, mask_out, column, work):
+def side_kernel(ids, species, tile_map, aux_out, mask_out, work):
     alpha = species[4:SUMS, :]
     lane = lax.broadcasted_iota(jnp.int32, (4, LANES), 1)
     rhs_lane = jnp.where(lane >= 2 * RHS, lane - 2 * RHS, jnp.where(lane >= RHS, lane - RHS, lane))
@@ -108,21 +140,6 @@
     place = lax.broadcasted_iota(jnp.int32, (blocks, WIDE), 0)
     spread = jnp.where(place == wanted, 1.0, 0.0).astype(BF16)
     mask_out[...] = 0.5 * jnp.dot(lines, spread, preferred_element_type=F32)
-
-    cells = jnp.concatenate([pack[CELL_ROW : CELL_ROW + 1, :], pack[CELL_ROW + 1 : CELL_ROW + 2, :]], axis=1)
-    place = lax.broadcasted_iota(jnp.int32, (LANES, blocks), 1)
-    wanted = (lax.broadcasted_iota(jnp.int32, (LANES, blocks), 0) >> 3) * GROUP + ids[1]
-    cell = jnp.sum(jnp.where(place == wanted, cells, 0.0), axis=1, keepdims=True).astype(jnp.int32)
-    comp = lax.broadcasted_iota(jnp.int32, (LANES, LANES), 0) & 7
-    work[...] = jnp.zeros_like(work)
-    for slot in range(GROUP):
-        work[slot * SUMS : slot * SUMS + COMPS, 0:ATOMS] = jitters[slot]
-    down = (lattice(comp, lane_ids(LANES), cell) + work[...]).T[0:ATOMS, :]
-    for slot in range(GROUP):
-        rows = slice(slot * ATOMS, (slot + 1) * ATOMS)
-        for comp in range(COMPS):
-            lane = slot * SUMS + comp
-            column[comp, rows, :] = jnp.broadcast_to(down[:, lane : lane + 1], (ATOMS, LANES))
 
 
 def right_side(vectors, side):
@@ -321,20 +338,36 @@
     return pl.BlockSpec(dims, lambda i: (0,) * len(dims))
 
 
+def number(row, z, core):
+    return row * GROUP + z * 2 + core
+
+
 def core_swap(value):
-    return lax.ppermute(value, "core", [(0, 1), (1, 0)])
-
-
-def gather_own(value):
-    return lax.all_to_all(value, "z", 0, 0)
+    return lax.ppermute(value, "device", [(here, here ^ 1) for here in range(GROUP * GROUP)])
+
+
+def exchange(value, groups):
+    return lax.all_to_all(value, "device", 0, 0, axis_index_groups=groups)
+
+
+ROWS = [[number(row, z, core) for row in range(GROUP)] for z in range(HALF) for core in range(2)]
+LINES = [[number(row, z, core) for z in range(HALF)] for row in range(GROUP) for core in range(2)]
+CHIPS = [[number(row, z, core) for row in range(GROUP) for z in range(HALF)] for core in range(2)]
+MIXED = [[number(row, z, 1) for row in (pair, pair + 1) for z in range(HALF)] for pair in range(0, GROUP, 2)] + [
+    [number(row, z, 0) for row in range(GROUP)] for z in range(HALF)
+]
 
 
 def local(external_field, jitter, species, alpha_table, block_cell, tile_map):
-    ids = jnp.stack([lax.axis_index("row"), lax.axis_index(("z", "core"))]).astype(jnp.int32)
-    jitters = lax.all_to_all(jnp.broadcast_to(jitter, (GROUP, COMPS, ATOMS)), "row", 0, 0)
+    me = lax.axis_index("device")
+    ids = jnp.stack([me // GROUP, me % GROUP]).astype(jnp.int32)
+    field = external_field.transpose(0, 2, 1)
+    across_jitter = core_swap(jitter)
+    across_field = core_swap(field)
     pack = jnp.concatenate(
         [
-            jnp.pad(jitter, ((0, CELL_ROW - COMPS), (0, LANES - ATOMS))),
+            jnp.pad(jitter, ((0, SUMS - COMPS), (0, LANES - ATOMS))),
+            jnp.pad(across_jitter, ((0, SUMS - COMPS), (0, LANES - ATOMS))),
             jnp.pad(block_cell.astype(F32).reshape(2, LANES), ((0, 6), (0, 0))),
         ]
     )
@@ -346,25 +379,32 @@
     )
     vec, vector = pl.pallas_call(
         prepare_kernel,
-        out_shape=(shape(HALF, ATOMS, LANES), shape(ATOMS, LANES)),
+        out_shape=(shape(GROUP, 2 * ATOMS, LANES), shape(ATOMS, LANES)),
+        in_specs=[SMEM, VMEM, VMEM, VMEM],
+        out_specs=(VMEM, VMEM),
+        scratch_shapes=[SQUARE, pltpu.VMEM((ATOMS, LANES), F32)],
+        compiler_params=PARAMS,
+        name="prepare",
+    )(ids, pack, field, across_field)
+    aux, mask = pl.pallas_call(
+        side_kernel,
+        out_shape=(shape(ATOMS + SUMS, LANES), shape(GROUP, WIDE)),
         in_specs=[SMEM, VMEM, VMEM],
         out_specs=(VMEM, VMEM),
-        scratch_shapes=[SQUARE, pltpu.VMEM((ATOMS, LANES), F32)],
-        compiler_params=PARAMS,
-        name="prepare",
-    )(ids, pack, external_field.transpose(0, 2, 1))
-    aux, mask, column = pl.pallas_call(
-        side_kernel,
-        out_shape=(shape(ATOMS + SUMS, LANES), shape(GROUP, WIDE), shape(COMPS, WIDE, LANES)),
-        in_specs=[SMEM, VMEM, VMEM, VMEM, VMEM],
+        scratch_shapes=[SQUARE],
+        compiler_params=PARAMS,
+        name="side",
+    )(ids, kinds, tile_map)
+    mine, aux, mask = lax.optimization_barrier((exchange(vec, MIXED), aux, mask))
+    half = shape(HALF, ATOMS, LANES)
+    own, other, column = pl.pallas_call(
+        pick_kernel,
+        out_shape=(half, half, shape(COMPS, WIDE, LANES)),
+        in_specs=[SMEM, VMEM, VMEM],
         out_specs=(VMEM, VMEM, VMEM),
-        scratch_shapes=[SQUARE],
-        compiler_params=PARAMS,
-        name="side",
-    )(ids, pack, kinds, tile_map, jitters)
-    own = gather_own(vec)
-    own, aux, mask, column = lax.optimization_barrier((own, aux, mask, column))
-    other = core_swap(own)
+        compiler_params=PARAMS,
+        name="pick",
+    )(ids, mine, core_swap(mine))
     side = pltpu.VMEM((PAIRS * NARROW, 2 * LANES), BF16)
     tile = shape(WIDE, PAIRS * NARROW, dtype=BF16)
     total, high0, low0 = pl.pallas_call(
@@ -385,7 +425,7 @@
         compiler_params=PARAMS,
         name="first_other",
     )(mask, column, other, total)
-    parts = lax.all_to_all(part, "row", 0, 0)
+    parts = exchange(part, ROWS)
     blocks = whole(GROUP, ATOMS, LANES)
     block = whole(1, ATOMS, LANES)
     shifted = pl.pallas_call(
@@ -398,7 +438,7 @@
         compiler_params=PARAMS,
         name="shifted",
     )(parts, vector, aux)
-    own2 = gather_own(shifted)
+    own2 = exchange(shifted, LINES)
     other2 = core_swap(own2)
     total2 = pl.pallas_call(
         second_own_kernel,
@@ -418,7 +458,7 @@
         compiler_params=PARAMS,
         name="second_other",
     )(other2, high1, low1, total2)
-    parts2 = lax.all_to_all(part2, "row", 0, 0)
+    parts2 = exchange(part2, ROWS)
     sums, state = pl.pallas_call(
         step_kernel,
         grid=(1,),
@@ -438,7 +478,7 @@
         name="pair",
     )(sums, core_swap(sums))
     pair = pair.reshape(GROUP * HALF, 1, LANES)
-    all_sums = lax.all_to_all(pair, ("row", "z"), 0, 0).reshape(GROUP, SUMS, LANES)
+    all_sums = exchange(pair, CHIPS).reshape(GROUP, SUMS, LANES)
     dipoles, residual = pl.pallas_call(
         finish_kernel,
         out_shape=(shape(COMPS, ATOMS, RHS), shape(COMPS, ATOMS, RHS)),
@@ -451,11 +491,11 @@
 
 
 def solution(mesh):
-    split = Mesh(mesh.devices.reshape(GROUP, HALF, 2), ("row", "z", "core"))
-    every = ("row", "z", "core")
+    flat = Mesh(mesh.devices.reshape(GROUP * GROUP), ("device",))
+    every = "device"
     return jax.shard_map(
         local,
-        mesh=split,
+        mesh=flat,
         in_specs=(P(None, None, every), P(None, every), P(every), P(), P(), P()),
         out_specs=(P(None, None, every), P(None, None, every)),
         check_vma=False,

time: 96 us -> 94.6 us (0.985)
  starting transfers between devices: 23.2 us -> 15.3 us
  blocking collectives: 48.3 us -> 53.7 us
  waiting for transfers between devices: 8.41 us -> 11.1 us
  local copies, waits for them, and re-layouts: 3.05 us -> 0.8 us
    all_to_all x2 -> x1, starting transfers between devices: 15.8 us -> 7.48 us  [exchange(): return lax.all_to_all(value, 'device', 0, 0, axis_index_groups=groups)]
    all_to_all x4, blocking collectives: 48.3 us -> 53.7 us  [exchange(): return lax.all_to_all(value, 'device', 0, 0, axis_index_groups=groups)]
    ppermute x3 -> x5, waiting for transfers between devices: 0.93 us -> 3.01 us  [core_swap(): lax.ppermute(value, 'device', [(here, here ^ 1) for here in range(GROUP *...]
    broadcast_in_dim x1 -> x0, local copies, waits for them, and re-layouts: 1.3 us -> none  [local(): jnp.broadcast_to(jitter, (GROUP, COMPS, ATOMS))]
    pallas_call x1 -> x2, Pallas kernels: 1.35 us -> 2.36 us  [the longest x1 1.54 us: local(): pl.pallas_call(prepare_kernel, out_shape=(shape(GROUP, 2 * ATOMS, LANES),...]
    all_to_all x2 -> x1, waiting for transfers between devices: 7.48 us -> 8.13 us  [exchange(): return lax.all_to_all(value, 'device', 0, 0, axis_index_groups=groups)]
    ppermute x3 -> x5, starting transfers between devices: 7.4 us -> 7.81 us  [core_swap(): lax.ppermute(value, 'device', [(here, here ^ 1) for here in range(GROUP *...]
  transfers between devices with their start and end apart: 5 -> 6, of which waited for: 4 -> 5; matrix products, arithmetic and copies ran while one was open for 3% -> 3% of each run, Pallas kernels for 5% -> 2%
where the time goes in v6:
time: 94.6 us; the launch traced here: 94.1 us
  blocking collectives  53.7 us (57%)
  starting transfers between devices  15.3 us (16%)
  waiting for transfers between devices  11.1 us (12%)
  Pallas kernels  9.7 us (10%)
  other arithmetic  2.79 us (3%)
    all_to_all x4, blocking collectives, exchange(): return lax.all_to_all(value, 'device', 0, 0, axis_index_groups=groups)  53.7 us
    all_to_all x1, waiting for transfers between devices, exchange(): return lax.all_to_all(value, 'device', 0, 0, axis_index_groups=groups)  8.13 us
    ppermute x5, starting transfers between devices, core_swap(): lax.ppermute(value, 'device', [(here, here ^ 1) for here in range(GROUP *...  7.81 us
    all_to_all x1, starting transfers between devices, exchange(): return lax.all_to_all(value, 'device', 0, 0, axis_index_groups=groups)  7.48 us
    ppermute x5, waiting for transfers between devices, core_swap(): lax.ppermute(value, 'device', [(here, here ^ 1) for here in range(GROUP *...  3.01 us
  transfers between devices with their start and end apart: 6, of which 5 were waited for; matrix products, arithmetic and copies ran while one was open for 3% of the time, Pallas kernels for 2%

profile of v6, /device:TPU:1, one launch (start us, length us, event | category | flops | bytes accessed | tf_op | source)
XLA Modules:
  0.0 94.1 jit_solution(4274024664944327146)
XLA Ops:
  0.6 3.3 %collective-permute-start = (f32[3,32]{1,0:T(4,128)}, f32[3,32]{1,0:T(4,128)S(1)}, u32[]{:S(2)}, u32[]{:S(2)}) collective-permute-start(f32[3,32]{1,0:T(4,128)} %param.7), channel_id=1, source_target_pairs={{0,1},{1,0},{2,3},{3,2},{4,5},{5,4},{6,7},{7,6},{8,9},{9,8},{10,11... | collective-permute-start | bytes 1160 | tf_op jit(solution)/shard_map/ppermute | solution.py:346
  4.0 0.1 collective-permute-start.1
  4.1 0.7 convert_bitcast_fusion
  4.8 0.1 pad_add_fusion.ids
  4.8 0.2 collective-permute-done
  5.0 0.7 select_maximum_fusion.pack
  5.7 0.0 collective-permute-done.1.partner
  5.7 0.8 copy-done.1
  6.5 1.5 %prepare.1 = (f32[16,64,128]{2,1,0:T(8,128)}, f32[32,128]{1,0:T(8,128)S(1)}) custom-call(s32[2]{0:T(128)S(1)} %pad_add_fusion.ids, f32[24,128]{1,0:T(8,128)S(1)} %select_maximum_fusion.pack, f32[3,32,36]{2,1,0:T(8,128)S(1)} %bitcast.17, f32[3,32,36]{2,1,0:T(8,128)S(1)} %collective-permute-done.1.partner), custom_call_target="tpu_custom_call" | custom-call | tf_op jit(solution)/shard_map/prepare/pallas_call | solution.py:380
  8.0 7.5 %all-to-all-start = ((f32[16,64,128]{2,1,0:T(8,128)}), f32[16,64,128]{2,1,0:T(8,128)S(1)}, u32[]{:S(2)}, u32[]{:S(2)}) async-start(f32[16,64,128]{2,1,0:T(8,128)} %get-tuple-element.22), calls=%async_computation | async-start | bytes 1048576 | tf_op jit(solution)/shard_map/all_to_all | solution.py:350
  15.5 0.7 convert_bitcast_fusion.1
  16.2 0.7 select_maximum_fusion.2.species
  16.9 0.8 side.1
  17.7 8.1 %all-to-all-done.mine = f32[16,64,128]{2,1,0:T(8,128)S(1)} async-done(((f32[16,64,128]{2,1,0:T(8,128)}), f32[16,64,128]{2,1,0:T(8,128)S(1)}, u32[]{:S(2)}, u32[]{:S(2)}) %all-to-all-start) | async-done | bytes 524320 | tf_op jit(solution)/shard_map/all_to_all | solution.py:350
  25.8 0.0 collective-permute-start.2
  25.8 1.9 %collective-permute-done.2.theirs = f32[16,64,128]{2,1,0:T(8,128)S(1)} collective-permute-done((f32[16,64,128]{2,1,0:T(8,128)S(1)}, f32[16,64,128]{2,1,0:T(8,128)S(1)}, u32[]{:S(2)}, u32[]{:S(2)}) %collective-permute-start.2) | collective-permute-done | bytes 524320 | tf_op jit(solution)/shard_map/ppermute | solution.py:346
  27.7 0.8 pick.1
  28.5 1.7 %first_own.1 = (f32[512,128]{1,0:T(8,128)S(1)}, bf16[512,1280]{1,0:T(8,128)(2,1)S(1)}, bf16[512,1280]{1,0:T(8,128)(2,1)S(1)}) custom-call(f32[16,512]{1,0:T(8,128)S(1)} %get-tuple-element.25.mask, f32[3,512,128]{2,1,0:T(8,128)S(1)} %get-tuple-element.27.column, f32[8,32,128]{2,1,0:T(8,128)S(1)} %get-tuple-element.29.gathered), custom_call_target="tpu_custom_call" | custom-call | tf_op jit(solution)/shard_map/first_own/pallas_call | solution.py:410
  30.3 1.7 %first_other.1 = (f32[16,32,128]{2,1,0:T(8,128)S(1)}, bf16[512,1280]{1,0:T(8,128)(2,1)S(1)}, bf16[512,1280]{1,0:T(8,128)(2,1)S(1)}) custom-call(f32[16,512]{1,0:T(8,128)S(1)} %get-tuple-element.25.mask, f32[3,512,128]{2,1,0:T(8,128)S(1)} %get-tuple-element.27.column, f32[8,32,128]{2,1,0:T(8,128)S(1)} %get-tuple-element.28.gathered, ...), custom_call_target="tpu_custom_call" | custom-call | tf_op jit(solution)/shard_map/first_other/pallas_call | solution.py:419
  32.0 14.6 %all_to_all.25.parts = f32[16,32,128]{2,1,0:T(8,128)S(1)} all-to-all(f32[16,32,128]{2,1,0:T(8,128)S(1)} %get-tuple-element.31), channel_id=1, replica_groups={{0,16,32,48,64,80,96,112,128,144,160,176,192,208,224,240},{1,17,33,49,6..., dimensions={0} | all-to-all | bytes 524288 | tf_op jit(solution)/shard_map/all_to_all | solution.py:350
  46.6 0.2 shifted.1
  46.8 12.2 %all_to_all.26.gathered = f32[8,32,128]{2,1,0:T(8,128)S(1)} all-to-all(f32[8,32,128]{2,1,0:T(8,128)S(1)} %shifted.1), channel_id=1, replica_groups={{0,2,4,6,8,10,12,14},{1,3,5,7,9,11,13,15},{16,18,20,22,24,26,28,30},{17..., dimensions={0} | all-to-all | bytes 262144 | tf_op jit(solution)/shard_map/all_to_all | solution.py:350
  59.0 2.8 %collective-permute-start.3 = (f32[8,32,128]{2,1,0:T(8,128)S(1)}, f32[8,32,128]{2,1,0:T(8,128)S(1)}, u32[]{:S(2)}, u32[]{:S(2)}) collective-permute-start(f32[8,32,128]{2,1,0:T(8,128)S(1)} %all_to_all.26.gathered), channel_id=1, source_target_pairs={{0,1},{1,0},{2,3},{3,2},{4,5},{5,4},{6,7},{7,6},{8,9},{9,8},{10,11... | collective-permute-start | bytes 393224 | tf_op jit(solution)/shard_map/ppermute | solution.py:346
  61.8 0.9 second_own.1.total
  62.7 0.1 collective-permute-done.3.gathered
  62.8 0.9 second_other.1
  63.7 10.7 %all_to_all.27.parts = f32[16,32,128]{2,1,0:T(8,128)S(1)} all-to-all(f32[16,32,128]{2,1,0:T(8,128)S(1)} %second_other.1), channel_id=1, replica_groups={{0,16,32,48,64,80,96,112,128,144,160,176,192,208,224,240},{1,17,33,49,6..., dimensions={0} | all-to-all | bytes 524288 | tf_op jit(solution)/shard_map/all_to_all | solution.py:350
  74.4 0.4 step.1
  74.8 1.6 %collective-permute-start.4 = (f32[8,128]{1,0:T(8,128)S(1)}, f32[8,128]{1,0:T(8,128)S(1)}, u32[]{:S(2)}, u32[]{:S(2)}) collective-permute-start(f32[8,128]{1,0:T(8,128)S(1)} %get-tuple-element.38.sums), channel_id=1, source_target_pairs={{0,1},{1,0},{2,3},{3,2},{4,5},{5,4},{6,7},{7,6},{8,9},{9,8},{10,11... | collective-permute-start | bytes 12296 | tf_op jit(solution)/shard_map/ppermute | solution.py:346
  76.3 0.8 collective-permute-done.4.swapped
  77.2 16.1 %all_to_all.28 = f32[128,1,128]{2,1,0:T(1,128)S(1)} all-to-all(f32[128,1,128]{2,1,0:T(1,128)S(1)} %bitcast.15), channel_id=1, replica_groups={{0,2,4,6,8,10,12,14,16,18,20,22,24,26,28,30,32,34,36,38,40,42,44,46,48,..., dimensions={0} | all-to-all | bytes 131072 | tf_op jit(solution)/shard_map/all_to_all | solution.py:350
  93.3 0.8 finish.1
  (4 shorter events, 0.0 us)
Async XLA Ops:
  0.6 16.2 %copy-start = (s32[256,256]{1,0:T(8,128)S(1)}, s32[256,256]{1,0:T(8,128)}, u32[]{:S(2)}) copy-start(s32[256,256]{1,0:T(8,128)} %tile_map.1) | copy-start | bytes 786436
  0.6 4.4 %collective-permute-start = (f32[3,32]{1,0:T(4,128)}, f32[3,32]{1,0:T(4,128)S(1)}, u32[]{:S(2)}, u32[]{:S(2)}) collective-permute-start(f32[3,32]{1,0:T(4,128)} %param.7), channel_id=1, source_target_pairs={{0,1},{1,0},{2,3},{3,2},{4,5},{5,4},{6,7},{7,6},{8,9},{9,8},{10,11... | collective-permute-start | bytes 1160 | tf_op jit(solution)/shard_map/ppermute | solution.py:346
  4.0 1.7 %collective-permute-start.1 = (f32[3,32,36]{2,1,0:T(8,128)}, f32[3,32,36]{2,1,0:T(8,128)S(1)}, u32[]{:S(2)}, u32[]{:S(2)}) collective-permute-start(f32[3,32,36]{2,1,0:T(8,128)} %bitcast.16), channel_id=1, source_target_pairs={{0,1},{1,0},{2,3},{3,2},{4,5},{5,4},{6,7},{7,6},{8,9},{9,8},{10,11... | collective-permute-start | bytes 41480 | tf_op jit(solution)/shard_map/ppermute | solution.py:346
  5.7 0.8 copy-start.1
  8.0 17.8 %all-to-all-start = ((f32[16,64,128]{2,1,0:T(8,128)}), f32[16,64,128]{2,1,0:T(8,128)S(1)}, u32[]{:S(2)}, u32[]{:S(2)}) async-start(f32[16,64,128]{2,1,0:T(8,128)} %get-tuple-element.22), calls=%async_computation | async-start | bytes 1048576 | tf_op jit(solution)/shard_map/all_to_all | solution.py:350
  25.8 1.9 %collective-permute-start.2 = (f32[16,64,128]{2,1,0:T(8,128)S(1)}, f32[16,64,128]{2,1,0:T(8,128)S(1)}, u32[]{:S(2)}, u32[]{:S(2)}) collective-permute-start(f32[16,64,128]{2,1,0:T(8,128)S(1)} %all-to-all-done.mine), channel_id=1, source_target_pairs={{0,1},{1,0},{2,3},{3,2},{4,5},{5,4},{6,7},{7,6},{8,9},{9,8},{10,11... | collective-permute-start | bytes 1572872 | tf_op jit(solution)/shard_map/ppermute | solution.py:346
  59.0 3.8 %collective-permute-start.3 = (f32[8,32,128]{2,1,0:T(8,128)S(1)}, f32[8,32,128]{2,1,0:T(8,128)S(1)}, u32[]{:S(2)}, u32[]{:S(2)}) collective-permute-start(f32[8,32,128]{2,1,0:T(8,128)S(1)} %all_to_all.26.gathered), channel_id=1, source_target_pairs={{0,1},{1,0},{2,3},{3,2},{4,5},{5,4},{6,7},{7,6},{8,9},{9,8},{10,11... | collective-permute-start | bytes 393224 | tf_op jit(solution)/shard_map/ppermute | solution.py:346
  74.8 2.4 %collective-permute-start.4 = (f32[8,128]{1,0:T(8,128)S(1)}, f32[8,128]{1,0:T(8,128)S(1)}, u32[]{:S(2)}, u32[]{:S(2)}) collective-permute-start(f32[8,128]{1,0:T(8,128)S(1)} %get-tuple-element.38.sums), channel_id=1, source_target_pairs={{0,1},{1,0},{2,3},{3,2},{4,5},{5,4},{6,7},{7,6},{8,9},{9,8},{10,11... | collective-permute-start | bytes 12296 | tf_op jit(solution)/shard_map/ppermute | solution.py:346

commit v7 on v6

--- a/solution.py
+++ b/solution.py
@@ -53,45 +53,50 @@
     return jnp.where(first, of_first, jnp.where(second, of_second, jnp.where(third, of_third, 1.0)))
 
 
-def block_rows(own, pack, jitter_row, field, work, wide):
+def block_sites(block, pack, jitter_row):
     index = lax.broadcasted_iota(jnp.int32, (SUMS, LANES), 0) * LANES + lane_ids(SUMS)
-    found = jnp.where(index == own, pack[CELL_ROW : CELL_ROW + SUMS, :], 0.0)
+    found = jnp.where(index == block, pack[CELL_ROW : CELL_ROW + SUMS, :], 0.0)
     cell = jnp.sum(jnp.sum(found, axis=0, keepdims=True), axis=1, keepdims=True).astype(jnp.int32)
     comp = lax.broadcasted_iota(jnp.int32, (SUMS, LANES), 0)
-    work[SITE : SITE + SUMS, :] = lattice(comp, lane_ids(SUMS), cell) + pack[jitter_row : jitter_row + SUMS, :]
-    wide[...] = work[...].T[0:ATOMS, :]
-    for comp in range(COMPS):
-        wide[:, comp * RHS : (comp + 1) * RHS] = field[comp]
-    return wide[...]
+    return lattice(comp, lane_ids(SUMS), cell) + pack[jitter_row : jitter_row + SUMS, :]
 
 
 def prepare_kernel(ids, pack, field, partner, vec_out, own_out, work, wide):
     work[...] = jnp.zeros_like(work)
     block = ids[0] * GROUP + ids[1]
     core = ids[1] % 2
-    mine = block_rows(block, pack, 0, field, work, wide)
-    own_out[...] = mine
-    here = pl.ds(pl.multiple_of(core * ATOMS, ATOMS), ATOMS)
-    for slot in range(GROUP):
-        vec_out[slot, here, :] = mine
-    theirs = block_rows(block ^ 1, pack, SUMS, partner, work, wide)
-    there = pl.ds(pl.multiple_of((1 - core) * ATOMS, ATOMS), ATOMS)
-    for slot in range(GROUP):
-        vec_out[slot, there, :] = theirs
+    comp = lax.broadcasted_iota(jnp.int32, (SUMS, LANES), 0)
+    for flip, vectors in ((0, field), (1, partner)):
+        near = block_sites(block ^ flip, pack, flip * SUMS)
+        beside = block_sites(block ^ flip ^ GROUP, pack, (3 + flip) * SUMS)
+        work[SITE : SITE + SUMS, :] = jnp.where(comp < 4, near, pltpu.roll(beside, 4, 0))
+        wide[...] = work[...].T[0:ATOMS, :]
+        for part in range(COMPS):
+            wide[:, part * RHS : (part + 1) * RHS] = vectors[part]
+        turned = wide[...]
+        if flip == 0:
+            own_out[...] = turned
+        rows = pl.ds(pl.multiple_of((core ^ flip) * ATOMS, ATOMS), ATOMS)
+        for slot in range(HALF):
+            vec_out[slot, rows, :] = turned
 
 
 def pick_kernel(ids, mine, theirs, own, other, column):
     core = ids[1] % 2
-    line = pl.ds(pl.multiple_of((ids[0] % 2) * HALF, HALF), HALF)
+    side = ids[0] % 2
     here = pl.ds(pl.multiple_of(core * ATOMS, ATOMS), ATOMS)
     there = pl.ds(pl.multiple_of((1 - core) * ATOMS, ATOMS), ATOMS)
 
     def take(along_z, along_row):
-        own[...] = along_z[line, here, :]
-        other[...] = along_z[line, there, :]
-        rows = along_row[:, here, :].reshape(WIDE, LANES)
-        for comp in range(COMPS):
-            column[comp] = jnp.broadcast_to(rows[:, SITE + comp : SITE + comp + 1], (WIDE, LANES))
+        own[...] = along_z[:, here, :]
+        other[...] = along_z[:, there, :]
+        for slot in range(HALF):
+            rows = along_row[slot, here, :]
+            for flip in range(2):
+                place = pl.ds(pl.multiple_of((2 * slot + (side ^ flip)) * ATOMS, ATOMS), ATOMS)
+                for comp in range(COMPS):
+                    lane = SITE + 4 * flip + comp
+                    column[comp, place, :] = jnp.broadcast_to(rows[:, lane : lane + 1], (ATOMS, LANES))
 
     @pl.when(core == 0)
     def _():
@@ -342,8 +347,12 @@
     return row * GROUP + z * 2 + core
 
 
+def trade(value, bits):
+    return lax.ppermute(value, "device", [(here, here ^ bits) for here in range(GROUP * GROUP)])
+
+
 def core_swap(value):
-    return lax.ppermute(value, "device", [(here, here ^ 1) for here in range(GROUP * GROUP)])
+    return trade(value, 1)
 
 
 def exchange(value, groups):
@@ -353,8 +362,8 @@
 ROWS = [[number(row, z, core) for row in range(GROUP)] for z in range(HALF) for core in range(2)]
 LINES = [[number(row, z, core) for z in range(HALF)] for row in range(GROUP) for core in range(2)]
 CHIPS = [[number(row, z, core) for row in range(GROUP) for z in range(HALF)] for core in range(2)]
-MIXED = [[number(row, z, 1) for row in (pair, pair + 1) for z in range(HALF)] for pair in range(0, GROUP, 2)] + [
-    [number(row, z, 0) for row in range(GROUP)] for z in range(HALF)
+MIXED = [[number(row, z, 1) for z in range(HALF)] for row in range(GROUP)] + [
+    [number(row, z, 0) for row in range(first, GROUP, 2)] for first in range(2) for z in range(HALF)
 ]
 
 
@@ -362,15 +371,11 @@
     me = lax.axis_index("device")
     ids = jnp.stack([me // GROUP, me % GROUP]).astype(jnp.int32)
     field = external_field.transpose(0, 2, 1)
-    across_jitter = core_swap(jitter)
     across_field = core_swap(field)
-    pack = jnp.concatenate(
-        [
-            jnp.pad(jitter, ((0, SUMS - COMPS), (0, LANES - ATOMS))),
-            jnp.pad(across_jitter, ((0, SUMS - COMPS), (0, LANES - ATOMS))),
-            jnp.pad(block_cell.astype(F32).reshape(2, LANES), ((0, 6), (0, 0))),
-        ]
-    )
+    shifts = [jitter] + [trade(jitter, bits) for bits in (1, GROUP, GROUP + 1)]
+    shifts = [jnp.pad(shift, ((0, SUMS - COMPS), (0, LANES - ATOMS))) for shift in shifts]
+    cells = jnp.pad(block_cell.astype(F32).reshape(2, LANES), ((0, 6), (0, 0)))
+    pack = jnp.concatenate(shifts[:2] + [cells] + shifts[2:])
     kinds = jnp.concatenate(
         [
             jnp.pad(species.astype(F32)[None], ((0, 3), (0, LANES - ATOMS))),
@@ -379,7 +384,7 @@
     )
     vec, vector = pl.pallas_call(
         prepare_kernel,
-        out_shape=(shape(GROUP, 2 * ATOMS, LANES), shape(ATOMS, LANES)),
+        out_shape=(shape(HALF, 2 * ATOMS, LANES), shape(ATOMS, LANES)),
         in_specs=[SMEM, VMEM, VMEM, VMEM],
         out_specs=(VMEM, VMEM),
         scratch_shapes=[SQUARE, pltpu.VMEM((ATOMS, LANES), F32)],

time: 94.6 us -> 93.4 us (0.987)
  waiting for transfers between devices: 11.1 us -> 8.7 us
  local copies, waits for them, and re-layouts: 0.8 us -> 2.44 us
  starting transfers between devices: 15.3 us -> 16.3 us
    all_to_all x1, waiting for transfers between devices: 8.13 us -> 6.23 us  [exchange(): return lax.all_to_all(value, 'device', 0, 0, axis_index_groups=groups)]
    ppermute x5 -> x7, starting transfers between devices: 7.81 us -> 9.69 us  [trade(): lax.ppermute(value, 'device', [(here, here ^ bits) for here in range(GROU...]
    unnamed x4 -> x8, local copies, waits for them, and re-layouts: 0.8 us -> 2.44 us
    ppermute x5 -> x7, waiting for transfers between devices: 3.01 us -> 2.47 us  [trade(): lax.ppermute(value, 'device', [(here, here ^ bits) for here in range(GROU...]
  transfers between devices with their start and end apart: 6 -> 8, of which waited for: 5 -> 4; matrix products, arithmetic and copies ran while one was open for 3% -> 3% of each run, Pallas kernels for 2% -> 2%
where the time goes in v7:
time: 93.4 us; the launch traced here: 92.9 us
  blocking collectives  52.9 us (57%)
  starting transfers between devices  16.3 us (17%)
  Pallas kernels  9.64 us (10%)
  waiting for transfers between devices  8.7 us (9%)
  local copies, waits for them, and re-layouts  2.44 us (3%)
  other arithmetic  2.1 us (2%)
    all_to_all x4, blocking collectives, exchange(): return lax.all_to_all(value, 'device', 0, 0, axis_index_groups=groups)  52.9 us
    ppermute x7, starting transfers between devices, trade(): lax.ppermute(value, 'device', [(here, here ^ bits) for here in range(GROU...  9.69 us
    all_to_all x1, starting transfers between devices, exchange(): return lax.all_to_all(value, 'device', 0, 0, axis_index_groups=groups)  6.65 us
    all_to_all x1, waiting for transfers between devices, exchange(): return lax.all_to_all(value, 'device', 0, 0, axis_index_groups=groups)  6.23 us
    ppermute x7, waiting for transfers between devices, trade(): lax.ppermute(value, 'device', [(here, here ^ bits) for here in range(GROU...  2.47 us
    unnamed x8, local copies, waits for them, and re-layouts  2.44 us
  transfers between devices with their start and end apart: 8, of which 4 were waited for; matrix products, arithmetic and copies ran while one was open for 3% of the time, Pallas kernels for 2%

profile of v7, /device:TPU:1, one launch (start us, length us, event | category | flops | bytes accessed | tf_op | source)
XLA Modules:
  0.0 92.9 jit_solution(4204437403660352031)
XLA Ops:
  0.6 3.3 %collective-permute-start = (f32[3,32]{1,0:T(4,128)}, f32[3,32]{1,0:T(4,128)S(1)}, u32[]{:S(2)}, u32[]{:S(2)}) collective-permute-start(f32[3,32]{1,0:T(4,128)} %param.7), channel_id=1, source_target_pairs={{0,1},{1,0},{2,3},{3,2},{4,5},{5,4},{6,7},{7,6},{8,9},{9,8},{10,11... | collective-permute-start | bytes 1160 | tf_op jit(solution)/shard_map/ppermute | solution.py:351
  4.0 1.4 %collective-permute-start.1 = (f32[3,32]{1,0:T(4,128)}, f32[3,32]{1,0:T(4,128)S(1)}, u32[]{:S(2)}, u32[]{:S(2)}) collective-permute-start(f32[3,32]{1,0:T(4,128)} %param.7), channel_id=1, source_target_pairs={{0,16},{1,17},{2,18},{3,19},{4,20},{5,21},{6,22},{7,23},{8,24},{9,... | collective-permute-start | bytes 1160 | tf_op jit(solution)/shard_map/ppermute | solution.py:351
  5.4 0.7 collective-permute-start.3
  6.1 0.7 constant_dynamic-update-slice_fusion.4
  6.8 0.7 convert_bitcast_fusion
  7.5 0.1 pad_add_fusion.ids
  7.6 0.0 copy-start.1
  7.6 0.8 copy-done.1
  8.4 1.4 %prepare.1 = (f32[8,64,128]{2,1,0:T(8,128)}, f32[32,128]{1,0:T(8,128)S(1)}) custom-call(s32[2]{0:T(128)S(1)} %pad_add_fusion.ids, f32[40,128]{1,0:T(8,128)S(1)} %constant_dynamic-update-slice_fusion.pack, f32[3,32,36]{2,1,0:T(8,128)S(1)} %bitcast.17, f32[3,32,36]{2,1,0:T(8,128)S(1)} %collective-permute-done.3.partner), custom_call_target="tpu_custom_call" | custom-call | tf_op jit(solution)/shard_map/prepare/pallas_call | solution.py:385
  9.9 6.6 %all-to-all-start = ((f32[8,64,128]{2,1,0:T(8,128)}), f32[8,64,128]{2,1,0:T(8,128)S(1)}, u32[]{:S(2)}, u32[]{:S(2)}) async-start(f32[8,64,128]{2,1,0:T(8,128)} %get-tuple-element.22), calls=%async_computation | async-start | bytes 524288 | tf_op jit(solution)/shard_map/all_to_all | solution.py:359
  16.5 0.7 convert_bitcast_fusion.1
  17.2 0.7 select_maximum_fusion.species
  17.9 0.9 %copy-done = s32[256,256]{1,0:T(8,128)S(1)} copy-done((s32[256,256]{1,0:T(8,128)S(1)}, s32[256,256]{1,0:T(8,128)}, u32[]{:S(2)}) %copy-start) | copy-done | bytes 262168
  18.8 0.8 side.1
  19.6 6.2 %all-to-all-done.mine = f32[8,64,128]{2,1,0:T(8,128)S(1)} async-done(((f32[8,64,128]{2,1,0:T(8,128)}), f32[8,64,128]{2,1,0:T(8,128)S(1)}, u32[]{:S(2)}, u32[]{:S(2)}) %all-to-all-start) | async-done | bytes 262176 | tf_op jit(solution)/shard_map/all_to_all | solution.py:359
  25.8 1.5 %collective-permute-done.4.theirs = f32[8,64,128]{2,1,0:T(8,128)S(1)} collective-permute-done((f32[8,64,128]{2,1,0:T(8,128)S(1)}, f32[8,64,128]{2,1,0:T(8,128)S(1)}, u32[]{:S(2)}, u32[]{:S(2)}) %collective-permute-start.4) | collective-permute-done | bytes 262176 | tf_op jit(solution)/shard_map/ppermute | solution.py:351
  27.4 0.9 pick.1
  28.3 1.7 %first_own.1 = (f32[512,128]{1,0:T(8,128)S(1)}, bf16[512,1280]{1,0:T(8,128)(2,1)S(1)}, bf16[512,1280]{1,0:T(8,128)(2,1)S(1)}) custom-call(f32[16,512]{1,0:T(8,128)S(1)} %get-tuple-element.25.mask, f32[3,512,128]{2,1,0:T(8,128)S(1)} %get-tuple-element.27.column, f32[8,32,128]{2,1,0:T(8,128)S(1)} %get-tuple-element.29.gathered), custom_call_target="tpu_custom_call" | custom-call | tf_op jit(solution)/shard_map/first_own/pallas_call | solution.py:415
  30.0 1.7 %first_other.1 = (f32[16,32,128]{2,1,0:T(8,128)S(1)}, bf16[512,1280]{1,0:T(8,128)(2,1)S(1)}, bf16[512,1280]{1,0:T(8,128)(2,1)S(1)}) custom-call(f32[16,512]{1,0:T(8,128)S(1)} %get-tuple-element.25.mask, f32[3,512,128]{2,1,0:T(8,128)S(1)} %get-tuple-element.27.column, f32[8,32,128]{2,1,0:T(8,128)S(1)} %get-tuple-element.28.gathered, ...), custom_call_target="tpu_custom_call" | custom-call | tf_op jit(solution)/shard_map/first_other/pallas_call | solution.py:424
  31.7 14.7 %all_to_all.25.parts = f32[16,32,128]{2,1,0:T(8,128)S(1)} all-to-all(f32[16,32,128]{2,1,0:T(8,128)S(1)} %get-tuple-element.31), channel_id=1, replica_groups={{0,16,32,48,64,80,96,112,128,144,160,176,192,208,224,240},{1,17,33,49,6..., dimensions={0} | all-to-all | bytes 524288 | tf_op jit(solution)/shard_map/all_to_all | solution.py:359
  46.4 0.2 shifted.1
  46.6 11.3 %all_to_all.26.gathered = f32[8,32,128]{2,1,0:T(8,128)S(1)} all-to-all(f32[8,32,128]{2,1,0:T(8,128)S(1)} %shifted.1), channel_id=1, replica_groups={{0,2,4,6,8,10,12,14},{1,3,5,7,9,11,13,15},{16,18,20,22,24,26,28,30},{17..., dimensions={0} | all-to-all | bytes 262144 | tf_op jit(solution)/shard_map/all_to_all | solution.py:359
  57.9 2.6 %collective-permute-start.5 = (f32[8,32,128]{2,1,0:T(8,128)S(1)}, f32[8,32,128]{2,1,0:T(8,128)S(1)}, u32[]{:S(2)}, u32[]{:S(2)}) collective-permute-start(f32[8,32,128]{2,1,0:T(8,128)S(1)} %all_to_all.26.gathered), channel_id=1, source_target_pairs={{0,1},{1,0},{2,3},{3,2},{4,5},{5,4},{6,7},{7,6},{8,9},{9,8},{10,11... | collective-permute-start | bytes 393224 | tf_op jit(solution)/shard_map/ppermute | solution.py:351
  60.6 0.9 second_own.1.total
  61.5 0.1 collective-permute-done.5.gathered
  61.6 0.9 second_other.1
  62.5 10.8 %all_to_all.27.parts = f32[16,32,128]{2,1,0:T(8,128)S(1)} all-to-all(f32[16,32,128]{2,1,0:T(8,128)S(1)} %second_other.1), channel_id=1, replica_groups={{0,16,32,48,64,80,96,112,128,144,160,176,192,208,224,240},{1,17,33,49,6..., dimensions={0} | all-to-all | bytes 524288 | tf_op jit(solution)/shard_map/all_to_all | solution.py:359
  73.2 0.4 step.1
  73.6 1.6 %collective-permute-start.6 = (f32[8,128]{1,0:T(8,128)S(1)}, f32[8,128]{1,0:T(8,128)S(1)}, u32[]{:S(2)}, u32[]{:S(2)}) collective-permute-start(f32[8,128]{1,0:T(8,128)S(1)} %get-tuple-element.38.sums), channel_id=1, source_target_pairs={{0,1},{1,0},{2,3},{3,2},{4,5},{5,4},{6,7},{7,6},{8,9},{9,8},{10,11... | collective-permute-start | bytes 12296 | tf_op jit(solution)/shard_map/ppermute | solution.py:351
  75.1 0.8 collective-permute-done.6.swapped
  75.9 16.1 %all_to_all.28 = f32[128,1,128]{2,1,0:T(1,128)S(1)} all-to-all(f32[128,1,128]{2,1,0:T(1,128)S(1)} %bitcast.15), channel_id=1, replica_groups={{0,2,4,6,8,10,12,14,16,18,20,22,24,26,28,30,32,34,36,38,40,42,44,46,48,..., dimensions={0} | all-to-all | bytes 131072 | tf_op jit(solution)/shard_map/all_to_all | solution.py:359
  92.1 0.8 finish.1
  (12 shorter events, 0.0 us)
Async XLA Ops:
  0.6 6.9 %collective-permute-start = (f32[3,32]{1,0:T(4,128)}, f32[3,32]{1,0:T(4,128)S(1)}, u32[]{:S(2)}, u32[]{:S(2)}) collective-permute-start(f32[3,32]{1,0:T(4,128)} %param.7), channel_id=1, source_target_pairs={{0,1},{1,0},{2,3},{3,2},{4,5},{5,4},{6,7},{7,6},{8,9},{9,8},{10,11... | collective-permute-start | bytes 1160 | tf_op jit(solution)/shard_map/ppermute | solution.py:351
  4.0 3.6 %collective-permute-start.2 = (f32[3,32]{1,0:T(4,128)}, f32[3,32]{1,0:T(4,128)S(1)}, u32[]{:S(2)}, u32[]{:S(2)}) collective-permute-start(f32[3,32]{1,0:T(4,128)} %param.7), channel_id=1, source_target_pairs={{0,17},{1,16},{2,19},{3,18},{4,21},{5,20},{6,23},{7,22},{8,25},{9,... | collective-permute-start | bytes 1160 | tf_op jit(solution)/shard_map/ppermute | solution.py:351
  4.0 3.6 %collective-permute-start.1 = (f32[3,32]{1,0:T(4,128)}, f32[3,32]{1,0:T(4,128)S(1)}, u32[]{:S(2)}, u32[]{:S(2)}) collective-permute-start(f32[3,32]{1,0:T(4,128)} %param.7), channel_id=1, source_target_pairs={{0,16},{1,17},{2,18},{3,19},{4,20},{5,21},{6,22},{7,23},{8,24},{9,... | collective-permute-start | bytes 1160 | tf_op jit(solution)/shard_map/ppermute | solution.py:351
  5.4 2.2 %collective-permute-start.3 = (f32[3,32,36]{2,1,0:T(8,128)}, f32[3,32,36]{2,1,0:T(8,128)S(1)}, u32[]{:S(2)}, u32[]{:S(2)}) collective-permute-start(f32[3,32,36]{2,1,0:T(8,128)} %bitcast.16), channel_id=1, source_target_pairs={{0,1},{1,0},{2,3},{3,2},{4,5},{5,4},{6,7},{7,6},{8,9},{9,8},{10,11... | collective-permute-start | bytes 41480 | tf_op jit(solution)/shard_map/ppermute | solution.py:351
  7.6 0.8 copy-start.1
  9.9 16.0 %all-to-all-start = ((f32[8,64,128]{2,1,0:T(8,128)}), f32[8,64,128]{2,1,0:T(8,128)S(1)}, u32[]{:S(2)}, u32[]{:S(2)}) async-start(f32[8,64,128]{2,1,0:T(8,128)} %get-tuple-element.22), calls=%async_computation | async-start | bytes 524288 | tf_op jit(solution)/shard_map/all_to_all | solution.py:359
  17.8 0.9 %copy-start = (s32[256,256]{1,0:T(8,128)S(1)}, s32[256,256]{1,0:T(8,128)}, u32[]{:S(2)}) copy-start(s32[256,256]{1,0:T(8,128)} %tile_map.1) | copy-start | bytes 786436
  25.8 1.5 %collective-permute-start.4 = (f32[8,64,128]{2,1,0:T(8,128)S(1)}, f32[8,64,128]{2,1,0:T(8,128)S(1)}, u32[]{:S(2)}, u32[]{:S(2)}) collective-permute-start(f32[8,64,128]{2,1,0:T(8,128)S(1)} %all-to-all-done.mine), channel_id=1, source_target_pairs={{0,1},{1,0},{2,3},{3,2},{4,5},{5,4},{6,7},{7,6},{8,9},{9,8},{10,11... | collective-permute-start | bytes 786440 | tf_op jit(solution)/shard_map/ppermute | solution.py:351
  57.9 3.6 %collective-permute-start.5 = (f32[8,32,128]{2,1,0:T(8,128)S(1)}, f32[8,32,128]{2,1,0:T(8,128)S(1)}, u32[]{:S(2)}, u32[]{:S(2)}) collective-permute-start(f32[8,32,128]{2,1,0:T(8,128)S(1)} %all_to_all.26.gathered), channel_id=1, source_target_pairs={{0,1},{1,0},{2,3},{3,2},{4,5},{5,4},{6,7},{7,6},{8,9},{9,8},{10,11... | collective-permute-start | bytes 393224 | tf_op jit(solution)/shard_map/ppermute | solution.py:351
  73.6 2.4 %collective-permute-start.6 = (f32[8,128]{1,0:T(8,128)S(1)}, f32[8,128]{1,0:T(8,128)S(1)}, u32[]{:S(2)}, u32[]{:S(2)}) collective-permute-start(f32[8,128]{1,0:T(8,128)S(1)} %get-tuple-element.38.sums), channel_id=1, source_target_pairs={{0,1},{1,0},{2,3},{3,2},{4,5},{5,4},{6,7},{7,6},{8,9},{9,8},{10,11... | collective-permute-start | bytes 12296 | tf_op jit(solution)/shard_map/ppermute | solution.py:351

commit v8 on v7

--- a/solution.py
+++ b/solution.py
@@ -14,7 +14,6 @@
 SUMS = 8
 SITE = 120
 SUM_ROW = 104
-CELL_ROW = 16
 WIDE = GROUP * ATOMS
 NARROW = HALF * ATOMS
 CHUNK = 256
@@ -53,26 +52,15 @@
     return jnp.where(first, of_first, jnp.where(second, of_second, jnp.where(third, of_third, 1.0)))
 
 
-def block_sites(block, pack, jitter_row):
-    index = lax.broadcasted_iota(jnp.int32, (SUMS, LANES), 0) * LANES + lane_ids(SUMS)
-    found = jnp.where(index == block, pack[CELL_ROW : CELL_ROW + SUMS, :], 0.0)
-    cell = jnp.sum(jnp.sum(found, axis=0, keepdims=True), axis=1, keepdims=True).astype(jnp.int32)
-    comp = lax.broadcasted_iota(jnp.int32, (SUMS, LANES), 0)
-    return lattice(comp, lane_ids(SUMS), cell) + pack[jitter_row : jitter_row + SUMS, :]
-
-
-def prepare_kernel(ids, pack, field, partner, vec_out, own_out, work, wide):
+def prepare_kernel(ids, jitter, across, beside, corner, field, partner, vec_out, own_out, work, wide):
     work[...] = jnp.zeros_like(work)
-    block = ids[0] * GROUP + ids[1]
     core = ids[1] % 2
-    comp = lax.broadcasted_iota(jnp.int32, (SUMS, LANES), 0)
-    for flip, vectors in ((0, field), (1, partner)):
-        near = block_sites(block ^ flip, pack, flip * SUMS)
-        beside = block_sites(block ^ flip ^ GROUP, pack, (3 + flip) * SUMS)
-        work[SITE : SITE + SUMS, :] = jnp.where(comp < 4, near, pltpu.roll(beside, 4, 0))
+    for flip, near, far, vectors in ((0, jitter, beside, field), (1, across, corner, partner)):
+        work[SITE : SITE + COMPS, 0:ATOMS] = near[:, 0:ATOMS]
+        work[SITE + 4 : SITE + 4 + COMPS, 0:ATOMS] = far[...]
         wide[...] = work[...].T[0:ATOMS, :]
         for part in range(COMPS):
-            wide[:, part * RHS : (part + 1) * RHS] = vectors[part]
+            wide[:, part * RHS : (part + 1) * RHS] = vectors[part, :, 0:RHS]
         turned = wide[...]
         if flip == 0:
             own_out[...] = turned
@@ -81,7 +69,7 @@
             vec_out[slot, rows, :] = turned
 
 
-def pick_kernel(ids, mine, theirs, own, other, column):
+def pick_kernel(ids, points, mine, theirs, own, other, column):
     core = ids[1] % 2
     side = ids[0] % 2
     here = pl.ds(pl.multiple_of(core * ATOMS, ATOMS), ATOMS)
@@ -96,7 +84,7 @@
                 place = pl.ds(pl.multiple_of((2 * slot + (side ^ flip)) * ATOMS, ATOMS), ATOMS)
                 for comp in range(COMPS):
                     lane = SITE + 4 * flip + comp
-                    column[comp, place, :] = jnp.broadcast_to(rows[:, lane : lane + 1], (ATOMS, LANES))
+                    column[comp, place, :] = points[comp, place, :] + rows[:, lane : lane + 1]
 
     @pl.when(core == 0)
     def _():
@@ -108,12 +96,16 @@
 
 
 def lattice(comp, atom, cell):
+    if isinstance(comp, int):
+        inner = (atom >> 3, (atom >> 1) & 3, atom & 1)[comp]
+        corner = ((cell >> 5) * 4, ((cell >> 2) & 7) * 4, (cell & 3) * 2)[comp]
+        return (corner + inner).astype(F32) * SPACING
     inner = jnp.where(comp == 0, atom >> 3, jnp.where(comp == 1, (atom >> 1) & 3, atom & 1))
     corner = jnp.where(comp == 0, (cell >> 5) * 4, jnp.where(comp == 1, ((cell >> 2) & 7) * 4, (cell & 3) * 2))
     return (corner + inner).astype(F32) * SPACING
 
 
-def side_kernel(ids, species, tile_map, aux_out, mask_out, work):
+def side_kernel(ids, species, cells, tile_map, aux_out, mask_out, points, across, work):
     alpha = species[4:SUMS, :]
     lane = lax.broadcasted_iota(jnp.int32, (4, LANES), 1)
     rhs_lane = jnp.where(lane >= 2 * RHS, lane - 2 * RHS, jnp.where(lane >= RHS, lane - RHS, lane))
@@ -146,6 +138,18 @@
     spread = jnp.where(place == wanted, 1.0, 0.0).astype(BF16)
     mask_out[...] = 0.5 * jnp.dot(lines, spread, preferred_element_type=F32)
 
+    cell = jnp.dot(cells[...].astype(BF16), spread, preferred_element_type=F32)[0:1, :].astype(jnp.int32)
+    comp = lax.broadcasted_iota(jnp.int32, (SUMS, WIDE), 0)
+    atom = lax.broadcasted_iota(jnp.int32, (SUMS, WIDE), 1) & (ATOMS - 1)
+    across[...] = lattice(comp, atom, cell)
+    place = lax.broadcasted_iota(jnp.int32, (WIDE, blocks), 1)
+    row = lax.broadcasted_iota(jnp.int32, (WIDE, blocks), 0)
+    wanted = (row // ATOMS) * GROUP + ids[1]
+    cell = jnp.sum(jnp.where(place == wanted, cells[0:1, :], 0.0), axis=1, keepdims=True).astype(jnp.int32)
+    atom = lax.broadcasted_iota(jnp.int32, (WIDE, LANES), 0) & (ATOMS - 1)
+    for comp in range(COMPS):
+        points[comp] = lattice(comp, atom, cell)
+
 
 def right_side(vectors, side):
     first, second, third = component_lanes(NARROW)
@@ -174,8 +178,8 @@
     return both[:, 0:LANES] + (both[:, LANES:] + rest)
 
 
-def build_and_apply(mask, vectors, column, high, low, side, first_lane):
-    across = vectors.T[SITE : SITE + SUMS, :]
+def build_and_apply(mask, vectors, column, points, high, low, side, first_lane):
+    across = vectors.T[SITE : SITE + SUMS, :] + points[:, first_lane : first_lane + NARROW]
     across_x, across_y, across_z = across[0:1, :], across[1:2, :], across[2:3, :]
 
     def rows16(step):
@@ -222,16 +226,16 @@
     return jnp.concatenate(outs, axis=0)
 
 
-def first_own_kernel(mask, column, gathered, total, high, low, side):
+def first_own_kernel(mask, column, points, gathered, total, high, low, side):
     vectors = gathered[...].reshape(NARROW, LANES)
     right_side(vectors, side)
-    total[...] = build_and_apply(mask, vectors, column, high, low, side, 0)
-
-
-def first_other_kernel(mask, column, gathered, total, part_out, high, low, side):
+    total[...] = build_and_apply(mask, vectors, column, points, high, low, side, 0)
+
+
+def first_other_kernel(mask, column, points, gathered, total, part_out, high, low, side):
     vectors = gathered[...].reshape(NARROW, LANES)
     right_side(vectors, side)
-    out = build_and_apply(mask, vectors, column, high, low, side, NARROW)
+    out = build_and_apply(mask, vectors, column, points, high, low, side, NARROW)
     part_out[...] = (total[...] + out).reshape(GROUP, ATOMS, LANES)
 
 
@@ -372,10 +376,9 @@
     ids = jnp.stack([me // GROUP, me % GROUP]).astype(jnp.int32)
     field = external_field.transpose(0, 2, 1)
     across_field = core_swap(field)
-    shifts = [jitter] + [trade(jitter, bits) for bits in (1, GROUP, GROUP + 1)]
-    shifts = [jnp.pad(shift, ((0, SUMS - COMPS), (0, LANES - ATOMS))) for shift in shifts]
-    cells = jnp.pad(block_cell.astype(F32).reshape(2, LANES), ((0, 6), (0, 0)))
-    pack = jnp.concatenate(shifts[:2] + [cells] + shifts[2:])
+    shifts = [jnp.pad(jitter, ((0, 0), (0, LANES - ATOMS)))]
+    shifts = shifts + [trade(jitter, bits) for bits in (1, GROUP, GROUP + 1)]
+    cells = jnp.pad(block_cell.astype(F32)[None], ((0, SUMS - 1), (0, 0)))
     kinds = jnp.concatenate(
         [
             jnp.pad(species.astype(F32)[None], ((0, 3), (0, LANES - ATOMS))),
@@ -385,51 +388,54 @@
     vec, vector = pl.pallas_call(
         prepare_kernel,
         out_shape=(shape(HALF, 2 * ATOMS, LANES), shape(ATOMS, LANES)),
-        in_specs=[SMEM, VMEM, VMEM, VMEM],
+        in_specs=[SMEM] + [VMEM] * 6,
         out_specs=(VMEM, VMEM),
         scratch_shapes=[SQUARE, pltpu.VMEM((ATOMS, LANES), F32)],
         compiler_params=PARAMS,
         name="prepare",
-    )(ids, pack, field, across_field)
-    aux, mask = pl.pallas_call(
+    )(ids, *shifts, jnp.pad(field, ((0, 0), (0, 0), (0, LANES - RHS))), across_field)
+    column_shape = shape(COMPS, WIDE, LANES)
+    aux, mask, points, across = pl.pallas_call(
         side_kernel,
-        out_shape=(shape(ATOMS + SUMS, LANES), shape(GROUP, WIDE)),
-        in_specs=[SMEM, VMEM, VMEM],
-        out_specs=(VMEM, VMEM),
+        out_shape=(shape(ATOMS + SUMS, LANES), shape(GROUP, WIDE), column_shape, shape(SUMS, WIDE)),
+        in_specs=[SMEM, VMEM, VMEM, VMEM],
+        out_specs=(VMEM, VMEM, VMEM, VMEM),
         scratch_shapes=[SQUARE],
         compiler_params=PARAMS,
         name="side",
-    )(ids, kinds, tile_map)
-    mine, aux, mask = lax.optimization_barrier((exchange(vec, MIXED), aux, mask))
+    )(ids, kinds, cells, tile_map)
+    mine, aux, mask, points, across = lax.optimization_barrier(
+        (exchange(vec, MIXED), aux, mask, points, across)
+    )
     half = shape(HALF, ATOMS, LANES)
     own, other, column = pl.pallas_call(
         pick_kernel,
-        out_shape=(half, half, shape(COMPS, WIDE, LANES)),
-        in_specs=[SMEM, VMEM, VMEM],
+        out_shape=(half, half, column_shape),
+        in_specs=[SMEM, VMEM, VMEM, VMEM],
         out_specs=(VMEM, VMEM, VMEM),
         compiler_params=PARAMS,
         name="pick",
-    )(ids, mine, core_swap(mine))
+    )(ids, points, mine, core_swap(mine))
     side = pltpu.VMEM((PAIRS * NARROW, 2 * LANES), BF16)
     tile = shape(WIDE, PAIRS * NARROW, dtype=BF16)
     total, high0, low0 = pl.pallas_call(
         first_own_kernel,
         out_shape=(shape(WIDE, LANES), tile, tile),
-        in_specs=[VMEM] * 3,
+        in_specs=[VMEM] * 4,
         out_specs=(VMEM, VMEM, VMEM),
         scratch_shapes=[side],
         compiler_params=PARAMS,
         name="first_own",
-    )(mask, column, own)
+    )(mask, column, across, own)
     part, high1, low1 = pl.pallas_call(
         first_other_kernel,
         out_shape=(shape(GROUP, ATOMS, LANES), tile, tile),
-        in_specs=[VMEM] * 4,
+        in_specs=[VMEM] * 5,
         out_specs=(VMEM, VMEM, VMEM),
         scratch_shapes=[side],
         compiler_params=PARAMS,
         name="first_other",
-    )(mask, column, other, total)
+    )(mask, column, across, other, total)
     parts = exchange(part, ROWS)
     blocks = whole(GROUP, ATOMS, LANES)
     block = whole(1, ATOMS, LANES)

time: 93.4 us -> 92.5 us (level)
    pad x0 -> x3, local copies, waits for them, and re-layouts: none -> 1.5 us  [the longest x1 0.8 us: local(): jnp.pad(field, ((0, 0), (0, 0), (0, LANES - RHS)))]
    unnamed x8 -> x2, local copies, waits for them, and re-layouts: 2.44 us -> 0.95 us
  transfers between devices with their start and end apart: 8 -> 8, of which waited for: 4 -> 4; matrix products, arithmetic and copies ran while one was open for 3% -> 4% of each run, Pallas kernels for 2% -> 2%
where the time goes in v8:
time: 92.5 us; the launch traced here: 92 us
  blocking collectives  52.9 us (57%)
  starting transfers between devices  16.2 us (18%)
  Pallas kernels  9.77 us (11%)
  waiting for transfers between devices  7.86 us (8%)
  local copies, waits for them, and re-layouts  2.45 us (3%)
  other arithmetic  2.1 us (2%)
    all_to_all x4, blocking collectives, exchange(): return lax.all_to_all(value, 'device', 0, 0, axis_index_groups=groups)  52.9 us
    ppermute x7, starting transfers between devices, trade(): lax.ppermute(value, 'device', [(here, here ^ bits) for here in range(GROU...  9.69 us
    all_to_all x1, starting transfers between devices, exchange(): return lax.all_to_all(value, 'device', 0, 0, axis_index_groups=groups)  6.53 us
    all_to_all x1, waiting for transfers between devices, exchange(): return lax.all_to_all(value, 'device', 0, 0, axis_index_groups=groups)  5.39 us
    ppermute x7, waiting for transfers between devices, trade(): lax.ppermute(value, 'device', [(here, here ^ bits) for here in range(GROU...  2.47 us
  transfers between devices with their start and end apart: 8, of which 4 were waited for; matrix products, arithmetic and copies ran while one was open for 4% of the time, Pallas kernels for 2%

profile of v8, /device:TPU:1, one launch (start us, length us, event | category | flops | bytes accessed | tf_op | source)
XLA Modules:
  0.0 92.0 jit_solution(2893864435778906419)
XLA Ops:
  0.6 3.3 %collective-permute-start = (f32[3,32]{1,0:T(4,128)}, f32[3,32]{1,0:T(4,128)S(1)}, u32[]{:S(2)}, u32[]{:S(2)}) collective-permute-start(f32[3,32]{1,0:T(4,128)} %param.7), channel_id=1, source_target_pairs={{0,1},{1,0},{2,3},{3,2},{4,5},{5,4},{6,7},{7,6},{8,9},{9,8},{10,11... | collective-permute-start | bytes 1160 | tf_op jit(solution)/shard_map/ppermute | solution.py:355
  4.0 0.0 collective-permute-start.2
  4.0 1.5 %collective-permute-start.1 = (f32[3,32]{1,0:T(4,128)}, f32[3,32]{1,0:T(4,128)S(1)}, u32[]{:S(2)}, u32[]{:S(2)}) collective-permute-start(f32[3,32]{1,0:T(4,128)} %param.7), channel_id=1, source_target_pairs={{0,16},{1,17},{2,18},{3,19},{4,20},{5,21},{6,22},{7,23},{8,24},{9,... | collective-permute-start | bytes 1160 | tf_op jit(solution)/shard_map/ppermute | solution.py:355
  5.4 0.7 collective-permute-start.3
  6.1 0.1 pad_add_fusion.ids
  6.2 0.7 pad.20.jitter
  6.9 0.8 pad.21.field
  7.7 1.4 %prepare.1 = (f32[8,64,128]{2,1,0:T(8,128)}, f32[32,128]{1,0:T(8,128)S(1)}) custom-call(s32[2]{0:T(128)S(1)} %pad_add_fusion.ids, f32[3,128]{1,0:T(4,128)S(1)} %pad.20.jitter, f32[3,32]{1,0:T(4,128)S(1)} %collective-permute-done.across, f32[3,32]{1,0:T(4,128)S(1)} %collective-permute-done.1.beside, f32[3,32]{1,0:T(4,128)S(1)} %collective-permute-done.2.corner, ...), custom_call_target="tpu_custom_call" | custom-call | tf_op jit(solution)/shard_map/prepare/pallas_call | solution.py:388
  9.1 6.5 %all-to-all-start = ((f32[8,64,128]{2,1,0:T(8,128)}), f32[8,64,128]{2,1,0:T(8,128)S(1)}, u32[]{:S(2)}, u32[]{:S(2)}) async-start(f32[8,64,128]{2,1,0:T(8,128)} %get-tuple-element.26), calls=%async_computation | async-start | bytes 524288 | tf_op jit(solution)/shard_map/all_to_all | solution.py:363
  15.6 0.7 convert_element_type.17
  16.3 0.7 convert_bitcast_fusion
  17.0 0.7 select_maximum_fusion.species
  17.7 0.9 %copy-done = s32[256,256]{1,0:T(8,128)S(1)} copy-done((s32[256,256]{1,0:T(8,128)S(1)}, s32[256,256]{1,0:T(8,128)}, u32[]{:S(2)}) %copy-start) | copy-done | bytes 262168
  18.6 1.0 %side.1 = (f32[40,128]{1,0:T(8,128)S(1)}, f32[16,512]{1,0:T(8,128)S(1)}, f32[3,512,128]{2,1,0:T(8,128)S(1)}, f32[8,512]{1,0:T(8,128)S(1)}) custom-call(s32[2]{0:T(128)S(1)} %pad_add_fusion.ids, f32[8,128]{1,0:T(8,128)S(1)} %select_maximum_fusion.species, f32[8,256]{1,0:T(8,128)S(1)} %pad.24.cells, s32[256,256]{1,0:T(8,128)S(1)} %copy-done), custom_call_target="tpu_custom_call" | custom-call | tf_op jit(solution)/shard_map/side/pallas_call | solution.py:398
  19.6 5.4 %all-to-all-done.mine = f32[8,64,128]{2,1,0:T(8,128)S(1)} async-done(((f32[8,64,128]{2,1,0:T(8,128)}), f32[8,64,128]{2,1,0:T(8,128)S(1)}, u32[]{:S(2)}, u32[]{:S(2)}) %all-to-all-start) | async-done | bytes 262176 | tf_op jit(solution)/shard_map/all_to_all | solution.py:363
  25.0 1.5 %collective-permute-done.4.theirs = f32[8,64,128]{2,1,0:T(8,128)S(1)} collective-permute-done((f32[8,64,128]{2,1,0:T(8,128)S(1)}, f32[8,64,128]{2,1,0:T(8,128)S(1)}, u32[]{:S(2)}, u32[]{:S(2)}) %collective-permute-start.4) | collective-permute-done | bytes 262176 | tf_op jit(solution)/shard_map/ppermute | solution.py:355
  26.5 0.9 pick.1
  27.4 1.7 %first_own.1 = (f32[512,128]{1,0:T(8,128)S(1)}, bf16[512,1280]{1,0:T(8,128)(2,1)S(1)}, bf16[512,1280]{1,0:T(8,128)(2,1)S(1)}) custom-call(f32[16,512]{1,0:T(8,128)S(1)} %get-tuple-element.31.mask, f32[3,512,128]{2,1,0:T(8,128)S(1)} %get-tuple-element.34.column, f32[8,512]{1,0:T(8,128)S(1)} %get-tuple-element.35.points, ...), custom_call_target="tpu_custom_call" | custom-call | tf_op jit(solution)/shard_map/first_own/pallas_call | solution.py:421
  29.1 1.7 %first_other.1 = (f32[16,32,128]{2,1,0:T(8,128)S(1)}, bf16[512,1280]{1,0:T(8,128)(2,1)S(1)}, bf16[512,1280]{1,0:T(8,128)(2,1)S(1)}) custom-call(f32[16,512]{1,0:T(8,128)S(1)} %get-tuple-element.31.mask, f32[3,512,128]{2,1,0:T(8,128)S(1)} %get-tuple-element.34.column, f32[8,512]{1,0:T(8,128)S(1)} %get-tuple-element.35.points, ...), custom_call_target="tpu_custom_call" | custom-call | tf_op jit(solution)/shard_map/first_other/pallas_call | solution.py:430
  30.9 14.8 %all_to_all.25.parts = f32[16,32,128]{2,1,0:T(8,128)S(1)} all-to-all(f32[16,32,128]{2,1,0:T(8,128)S(1)} %get-tuple-element.39), channel_id=1, replica_groups={{0,16,32,48,64,80,96,112,128,144,160,176,192,208,224,240},{1,17,33,49,6..., dimensions={0} | all-to-all | bytes 524288 | tf_op jit(solution)/shard_map/all_to_all | solution.py:363
  45.7 0.2 shifted.1
  45.9 11.2 %all_to_all.26.gathered = f32[8,32,128]{2,1,0:T(8,128)S(1)} all-to-all(f32[8,32,128]{2,1,0:T(8,128)S(1)} %shifted.1), channel_id=1, replica_groups={{0,2,4,6,8,10,12,14},{1,3,5,7,9,11,13,15},{16,18,20,22,24,26,28,30},{17..., dimensions={0} | all-to-all | bytes 262144 | tf_op jit(solution)/shard_map/all_to_all | solution.py:363
  57.1 2.6 %collective-permute-start.5 = (f32[8,32,128]{2,1,0:T(8,128)S(1)}, f32[8,32,128]{2,1,0:T(8,128)S(1)}, u32[]{:S(2)}, u32[]{:S(2)}) collective-permute-start(f32[8,32,128]{2,1,0:T(8,128)S(1)} %all_to_all.26.gathered), channel_id=1, source_target_pairs={{0,1},{1,0},{2,3},{3,2},{4,5},{5,4},{6,7},{7,6},{8,9},{9,8},{10,11... | collective-permute-start | bytes 393224 | tf_op jit(solution)/shard_map/ppermute | solution.py:355
  59.8 0.9 second_own.1.total
  60.6 0.1 collective-permute-done.5.gathered
  60.7 0.9 second_other.1
  61.6 10.8 %all_to_all.27.parts = f32[16,32,128]{2,1,0:T(8,128)S(1)} all-to-all(f32[16,32,128]{2,1,0:T(8,128)S(1)} %second_other.1), channel_id=1, replica_groups={{0,16,32,48,64,80,96,112,128,144,160,176,192,208,224,240},{1,17,33,49,6..., dimensions={0} | all-to-all | bytes 524288 | tf_op jit(solution)/shard_map/all_to_all | solution.py:363
  72.4 0.4 step.1
  72.7 1.6 %collective-permute-start.6 = (f32[8,128]{1,0:T(8,128)S(1)}, f32[8,128]{1,0:T(8,128)S(1)}, u32[]{:S(2)}, u32[]{:S(2)}) collective-permute-start(f32[8,128]{1,0:T(8,128)S(1)} %get-tuple-element.46.sums), channel_id=1, source_target_pairs={{0,1},{1,0},{2,3},{3,2},{4,5},{5,4},{6,7},{7,6},{8,9},{9,8},{10,11... | collective-permute-start | bytes 12296 | tf_op jit(solution)/shard_map/ppermute | solution.py:355
  74.3 0.8 collective-permute-done.6.swapped
  75.1 16.1 %all_to_all.28 = f32[128,1,128]{2,1,0:T(1,128)S(1)} all-to-all(f32[128,1,128]{2,1,0:T(1,128)S(1)} %bitcast.14), channel_id=1, replica_groups={{0,2,4,6,8,10,12,14,16,18,20,22,24,26,28,30,32,34,36,38,40,42,44,46,48,..., dimensions={0} | all-to-all | bytes 131072 | tf_op jit(solution)/shard_map/all_to_all | solution.py:363
  91.2 0.8 finish.1
  (8 shorter events, 0.0 us)
Async XLA Ops:
  0.6 7.1 %collective-permute-start = (f32[3,32]{1,0:T(4,128)}, f32[3,32]{1,0:T(4,128)S(1)}, u32[]{:S(2)}, u32[]{:S(2)}) collective-permute-start(f32[3,32]{1,0:T(4,128)} %param.7), channel_id=1, source_target_pairs={{0,1},{1,0},{2,3},{3,2},{4,5},{5,4},{6,7},{7,6},{8,9},{9,8},{10,11... | collective-permute-start | bytes 1160 | tf_op jit(solution)/shard_map/ppermute | solution.py:355
  4.0 3.7 %collective-permute-start.2 = (f32[3,32]{1,0:T(4,128)}, f32[3,32]{1,0:T(4,128)S(1)}, u32[]{:S(2)}, u32[]{:S(2)}) collective-permute-start(f32[3,32]{1,0:T(4,128)} %param.7), channel_id=1, source_target_pairs={{0,17},{1,16},{2,19},{3,18},{4,21},{5,20},{6,23},{7,22},{8,25},{9,... | collective-permute-start | bytes 1160 | tf_op jit(solution)/shard_map/ppermute | solution.py:355
  4.0 3.7 %collective-permute-start.1 = (f32[3,32]{1,0:T(4,128)}, f32[3,32]{1,0:T(4,128)S(1)}, u32[]{:S(2)}, u32[]{:S(2)}) collective-permute-start(f32[3,32]{1,0:T(4,128)} %param.7), channel_id=1, source_target_pairs={{0,16},{1,17},{2,18},{3,19},{4,20},{5,21},{6,22},{7,23},{8,24},{9,... | collective-permute-start | bytes 1160 | tf_op jit(solution)/shard_map/ppermute | solution.py:355
  5.4 2.3 %collective-permute-start.3 = (f32[3,32,36]{2,1,0:T(8,128)}, f32[3,32,36]{2,1,0:T(8,128)S(1)}, u32[]{:S(2)}, u32[]{:S(2)}) collective-permute-start(f32[3,32,36]{2,1,0:T(8,128)} %bitcast.15), channel_id=1, source_target_pairs={{0,1},{1,0},{2,3},{3,2},{4,5},{5,4},{6,7},{7,6},{8,9},{9,8},{10,11... | collective-permute-start | bytes 41480 | tf_op jit(solution)/shard_map/ppermute | solution.py:355
  9.1 15.9 %all-to-all-start = ((f32[8,64,128]{2,1,0:T(8,128)}), f32[8,64,128]{2,1,0:T(8,128)S(1)}, u32[]{:S(2)}, u32[]{:S(2)}) async-start(f32[8,64,128]{2,1,0:T(8,128)} %get-tuple-element.26), calls=%async_computation | async-start | bytes 524288 | tf_op jit(solution)/shard_map/all_to_all | solution.py:363
  17.7 0.9 %copy-start = (s32[256,256]{1,0:T(8,128)S(1)}, s32[256,256]{1,0:T(8,128)}, u32[]{:S(2)}) copy-start(s32[256,256]{1,0:T(8,128)} %tile_map.1) | copy-start | bytes 786436
  25.0 1.5 %collective-permute-start.4 = (f32[8,64,128]{2,1,0:T(8,128)S(1)}, f32[8,64,128]{2,1,0:T(8,128)S(1)}, u32[]{:S(2)}, u32[]{:S(2)}) collective-permute-start(f32[8,64,128]{2,1,0:T(8,128)S(1)} %all-to-all-done.mine), channel_id=1, source_target_pairs={{0,1},{1,0},{2,3},{3,2},{4,5},{5,4},{6,7},{7,6},{8,9},{9,8},{10,11... | collective-permute-start | bytes 786440 | tf_op jit(solution)/shard_map/ppermute | solution.py:355
  57.1 3.6 %collective-permute-start.5 = (f32[8,32,128]{2,1,0:T(8,128)S(1)}, f32[8,32,128]{2,1,0:T(8,128)S(1)}, u32[]{:S(2)}, u32[]{:S(2)}) collective-permute-start(f32[8,32,128]{2,1,0:T(8,128)S(1)} %all_to_all.26.gathered), channel_id=1, source_target_pairs={{0,1},{1,0},{2,3},{3,2},{4,5},{5,4},{6,7},{7,6},{8,9},{9,8},{10,11... | collective-permute-start | bytes 393224 | tf_op jit(solution)/shard_map/ppermute | solution.py:355
  72.7 2.4 %collective-permute-start.6 = (f32[8,128]{1,0:T(8,128)S(1)}, f32[8,128]{1,0:T(8,128)S(1)}, u32[]{:S(2)}, u32[]{:S(2)}) collective-permute-start(f32[8,128]{1,0:T(8,128)S(1)} %get-tuple-element.46.sums), channel_id=1, source_target_pairs={{0,1},{1,0},{2,3},{3,2},{4,5},{5,4},{6,7},{7,6},{8,9},{9,8},{10,11... | collective-permute-start | bytes 12296 | tf_op jit(solution)/shard_map/ppermute | solution.py:355

commit v9 on v8

--- a/solution.py
+++ b/solution.py
@@ -52,9 +52,8 @@
     return jnp.where(first, of_first, jnp.where(second, of_second, jnp.where(third, of_third, 1.0)))
 
 
-def prepare_kernel(ids, jitter, across, beside, corner, field, partner, vec_out, own_out, work, wide):
+def prepare_kernel(jitter, across, beside, corner, field, partner, vec_out, own_out, work, wide):
     work[...] = jnp.zeros_like(work)
-    core = ids[1] % 2
     for flip, near, far, vectors in ((0, jitter, beside, field), (1, across, corner, partner)):
         work[SITE : SITE + COMPS, 0:ATOMS] = near[:, 0:ATOMS]
         work[SITE + 4 : SITE + 4 + COMPS, 0:ATOMS] = far[...]
@@ -64,35 +63,27 @@
         turned = wide[...]
         if flip == 0:
             own_out[...] = turned
-        rows = pl.ds(pl.multiple_of((core ^ flip) * ATOMS, ATOMS), ATOMS)
         for slot in range(HALF):
-            vec_out[slot, rows, :] = turned
-
-
-def pick_kernel(ids, points, mine, theirs, own, other, column):
-    core = ids[1] % 2
-    side = ids[0] % 2
-    here = pl.ds(pl.multiple_of(core * ATOMS, ATOMS), ATOMS)
-    there = pl.ds(pl.multiple_of((1 - core) * ATOMS, ATOMS), ATOMS)
-
-    def take(along_z, along_row):
-        own[...] = along_z[:, here, :]
-        other[...] = along_z[:, there, :]
-        for slot in range(HALF):
-            rows = along_row[slot, here, :]
-            for flip in range(2):
-                place = pl.ds(pl.multiple_of((2 * slot + (side ^ flip)) * ATOMS, ATOMS), ATOMS)
-                for comp in range(COMPS):
-                    lane = SITE + 4 * flip + comp
-                    column[comp, place, :] = points[comp, place, :] + rows[:, lane : lane + 1]
-
-    @pl.when(core == 0)
-    def _():
-        take(theirs, mine)
-
-    @pl.when(core == 1)
-    def _():
-        take(mine, theirs)
+            vec_out[slot, flip * ATOMS : (flip + 1) * ATOMS, :] = turned
+
+
+def pick_kernel(flags, points, mine, theirs, own, other, column):
+    odd_core = flags[0:ATOMS, :] > 0.5
+    odd_row = flags[ATOMS : 2 * ATOMS, :] > 0.5
+    for slot in range(HALF):
+        first, second = mine[slot, 0:ATOMS, :], mine[slot, ATOMS : 2 * ATOMS, :]
+        third, fourth = theirs[slot, 0:ATOMS, :], theirs[slot, ATOMS : 2 * ATOMS, :]
+        own[slot] = jnp.where(odd_core, first, fourth)
+        other[slot] = jnp.where(odd_core, second, third)
+        rows = jnp.where(odd_core, fourth, first)
+        beside = pltpu.roll(rows, LANES - 4, 1)
+        for block, sites in (
+            (2 * slot, jnp.where(odd_row, beside, rows)),
+            (2 * slot + 1, jnp.where(odd_row, rows, beside)),
+        ):
+            place = slice(block * ATOMS, (block + 1) * ATOMS)
+            for comp in range(COMPS):
+                column[comp, place, :] = points[comp, place, :] + sites[:, SITE + comp : SITE + comp + 1]
 
 
 def lattice(comp, atom, cell):
@@ -105,7 +96,7 @@
     return (corner + inner).astype(F32) * SPACING
 
 
-def side_kernel(ids, species, cells, tile_map, aux_out, mask_out, points, across, work):
+def side_kernel(ids, species, cells, tile_map, aux_out, mask_out, points, across, flags, work):
     alpha = species[4:SUMS, :]
     lane = lax.broadcasted_iota(jnp.int32, (4, LANES), 1)
     rhs_lane = jnp.where(lane >= 2 * RHS, lane - 2 * RHS, jnp.where(lane >= RHS, lane - RHS, lane))
@@ -149,6 +140,8 @@
     atom = lax.broadcasted_iota(jnp.int32, (WIDE, LANES), 0) & (ATOMS - 1)
     for comp in range(COMPS):
         points[comp] = lattice(comp, atom, cell)
+    flags[0:ATOMS, :] = jnp.full((ATOMS, LANES), ids[1] % 2, jnp.int32).astype(F32)
+    flags[ATOMS : 2 * ATOMS, :] = jnp.full((ATOMS, LANES), ids[0] % 2, jnp.int32).astype(F32)
 
 
 def right_side(vectors, side):
@@ -388,34 +381,34 @@
     vec, vector = pl.pallas_call(
         prepare_kernel,
         out_shape=(shape(HALF, 2 * ATOMS, LANES), shape(ATOMS, LANES)),
-        in_specs=[SMEM] + [VMEM] * 6,
+        in_specs=[VMEM] * 6,
         out_specs=(VMEM, VMEM),
         scratch_shapes=[SQUARE, pltpu.VMEM((ATOMS, LANES), F32)],
         compiler_params=PARAMS,
         name="prepare",
-    )(ids, *shifts, jnp.pad(field, ((0, 0), (0, 0), (0, LANES - RHS))), across_field)
+    )(*shifts, jnp.pad(field, ((0, 0), (0, 0), (0, LANES - RHS))), across_field)
     column_shape = shape(COMPS, WIDE, LANES)
-    aux, mask, points, across = pl.pallas_call(
+    aux, mask, points, across, flags = pl.pallas_call(
         side_kernel,
-        out_shape=(shape(ATOMS + SUMS, LANES), shape(GROUP, WIDE), column_shape, shape(SUMS, WIDE)),
+        out_shape=(shape(ATOMS + SUMS, LANES), shape(GROUP, WIDE), column_shape, shape(SUMS, WIDE), shape(2 * ATOMS, LANES)),
         in_specs=[SMEM, VMEM, VMEM, VMEM],
-        out_specs=(VMEM, VMEM, VMEM, VMEM),
+        out_specs=(VMEM,) * 5,
         scratch_shapes=[SQUARE],
         compiler_params=PARAMS,
         name="side",
     )(ids, kinds, cells, tile_map)
-    mine, aux, mask, points, across = lax.optimization_barrier(
-        (exchange(vec, MIXED), aux, mask, points, across)
+    mine, aux, mask, points, across, flags = lax.optimization_barrier(
+        (exchange(vec, MIXED), aux, mask, points, across, flags)
     )
     half = shape(HALF, ATOMS, LANES)
     own, other, column = pl.pallas_call(
         pick_kernel,
         out_shape=(half, half, column_shape),
-        in_specs=[SMEM, VMEM, VMEM, VMEM],
+        in_specs=[VMEM, VMEM, VMEM, VMEM],
         out_specs=(VMEM, VMEM, VMEM),
         compiler_params=PARAMS,
         name="pick",
-    )(ids, points, mine, core_swap(mine))
+    )(flags, points, mine, core_swap(mine))
     side = pltpu.VMEM((PAIRS * NARROW, 2 * LANES), BF16)
     tile = shape(WIDE, PAIRS * NARROW, dtype=BF16)
     total, high0, low0 = pl.pallas_call(

time: 92.5 us -> 92.1 us (level)
  no operation moved by 1% of the time
where the time goes in v9:
time: 92.1 us; the launch traced here: 91.6 us
  blocking collectives  52.5 us (57%)
  starting transfers between devices  16.7 us (18%)
  Pallas kernels  9.23 us (10%)
  waiting for transfers between devices  7.78 us (8%)
  local copies, waits for them, and re-layouts  2.48 us (3%)
  other arithmetic  2.1 us (2%)
    all_to_all x4, blocking collectives, exchange(): return lax.all_to_all(value, 'device', 0, 0, axis_index_groups=groups)  52.5 us
    ppermute x7, starting transfers between devices, trade(): lax.ppermute(value, 'device', [(here, here ^ bits) for here in range(GROU...  9.41 us
    all_to_all x1, starting transfers between devices, exchange(): return lax.all_to_all(value, 'device', 0, 0, axis_index_groups=groups)  7.28 us
    all_to_all x1, waiting for transfers between devices, exchange(): return lax.all_to_all(value, 'device', 0, 0, axis_index_groups=groups)  5.31 us
    ppermute x7, waiting for transfers between devices, trade(): lax.ppermute(value, 'device', [(here, here ^ bits) for here in range(GROU...  2.47 us
  transfers between devices with their start and end apart: 8, of which 4 were waited for; matrix products, arithmetic and copies ran while one was open for 4% of the time, Pallas kernels for 2%

profile of v9, /device:TPU:1, one launch (start us, length us, event | category | flops | bytes accessed | tf_op | source)
XLA Modules:
  0.0 91.6 jit_solution(6789721886426410570)
XLA Ops:
  0.6 3.3 %collective-permute-start.3 = (f32[3,32,36]{2,1,0:T(8,128)}, f32[3,32,36]{2,1,0:T(8,128)S(1)}, u32[]{:S(2)}, u32[]{:S(2)}) collective-permute-start(f32[3,32,36]{2,1,0:T(8,128)} %bitcast.15), channel_id=1, source_target_pairs={{0,1},{1,0},{2,3},{3,2},{4,5},{5,4},{6,7},{7,6},{8,9},{9,8},{10,11... | collective-permute-start | bytes 41480 | tf_op jit(solution)/shard_map/ppermute | solution.py:348
  4.0 0.1 collective-permute-start
  4.1 0.0 collective-permute-start.2
  4.1 1.8 %collective-permute-start.1 = (f32[3,32]{1,0:T(4,128)}, f32[3,32]{1,0:T(4,128)S(1)}, u32[]{:S(2)}, u32[]{:S(2)}) collective-permute-start(f32[3,32]{1,0:T(4,128)} %param.7), channel_id=1, source_target_pairs={{0,16},{1,17},{2,18},{3,19},{4,20},{5,21},{6,22},{7,23},{8,24},{9,... | collective-permute-start | bytes 1160 | tf_op jit(solution)/shard_map/ppermute | solution.py:348
  5.8 0.7 pad.20.jitter
  6.6 0.8 pad.21.field
  7.4 0.8 prepare.1
  8.2 7.3 %all-to-all-start = ((f32[8,64,128]{2,1,0:T(8,128)}), f32[8,64,128]{2,1,0:T(8,128)S(1)}, u32[]{:S(2)}, u32[]{:S(2)}) async-start(f32[8,64,128]{2,1,0:T(8,128)} %get-tuple-element.28), calls=%async_computation | async-start | bytes 524288 | tf_op jit(solution)/shard_map/all_to_all | solution.py:356
  15.5 0.7 convert_element_type.17
  16.2 0.1 pad_add_fusion.ids
  16.3 0.7 convert_bitcast_fusion
  17.0 0.7 select_maximum_fusion.species
  17.6 0.9 %copy-done = s32[256,256]{1,0:T(8,128)S(1)} copy-done((s32[256,256]{1,0:T(8,128)S(1)}, s32[256,256]{1,0:T(8,128)}, u32[]{:S(2)}) %copy-start) | copy-done | bytes 262168
  18.6 1.0 %side.1 = (f32[40,128]{1,0:T(8,128)S(1)}, f32[16,512]{1,0:T(8,128)S(1)}, f32[3,512,128]{2,1,0:T(8,128)S(1)}, f32[8,512]{1,0:T(8,128)S(1)}, f32[64,128]{1,0:T(8,128)S(1)}) custom-call(s32[2]{0:T(128)S(1)} %pad_add_fusion.ids, f32[8,128]{1,0:T(8,128)S(1)} %select_maximum_fusion.species, f32[8,256]{1,0:T(8,128)S(1)} %pad.24.cells, s32[256,256]{1,0:T(8,128)S(1)} %copy-done), custom_call_target="tpu_custom_call" | custom-call | tf_op jit(solution)/shard_map/side/pallas_call | solution.py:391
  19.6 5.3 %all-to-all-done.mine = f32[8,64,128]{2,1,0:T(8,128)S(1)} async-done(((f32[8,64,128]{2,1,0:T(8,128)}), f32[8,64,128]{2,1,0:T(8,128)S(1)}, u32[]{:S(2)}, u32[]{:S(2)}) %all-to-all-start) | async-done | bytes 262176 | tf_op jit(solution)/shard_map/all_to_all | solution.py:356
  24.9 1.5 %collective-permute-done.4.theirs = f32[8,64,128]{2,1,0:T(8,128)S(1)} collective-permute-done((f32[8,64,128]{2,1,0:T(8,128)S(1)}, f32[8,64,128]{2,1,0:T(8,128)S(1)}, u32[]{:S(2)}, u32[]{:S(2)}) %collective-permute-start.4) | collective-permute-done | bytes 262176 | tf_op jit(solution)/shard_map/ppermute | solution.py:348
  26.4 0.9 pick.1
  27.3 1.7 %first_own.1 = (f32[512,128]{1,0:T(8,128)S(1)}, bf16[512,1280]{1,0:T(8,128)(2,1)S(1)}, bf16[512,1280]{1,0:T(8,128)(2,1)S(1)}) custom-call(f32[16,512]{1,0:T(8,128)S(1)} %get-tuple-element.34.mask, f32[3,512,128]{2,1,0:T(8,128)S(1)} %get-tuple-element.38.column, f32[8,512]{1,0:T(8,128)S(1)} %get-tuple-element.39.points, ...), custom_call_target="tpu_custom_call" | custom-call | tf_op jit(solution)/shard_map/first_own/pallas_call | solution.py:414
  29.0 1.7 %first_other.1 = (f32[16,32,128]{2,1,0:T(8,128)S(1)}, bf16[512,1280]{1,0:T(8,128)(2,1)S(1)}, bf16[512,1280]{1,0:T(8,128)(2,1)S(1)}) custom-call(f32[16,512]{1,0:T(8,128)S(1)} %get-tuple-element.34.mask, f32[3,512,128]{2,1,0:T(8,128)S(1)} %get-tuple-element.38.column, f32[8,512]{1,0:T(8,128)S(1)} %get-tuple-element.39.points, ...), custom_call_target="tpu_custom_call" | custom-call | tf_op jit(solution)/shard_map/first_other/pallas_call | solution.py:423
  30.7 14.6 %all_to_all.25.parts = f32[16,32,128]{2,1,0:T(8,128)S(1)} all-to-all(f32[16,32,128]{2,1,0:T(8,128)S(1)} %get-tuple-element.43), channel_id=1, replica_groups={{0,16,32,48,64,80,96,112,128,144,160,176,192,208,224,240},{1,17,33,49,6..., dimensions={0} | all-to-all | bytes 524288 | tf_op jit(solution)/shard_map/all_to_all | solution.py:356
  45.4 0.2 shifted.1
  45.6 11.1 %all_to_all.26.gathered = f32[8,32,128]{2,1,0:T(8,128)S(1)} all-to-all(f32[8,32,128]{2,1,0:T(8,128)S(1)} %shifted.1), channel_id=1, replica_groups={{0,2,4,6,8,10,12,14},{1,3,5,7,9,11,13,15},{16,18,20,22,24,26,28,30},{17..., dimensions={0} | all-to-all | bytes 262144 | tf_op jit(solution)/shard_map/all_to_all | solution.py:356
  56.6 2.6 %collective-permute-start.5 = (f32[8,32,128]{2,1,0:T(8,128)S(1)}, f32[8,32,128]{2,1,0:T(8,128)S(1)}, u32[]{:S(2)}, u32[]{:S(2)}) collective-permute-start(f32[8,32,128]{2,1,0:T(8,128)S(1)} %all_to_all.26.gathered), channel_id=1, source_target_pairs={{0,1},{1,0},{2,3},{3,2},{4,5},{5,4},{6,7},{7,6},{8,9},{9,8},{10,11... | collective-permute-start | bytes 393224 | tf_op jit(solution)/shard_map/ppermute | solution.py:348
  59.3 0.9 second_own.1.total
  60.2 0.1 collective-permute-done.5.gathered
  60.3 0.9 second_other.1
  61.2 10.7 %all_to_all.27.parts = f32[16,32,128]{2,1,0:T(8,128)S(1)} all-to-all(f32[16,32,128]{2,1,0:T(8,128)S(1)} %second_other.1), channel_id=1, replica_groups={{0,16,32,48,64,80,96,112,128,144,160,176,192,208,224,240},{1,17,33,49,6..., dimensions={0} | all-to-all | bytes 524288 | tf_op jit(solution)/shard_map/all_to_all | solution.py:356
  71.9 0.4 step.1
  72.3 1.6 %collective-permute-start.6 = (f32[8,128]{1,0:T(8,128)S(1)}, f32[8,128]{1,0:T(8,128)S(1)}, u32[]{:S(2)}, u32[]{:S(2)}) collective-permute-start(f32[8,128]{1,0:T(8,128)S(1)} %get-tuple-element.50.sums), channel_id=1, source_target_pairs={{0,1},{1,0},{2,3},{3,2},{4,5},{5,4},{6,7},{7,6},{8,9},{9,8},{10,11... | collective-permute-start | bytes 12296 | tf_op jit(solution)/shard_map/ppermute | solution.py:348
  73.8 0.8 collective-permute-done.6.swapped
  74.6 16.1 %all_to_all.28 = f32[128,1,128]{2,1,0:T(1,128)S(1)} all-to-all(f32[128,1,128]{2,1,0:T(1,128)S(1)} %bitcast.14), channel_id=1, replica_groups={{0,2,4,6,8,10,12,14,16,18,20,22,24,26,28,30,32,34,36,38,40,42,44,46,48,..., dimensions={0} | all-to-all | bytes 131072 | tf_op jit(solution)/shard_map/all_to_all | solution.py:356
  90.7 0.8 finish.1
  (8 shorter events, 0.0 us)
Async XLA Ops:
  0.6 6.8 %collective-permute-start.3 = (f32[3,32,36]{2,1,0:T(8,128)}, f32[3,32,36]{2,1,0:T(8,128)S(1)}, u32[]{:S(2)}, u32[]{:S(2)}) collective-permute-start(f32[3,32,36]{2,1,0:T(8,128)} %bitcast.15), channel_id=1, source_target_pairs={{0,1},{1,0},{2,3},{3,2},{4,5},{5,4},{6,7},{7,6},{8,9},{9,8},{10,11... | collective-permute-start | bytes 41480 | tf_op jit(solution)/shard_map/ppermute | solution.py:348
  4.0 3.4 %collective-permute-start = (f32[3,32]{1,0:T(4,128)}, f32[3,32]{1,0:T(4,128)S(1)}, u32[]{:S(2)}, u32[]{:S(2)}) collective-permute-start(f32[3,32]{1,0:T(4,128)} %param.7), channel_id=1, source_target_pairs={{0,1},{1,0},{2,3},{3,2},{4,5},{5,4},{6,7},{7,6},{8,9},{9,8},{10,11... | collective-permute-start | bytes 1160 | tf_op jit(solution)/shard_map/ppermute | solution.py:348
  4.1 3.3 %collective-permute-start.2 = (f32[3,32]{1,0:T(4,128)}, f32[3,32]{1,0:T(4,128)S(1)}, u32[]{:S(2)}, u32[]{:S(2)}) collective-permute-start(f32[3,32]{1,0:T(4,128)} %param.7), channel_id=1, source_target_pairs={{0,17},{1,16},{2,19},{3,18},{4,21},{5,20},{6,23},{7,22},{8,25},{9,... | collective-permute-start | bytes 1160 | tf_op jit(solution)/shard_map/ppermute | solution.py:348
  4.1 3.3 %collective-permute-start.1 = (f32[3,32]{1,0:T(4,128)}, f32[3,32]{1,0:T(4,128)S(1)}, u32[]{:S(2)}, u32[]{:S(2)}) collective-permute-start(f32[3,32]{1,0:T(4,128)} %param.7), channel_id=1, source_target_pairs={{0,16},{1,17},{2,18},{3,19},{4,20},{5,21},{6,22},{7,23},{8,24},{9,... | collective-permute-start | bytes 1160 | tf_op jit(solution)/shard_map/ppermute | solution.py:348
  8.2 16.6 %all-to-all-start = ((f32[8,64,128]{2,1,0:T(8,128)}), f32[8,64,128]{2,1,0:T(8,128)S(1)}, u32[]{:S(2)}, u32[]{:S(2)}) async-start(f32[8,64,128]{2,1,0:T(8,128)} %get-tuple-element.28), calls=%async_computation | async-start | bytes 524288 | tf_op jit(solution)/shard_map/all_to_all | solution.py:356
  17.6 0.9 %copy-start = (s32[256,256]{1,0:T(8,128)S(1)}, s32[256,256]{1,0:T(8,128)}, u32[]{:S(2)}) copy-start(s32[256,256]{1,0:T(8,128)} %tile_map.1) | copy-start | bytes 786436
  24.9 1.5 %collective-permute-start.4 = (f32[8,64,128]{2,1,0:T(8,128)S(1)}, f32[8,64,128]{2,1,0:T(8,128)S(1)}, u32[]{:S(2)}, u32[]{:S(2)}) collective-permute-start(f32[8,64,128]{2,1,0:T(8,128)S(1)} %all-to-all-done.mine), channel_id=1, source_target_pairs={{0,1},{1,0},{2,3},{3,2},{4,5},{5,4},{6,7},{7,6},{8,9},{9,8},{10,11... | collective-permute-start | bytes 786440 | tf_op jit(solution)/shard_map/ppermute | solution.py:348
  56.6 3.6 %collective-permute-start.5 = (f32[8,32,128]{2,1,0:T(8,128)S(1)}, f32[8,32,128]{2,1,0:T(8,128)S(1)}, u32[]{:S(2)}, u32[]{:S(2)}) collective-permute-start(f32[8,32,128]{2,1,0:T(8,128)S(1)} %all_to_all.26.gathered), channel_id=1, source_target_pairs={{0,1},{1,0},{2,3},{3,2},{4,5},{5,4},{6,7},{7,6},{8,9},{9,8},{10,11... | collective-permute-start | bytes 393224 | tf_op jit(solution)/shard_map/ppermute | solution.py:348
  72.3 2.4 %collective-permute-start.6 = (f32[8,128]{1,0:T(8,128)S(1)}, f32[8,128]{1,0:T(8,128)S(1)}, u32[]{:S(2)}, u32[]{:S(2)}) collective-permute-start(f32[8,128]{1,0:T(8,128)S(1)} %get-tuple-element.50.sums), channel_id=1, source_target_pairs={{0,1},{1,0},{2,3},{3,2},{4,5},{5,4},{6,7},{7,6},{8,9},{9,8},{10,11... | collective-permute-start | bytes 12296 | tf_op jit(solution)/shard_map/ppermute | solution.py:348

commit v10 on v9

--- a/solution.py
+++ b/solution.py
@@ -65,25 +65,6 @@
             own_out[...] = turned
         for slot in range(HALF):
             vec_out[slot, flip * ATOMS : (flip + 1) * ATOMS, :] = turned
-
-
-def pick_kernel(flags, points, mine, theirs, own, other, column):
-    odd_core = flags[0:ATOMS, :] > 0.5
-    odd_row = flags[ATOMS : 2 * ATOMS, :] > 0.5
-    for slot in range(HALF):
-        first, second = mine[slot, 0:ATOMS, :], mine[slot, ATOMS : 2 * ATOMS, :]
-        third, fourth = theirs[slot, 0:ATOMS, :], theirs[slot, ATOMS : 2 * ATOMS, :]
-        own[slot] = jnp.where(odd_core, first, fourth)
-        other[slot] = jnp.where(odd_core, second, third)
-        rows = jnp.where(odd_core, fourth, first)
-        beside = pltpu.roll(rows, LANES - 4, 1)
-        for block, sites in (
-            (2 * slot, jnp.where(odd_row, beside, rows)),
-            (2 * slot + 1, jnp.where(odd_row, rows, beside)),
-        ):
-            place = slice(block * ATOMS, (block + 1) * ATOMS)
-            for comp in range(COMPS):
-                column[comp, place, :] = points[comp, place, :] + sites[:, SITE + comp : SITE + comp + 1]
 
 
 def lattice(comp, atom, cell):
@@ -219,17 +200,34 @@
     return jnp.concatenate(outs, axis=0)
 
 
-def first_own_kernel(mask, column, points, gathered, total, high, low, side):
-    vectors = gathered[...].reshape(NARROW, LANES)
-    right_side(vectors, side)
-    total[...] = build_and_apply(mask, vectors, column, points, high, low, side, 0)
-
-
-def first_other_kernel(mask, column, points, gathered, total, part_out, high, low, side):
-    vectors = gathered[...].reshape(NARROW, LANES)
-    right_side(vectors, side)
-    out = build_and_apply(mask, vectors, column, points, high, low, side, NARROW)
-    part_out[...] = (total[...] + out).reshape(GROUP, ATOMS, LANES)
+def first_kernel(
+    flags, points, mask, across, mine, theirs,
+    part_out, high0, low0, high1, low1, own, other, column, side0, side1
+):
+    odd_core = flags[0:ATOMS, :] > 0.5
+    odd_row = flags[ATOMS : 2 * ATOMS, :] > 0.5
+    for slot in range(HALF):
+        first, second = mine[slot, 0:ATOMS, :], mine[slot, ATOMS : 2 * ATOMS, :]
+        third, fourth = theirs[slot, 0:ATOMS, :], theirs[slot, ATOMS : 2 * ATOMS, :]
+        own[slot] = jnp.where(odd_core, first, fourth)
+        other[slot] = jnp.where(odd_core, second, third)
+        rows = jnp.where(odd_core, fourth, first)
+        beside = pltpu.roll(rows, LANES - 4, 1)
+        for block, sites in (
+            (2 * slot, jnp.where(odd_row, beside, rows)),
+            (2 * slot + 1, jnp.where(odd_row, rows, beside)),
+        ):
+            place = slice(block * ATOMS, (block + 1) * ATOMS)
+            for comp in range(COMPS):
+                column[comp, place, :] = points[comp, place, :] + sites[:, SITE + comp : SITE + comp + 1]
+
+    total = jnp.zeros((WIDE, LANES), F32)
+    halves = ((own, high0, low0, side0), (other, high1, low1, side1))
+    for half, (gathered, high, low, right) in enumerate(halves):
+        vectors = gathered[...].reshape(NARROW, LANES)
+        right_side(vectors, right)
+        total = total + build_and_apply(mask, vectors, column, across, high, low, right, half * NARROW)
+    part_out[...] = total.reshape(GROUP, ATOMS, LANES)
 
 
 def spare_sums(vectors):
@@ -400,35 +398,18 @@
     mine, aux, mask, points, across, flags = lax.optimization_barrier(
         (exchange(vec, MIXED), aux, mask, points, across, flags)
     )
-    half = shape(HALF, ATOMS, LANES)
-    own, other, column = pl.pallas_call(
-        pick_kernel,
-        out_shape=(half, half, column_shape),
-        in_specs=[VMEM, VMEM, VMEM, VMEM],
-        out_specs=(VMEM, VMEM, VMEM),
-        compiler_params=PARAMS,
-        name="pick",
-    )(flags, points, mine, core_swap(mine))
     side = pltpu.VMEM((PAIRS * NARROW, 2 * LANES), BF16)
+    half = pltpu.VMEM((HALF, ATOMS, LANES), F32)
     tile = shape(WIDE, PAIRS * NARROW, dtype=BF16)
-    total, high0, low0 = pl.pallas_call(
-        first_own_kernel,
-        out_shape=(shape(WIDE, LANES), tile, tile),
-        in_specs=[VMEM] * 4,
-        out_specs=(VMEM, VMEM, VMEM),
-        scratch_shapes=[side],
-        compiler_params=PARAMS,
-        name="first_own",
-    )(mask, column, across, own)
-    part, high1, low1 = pl.pallas_call(
-        first_other_kernel,
-        out_shape=(shape(GROUP, ATOMS, LANES), tile, tile),
-        in_specs=[VMEM] * 5,
-        out_specs=(VMEM, VMEM, VMEM),
-        scratch_shapes=[side],
-        compiler_params=PARAMS,
-        name="first_other",
-    )(mask, column, across, other, total)
+    part, high0, low0, high1, low1 = pl.pallas_call(
+        first_kernel,
+        out_shape=(shape(GROUP, ATOMS, LANES), tile, tile, tile, tile),
+        in_specs=[VMEM] * 6,
+        out_specs=(VMEM,) * 5,
+        scratch_shapes=[half, half, pltpu.VMEM((COMPS, WIDE, LANES), F32), side, side],
+        compiler_params=PARAMS,
+        name="first",
+    )(flags, points, mask, across, mine, core_swap(mine))
     parts = exchange(part, ROWS)
     blocks = whole(GROUP, ATOMS, LANES)
     block = whole(1, ATOMS, LANES)

time: 92.1 us -> 92 us (level)
    pallas_call x3 -> x1, Pallas kernels: 4.32 us -> 4.25 us  [local(): pl.pallas_call(first_kernel, out_shape=(shape(GROUP, ATOMS, LANES), tile,...]
where the time goes in v10:
time: 92 us; the launch traced here: 91.5 us
  blocking collectives  52.5 us (57%)
  starting transfers between devices  16.7 us (18%)
  Pallas kernels  9.17 us (10%)
  waiting for transfers between devices  7.78 us (8%)
  local copies, waits for them, and re-layouts  2.48 us (3%)
  other arithmetic  2.1 us (2%)
    all_to_all x4, blocking collectives, exchange(): return lax.all_to_all(value, 'device', 0, 0, axis_index_groups=groups)  52.5 us
    ppermute x7, starting transfers between devices, trade(): lax.ppermute(value, 'device', [(here, here ^ bits) for here in range(GROU...  9.41 us
    all_to_all x1, starting transfers between devices, exchange(): return lax.all_to_all(value, 'device', 0, 0, axis_index_groups=groups)  7.28 us
    all_to_all x1, waiting for transfers between devices, exchange(): return lax.all_to_all(value, 'device', 0, 0, axis_index_groups=groups)  5.31 us
    pallas_call x1, Pallas kernels, local(): pl.pallas_call(first_kernel, out_shape=(shape(GROUP, ATOMS, LANES), tile,...  4.25 us
    ppermute x7, waiting for transfers between devices, trade(): lax.ppermute(value, 'device', [(here, here ^ bits) for here in range(GROU...  2.47 us
  transfers between devices with their start and end apart: 8, of which 4 were waited for; matrix products, arithmetic and copies ran while one was open for 4% of the time, Pallas kernels for 2%

profile of v10, /device:TPU:1, one launch (start us, length us, event | category | flops | bytes accessed | tf_op | source)
XLA Modules:
  0.0 91.5 jit_solution(4640580691357778043)
XLA Ops:
  0.6 3.3 %collective-permute-start.3 = (f32[3,32,36]{2,1,0:T(8,128)}, f32[3,32,36]{2,1,0:T(8,128)S(1)}, u32[]{:S(2)}, u32[]{:S(2)}) collective-permute-start(f32[3,32,36]{2,1,0:T(8,128)} %bitcast.15), channel_id=1, source_target_pairs={{0,1},{1,0},{2,3},{3,2},{4,5},{5,4},{6,7},{7,6},{8,9},{9,8},{10,11... | collective-permute-start | bytes 41480 | tf_op jit(solution)/shard_map/ppermute | solution.py:346
  4.0 0.1 collective-permute-start
  4.1 0.0 collective-permute-start.2
  4.1 1.8 %collective-permute-start.1 = (f32[3,32]{1,0:T(4,128)}, f32[3,32]{1,0:T(4,128)S(1)}, u32[]{:S(2)}, u32[]{:S(2)}) collective-permute-start(f32[3,32]{1,0:T(4,128)} %param.7), channel_id=1, source_target_pairs={{0,16},{1,17},{2,18},{3,19},{4,20},{5,21},{6,22},{7,23},{8,24},{9,... | collective-permute-start | bytes 1160 | tf_op jit(solution)/shard_map/ppermute | solution.py:346
  5.8 0.7 pad.20.jitter
  6.6 0.8 pad.21.field
  7.4 0.0 collective-permute-done.across
  7.4 0.0 collective-permute-done.1.beside
  7.4 0.9 prepare.1
  8.3 7.3 %all-to-all-start = ((f32[8,64,128]{2,1,0:T(8,128)}), f32[8,64,128]{2,1,0:T(8,128)S(1)}, u32[]{:S(2)}, u32[]{:S(2)}) async-start(f32[8,64,128]{2,1,0:T(8,128)} %get-tuple-element.24), calls=%async_computation | async-start | bytes 524288 | tf_op jit(solution)/shard_map/all_to_all | solution.py:354
  15.5 0.7 convert_element_type.17
  16.2 0.1 pad_add_fusion.ids
  16.3 0.7 convert_bitcast_fusion
  17.0 0.7 select_maximum_fusion.species
  17.7 0.9 %copy-done = s32[256,256]{1,0:T(8,128)S(1)} copy-done((s32[256,256]{1,0:T(8,128)S(1)}, s32[256,256]{1,0:T(8,128)}, u32[]{:S(2)}) %copy-start) | copy-done | bytes 262168
  18.6 1.0 %side.1 = (f32[40,128]{1,0:T(8,128)S(1)}, f32[16,512]{1,0:T(8,128)S(1)}, f32[3,512,128]{2,1,0:T(8,128)S(1)}, f32[8,512]{1,0:T(8,128)S(1)}, f32[64,128]{1,0:T(8,128)S(1)}) custom-call(s32[2]{0:T(128)S(1)} %pad_add_fusion.ids, f32[8,128]{1,0:T(8,128)S(1)} %select_maximum_fusion.species, f32[8,256]{1,0:T(8,128)S(1)} %pad.24.cells, s32[256,256]{1,0:T(8,128)S(1)} %copy-done), custom_call_target="tpu_custom_call" | custom-call | tf_op jit(solution)/shard_map/side/pallas_call | solution.py:389
  19.6 5.3 %all-to-all-done.mine = f32[8,64,128]{2,1,0:T(8,128)S(1)} async-done(((f32[8,64,128]{2,1,0:T(8,128)}), f32[8,64,128]{2,1,0:T(8,128)S(1)}, u32[]{:S(2)}, u32[]{:S(2)}) %all-to-all-start) | async-done | bytes 262176 | tf_op jit(solution)/shard_map/all_to_all | solution.py:354
  24.9 1.5 %collective-permute-done.4.theirs = f32[8,64,128]{2,1,0:T(8,128)S(1)} collective-permute-done((f32[8,64,128]{2,1,0:T(8,128)S(1)}, f32[8,64,128]{2,1,0:T(8,128)S(1)}, u32[]{:S(2)}, u32[]{:S(2)}) %collective-permute-start.4) | collective-permute-done | bytes 262176 | tf_op jit(solution)/shard_map/ppermute | solution.py:346
  26.4 4.3 %first.1 = (f32[16,32,128]{2,1,0:T(8,128)S(1)}, bf16[512,1280]{1,0:T(8,128)(2,1)S(1)}, bf16[512,1280]{1,0:T(8,128)(2,1)S(1)}, bf16[512,1280]{1,0:T(8,128)(2,1)S(1)}, bf16[512,1280]{1,0:T(8,128)(2,1)S(1)}) custom-call(f32[64,128]{1,0:T(8,128)S(1)} %get-tuple-element.30.flags, f32[3,512,128]{2,1,0:T(8,128)S(1)} %get-tuple-element.31.points, ...), custom_call_target="tpu_custom_call" | custom-call | tf_op jit(solution)/shard_map/first/pallas_call | solution.py:404
  30.7 14.6 %all_to_all.25.parts = f32[16,32,128]{2,1,0:T(8,128)S(1)} all-to-all(f32[16,32,128]{2,1,0:T(8,128)S(1)} %get-tuple-element.35), channel_id=1, replica_groups={{0,16,32,48,64,80,96,112,128,144,160,176,192,208,224,240},{1,17,33,49,6..., dimensions={0} | all-to-all | bytes 524288 | tf_op jit(solution)/shard_map/all_to_all | solution.py:354
  45.3 0.2 shifted.1
  45.5 11.1 %all_to_all.26.gathered = f32[8,32,128]{2,1,0:T(8,128)S(1)} all-to-all(f32[8,32,128]{2,1,0:T(8,128)S(1)} %shifted.1), channel_id=1, replica_groups={{0,2,4,6,8,10,12,14},{1,3,5,7,9,11,13,15},{16,18,20,22,24,26,28,30},{17..., dimensions={0} | all-to-all | bytes 262144 | tf_op jit(solution)/shard_map/all_to_all | solution.py:354
  56.6 2.6 %collective-permute-start.5 = (f32[8,32,128]{2,1,0:T(8,128)S(1)}, f32[8,32,128]{2,1,0:T(8,128)S(1)}, u32[]{:S(2)}, u32[]{:S(2)}) collective-permute-start(f32[8,32,128]{2,1,0:T(8,128)S(1)} %all_to_all.26.gathered), channel_id=1, source_target_pairs={{0,1},{1,0},{2,3},{3,2},{4,5},{5,4},{6,7},{7,6},{8,9},{9,8},{10,11... | collective-permute-start | bytes 393224 | tf_op jit(solution)/shard_map/ppermute | solution.py:346
  59.2 0.9 second_own.1.total
  60.1 0.1 collective-permute-done.5.gathered
  60.2 0.9 second_other.1
  61.1 10.8 %all_to_all.27.parts = f32[16,32,128]{2,1,0:T(8,128)S(1)} all-to-all(f32[16,32,128]{2,1,0:T(8,128)S(1)} %second_other.1), channel_id=1, replica_groups={{0,16,32,48,64,80,96,112,128,144,160,176,192,208,224,240},{1,17,33,49,6..., dimensions={0} | all-to-all | bytes 524288 | tf_op jit(solution)/shard_map/all_to_all | solution.py:354
  71.8 0.4 step.1
  72.2 1.6 %collective-permute-start.6 = (f32[8,128]{1,0:T(8,128)S(1)}, f32[8,128]{1,0:T(8,128)S(1)}, u32[]{:S(2)}, u32[]{:S(2)}) collective-permute-start(f32[8,128]{1,0:T(8,128)S(1)} %get-tuple-element.42.sums), channel_id=1, source_target_pairs={{0,1},{1,0},{2,3},{3,2},{4,5},{5,4},{6,7},{7,6},{8,9},{9,8},{10,11... | collective-permute-start | bytes 12296 | tf_op jit(solution)/shard_map/ppermute | solution.py:346
  73.8 0.8 collective-permute-done.6.swapped
  74.6 16.1 %all_to_all.28 = f32[128,1,128]{2,1,0:T(1,128)S(1)} all-to-all(f32[128,1,128]{2,1,0:T(1,128)S(1)} %bitcast.14), channel_id=1, replica_groups={{0,2,4,6,8,10,12,14,16,18,20,22,24,26,28,30,32,34,36,38,40,42,44,46,48,..., dimensions={0} | all-to-all | bytes 131072 | tf_op jit(solution)/shard_map/all_to_all | solution.py:354
  90.7 0.8 finish.1
  (6 shorter events, 0.0 us)
Async XLA Ops:
  0.6 6.8 %collective-permute-start.3 = (f32[3,32,36]{2,1,0:T(8,128)}, f32[3,32,36]{2,1,0:T(8,128)S(1)}, u32[]{:S(2)}, u32[]{:S(2)}) collective-permute-start(f32[3,32,36]{2,1,0:T(8,128)} %bitcast.15), channel_id=1, source_target_pairs={{0,1},{1,0},{2,3},{3,2},{4,5},{5,4},{6,7},{7,6},{8,9},{9,8},{10,11... | collective-permute-start | bytes 41480 | tf_op jit(solution)/shard_map/ppermute | solution.py:346
  4.0 3.4 %collective-permute-start = (f32[3,32]{1,0:T(4,128)}, f32[3,32]{1,0:T(4,128)S(1)}, u32[]{:S(2)}, u32[]{:S(2)}) collective-permute-start(f32[3,32]{1,0:T(4,128)} %param.7), channel_id=1, source_target_pairs={{0,1},{1,0},{2,3},{3,2},{4,5},{5,4},{6,7},{7,6},{8,9},{9,8},{10,11... | collective-permute-start | bytes 1160 | tf_op jit(solution)/shard_map/ppermute | solution.py:346
  4.1 3.3 %collective-permute-start.2 = (f32[3,32]{1,0:T(4,128)}, f32[3,32]{1,0:T(4,128)S(1)}, u32[]{:S(2)}, u32[]{:S(2)}) collective-permute-start(f32[3,32]{1,0:T(4,128)} %param.7), channel_id=1, source_target_pairs={{0,17},{1,16},{2,19},{3,18},{4,21},{5,20},{6,23},{7,22},{8,25},{9,... | collective-permute-start | bytes 1160 | tf_op jit(solution)/shard_map/ppermute | solution.py:346
  4.1 3.3 %collective-permute-start.1 = (f32[3,32]{1,0:T(4,128)}, f32[3,32]{1,0:T(4,128)S(1)}, u32[]{:S(2)}, u32[]{:S(2)}) collective-permute-start(f32[3,32]{1,0:T(4,128)} %param.7), channel_id=1, source_target_pairs={{0,16},{1,17},{2,18},{3,19},{4,20},{5,21},{6,22},{7,23},{8,24},{9,... | collective-permute-start | bytes 1160 | tf_op jit(solution)/shard_map/ppermute | solution.py:346
  8.3 16.6 %all-to-all-start = ((f32[8,64,128]{2,1,0:T(8,128)}), f32[8,64,128]{2,1,0:T(8,128)S(1)}, u32[]{:S(2)}, u32[]{:S(2)}) async-start(f32[8,64,128]{2,1,0:T(8,128)} %get-tuple-element.24), calls=%async_computation | async-start | bytes 524288 | tf_op jit(solution)/shard_map/all_to_all | solution.py:354
  17.7 0.9 %copy-start = (s32[256,256]{1,0:T(8,128)S(1)}, s32[256,256]{1,0:T(8,128)}, u32[]{:S(2)}) copy-start(s32[256,256]{1,0:T(8,128)} %tile_map.1) | copy-start | bytes 786436
  24.9 1.5 %collective-permute-start.4 = (f32[8,64,128]{2,1,0:T(8,128)S(1)}, f32[8,64,128]{2,1,0:T(8,128)S(1)}, u32[]{:S(2)}, u32[]{:S(2)}) collective-permute-start(f32[8,64,128]{2,1,0:T(8,128)S(1)} %all-to-all-done.mine), channel_id=1, source_target_pairs={{0,1},{1,0},{2,3},{3,2},{4,5},{5,4},{6,7},{7,6},{8,9},{9,8},{10,11... | collective-permute-start | bytes 786440 | tf_op jit(solution)/shard_map/ppermute | solution.py:346
  56.6 3.6 %collective-permute-start.5 = (f32[8,32,128]{2,1,0:T(8,128)S(1)}, f32[8,32,128]{2,1,0:T(8,128)S(1)}, u32[]{:S(2)}, u32[]{:S(2)}) collective-permute-start(f32[8,32,128]{2,1,0:T(8,128)S(1)} %all_to_all.26.gathered), channel_id=1, source_target_pairs={{0,1},{1,0},{2,3},{3,2},{4,5},{5,4},{6,7},{7,6},{8,9},{9,8},{10,11... | collective-permute-start | bytes 393224 | tf_op jit(solution)/shard_map/ppermute | solution.py:346
  72.2 2.4 %collective-permute-start.6 = (f32[8,128]{1,0:T(8,128)S(1)}, f32[8,128]{1,0:T(8,128)S(1)}, u32[]{:S(2)}, u32[]{:S(2)}) collective-permute-start(f32[8,128]{1,0:T(8,128)S(1)} %get-tuple-element.42.sums), channel_id=1, source_target_pairs={{0,1},{1,0},{2,3},{3,2},{4,5},{5,4},{6,7},{7,6},{8,9},{9,8},{10,11... | collective-permute-start | bytes 12296 | tf_op jit(solution)/shard_map/ppermute | solution.py:346

commit v11 on v10

--- a/solution.py
+++ b/solution.py
@@ -16,7 +16,7 @@
 SUM_ROW = 104
 WIDE = GROUP * ATOMS
 NARROW = HALF * ATOMS
-CHUNK = 256
+CHUNK = 128
 PAIRS = 5
 SPACING = 2.0
 F32 = jnp.float32

time: 92 us -> 92 us (level)
  no operation moved by 1% of the time
where the time goes in v11:
time: 92 us; the launch traced here: 91.5 us
  blocking collectives  52.5 us (57%)
  starting transfers between devices  16.7 us (18%)
  Pallas kernels  9.23 us (10%)
  waiting for transfers between devices  7.78 us (8%)
  local copies, waits for them, and re-layouts  2.48 us (3%)
  other arithmetic  2.1 us (2%)
    all_to_all x4, blocking collectives, exchange(): return lax.all_to_all(value, 'device', 0, 0, axis_index_groups=groups)  52.5 us
    ppermute x7, starting transfers between devices, trade(): lax.ppermute(value, 'device', [(here, here ^ bits) for here in range(GROU...  9.42 us
    all_to_all x1, starting transfers between devices, exchange(): return lax.all_to_all(value, 'device', 0, 0, axis_index_groups=groups)  7.28 us
    all_to_all x1, waiting for transfers between devices, exchange(): return lax.all_to_all(value, 'device', 0, 0, axis_index_groups=groups)  5.31 us
    pallas_call x1, Pallas kernels, local(): pl.pallas_call(first_kernel, out_shape=(shape(GROUP, ATOMS, LANES), tile,...  4.31 us
    ppermute x7, waiting for transfers between devices, trade(): lax.ppermute(value, 'device', [(here, here ^ bits) for here in range(GROU...  2.47 us
  transfers between devices with their start and end apart: 8, of which 4 were waited for; matrix products, arithmetic and copies ran while one was open for 4% of the time, Pallas kernels for 2%

profile of v11, /device:TPU:1, one launch (start us, length us, event | category | flops | bytes accessed | tf_op | source)
XLA Modules:
  0.0 91.5 jit_solution(15256699310744867537)
XLA Ops:
  0.6 3.3 %collective-permute-start.3 = (f32[3,32,36]{2,1,0:T(8,128)}, f32[3,32,36]{2,1,0:T(8,128)S(1)}, u32[]{:S(2)}, u32[]{:S(2)}) collective-permute-start(f32[3,32,36]{2,1,0:T(8,128)} %bitcast.15), channel_id=1, source_target_pairs={{0,1},{1,0},{2,3},{3,2},{4,5},{5,4},{6,7},{7,6},{8,9},{9,8},{10,11... | collective-permute-start | bytes 41480 | tf_op jit(solution)/shard_map/ppermute | solution.py:346
  4.0 0.1 collective-permute-start
  4.1 0.0 collective-permute-start.2
  4.1 1.8 %collective-permute-start.1 = (f32[3,32]{1,0:T(4,128)}, f32[3,32]{1,0:T(4,128)S(1)}, u32[]{:S(2)}, u32[]{:S(2)}) collective-permute-start(f32[3,32]{1,0:T(4,128)} %param.7), channel_id=1, source_target_pairs={{0,16},{1,17},{2,18},{3,19},{4,20},{5,21},{6,22},{7,23},{8,24},{9,... | collective-permute-start | bytes 1160 | tf_op jit(solution)/shard_map/ppermute | solution.py:346
  5.8 0.7 pad.20.jitter
  6.6 0.8 pad.21.field
  7.4 0.0 collective-permute-done.across
  7.4 0.0 collective-permute-done.1.beside
  7.4 0.9 prepare.1
  8.3 7.3 %all-to-all-start = ((f32[8,64,128]{2,1,0:T(8,128)}), f32[8,64,128]{2,1,0:T(8,128)S(1)}, u32[]{:S(2)}, u32[]{:S(2)}) async-start(f32[8,64,128]{2,1,0:T(8,128)} %get-tuple-element.24), calls=%async_computation | async-start | bytes 524288 | tf_op jit(solution)/shard_map/all_to_all | solution.py:354
  15.5 0.7 convert_element_type.17
  16.2 0.1 pad_add_fusion.ids
  16.3 0.7 convert_bitcast_fusion
  17.0 0.7 select_maximum_fusion.species
  17.7 0.9 %copy-done = s32[256,256]{1,0:T(8,128)S(1)} copy-done((s32[256,256]{1,0:T(8,128)S(1)}, s32[256,256]{1,0:T(8,128)}, u32[]{:S(2)}) %copy-start) | copy-done | bytes 262168
  18.6 1.0 %side.1 = (f32[40,128]{1,0:T(8,128)S(1)}, f32[16,512]{1,0:T(8,128)S(1)}, f32[3,512,128]{2,1,0:T(8,128)S(1)}, f32[8,512]{1,0:T(8,128)S(1)}, f32[64,128]{1,0:T(8,128)S(1)}) custom-call(s32[2]{0:T(128)S(1)} %pad_add_fusion.ids, f32[8,128]{1,0:T(8,128)S(1)} %select_maximum_fusion.species, f32[8,256]{1,0:T(8,128)S(1)} %pad.24.cells, s32[256,256]{1,0:T(8,128)S(1)} %copy-done), custom_call_target="tpu_custom_call" | custom-call | tf_op jit(solution)/shard_map/side/pallas_call | solution.py:389
  19.6 5.3 %all-to-all-done.mine = f32[8,64,128]{2,1,0:T(8,128)S(1)} async-done(((f32[8,64,128]{2,1,0:T(8,128)}), f32[8,64,128]{2,1,0:T(8,128)S(1)}, u32[]{:S(2)}, u32[]{:S(2)}) %all-to-all-start) | async-done | bytes 262176 | tf_op jit(solution)/shard_map/all_to_all | solution.py:354
  24.9 1.5 %collective-permute-done.4.theirs = f32[8,64,128]{2,1,0:T(8,128)S(1)} collective-permute-done((f32[8,64,128]{2,1,0:T(8,128)S(1)}, f32[8,64,128]{2,1,0:T(8,128)S(1)}, u32[]{:S(2)}, u32[]{:S(2)}) %collective-permute-start.4) | collective-permute-done | bytes 262176 | tf_op jit(solution)/shard_map/ppermute | solution.py:346
  26.4 4.3 %first.1 = (f32[16,32,128]{2,1,0:T(8,128)S(1)}, bf16[512,1280]{1,0:T(8,128)(2,1)S(1)}, bf16[512,1280]{1,0:T(8,128)(2,1)S(1)}, bf16[512,1280]{1,0:T(8,128)(2,1)S(1)}, bf16[512,1280]{1,0:T(8,128)(2,1)S(1)}) custom-call(f32[64,128]{1,0:T(8,128)S(1)} %get-tuple-element.30.flags, f32[3,512,128]{2,1,0:T(8,128)S(1)} %get-tuple-element.31.points, ...), custom_call_target="tpu_custom_call" | custom-call | tf_op jit(solution)/shard_map/first/pallas_call | solution.py:404
  30.7 14.6 %all_to_all.25.parts = f32[16,32,128]{2,1,0:T(8,128)S(1)} all-to-all(f32[16,32,128]{2,1,0:T(8,128)S(1)} %get-tuple-element.35), channel_id=1, replica_groups={{0,16,32,48,64,80,96,112,128,144,160,176,192,208,224,240},{1,17,33,49,6..., dimensions={0} | all-to-all | bytes 524288 | tf_op jit(solution)/shard_map/all_to_all | solution.py:354
  45.3 0.2 shifted.1
  45.6 11.1 %all_to_all.26.gathered = f32[8,32,128]{2,1,0:T(8,128)S(1)} all-to-all(f32[8,32,128]{2,1,0:T(8,128)S(1)} %shifted.1), channel_id=1, replica_groups={{0,2,4,6,8,10,12,14},{1,3,5,7,9,11,13,15},{16,18,20,22,24,26,28,30},{17..., dimensions={0} | all-to-all | bytes 262144 | tf_op jit(solution)/shard_map/all_to_all | solution.py:354
  56.6 2.7 %collective-permute-start.5 = (f32[8,32,128]{2,1,0:T(8,128)S(1)}, f32[8,32,128]{2,1,0:T(8,128)S(1)}, u32[]{:S(2)}, u32[]{:S(2)}) collective-permute-start(f32[8,32,128]{2,1,0:T(8,128)S(1)} %all_to_all.26.gathered), channel_id=1, source_target_pairs={{0,1},{1,0},{2,3},{3,2},{4,5},{5,4},{6,7},{7,6},{8,9},{9,8},{10,11... | collective-permute-start | bytes 393224 | tf_op jit(solution)/shard_map/ppermute | solution.py:346
  59.3 0.9 second_own.1.total
  60.2 0.1 collective-permute-done.5.gathered
  60.3 0.9 second_other.1
  61.1 10.7 %all_to_all.27.parts = f32[16,32,128]{2,1,0:T(8,128)S(1)} all-to-all(f32[16,32,128]{2,1,0:T(8,128)S(1)} %second_other.1), channel_id=1, replica_groups={{0,16,32,48,64,80,96,112,128,144,160,176,192,208,224,240},{1,17,33,49,6..., dimensions={0} | all-to-all | bytes 524288 | tf_op jit(solution)/shard_map/all_to_all | solution.py:354
  71.9 0.4 step.1
  72.2 1.6 %collective-permute-start.6 = (f32[8,128]{1,0:T(8,128)S(1)}, f32[8,128]{1,0:T(8,128)S(1)}, u32[]{:S(2)}, u32[]{:S(2)}) collective-permute-start(f32[8,128]{1,0:T(8,128)S(1)} %get-tuple-element.42.sums), channel_id=1, source_target_pairs={{0,1},{1,0},{2,3},{3,2},{4,5},{5,4},{6,7},{7,6},{8,9},{9,8},{10,11... | collective-permute-start | bytes 12296 | tf_op jit(solution)/shard_map/ppermute | solution.py:346
  73.8 0.8 collective-permute-done.6.swapped
  74.6 16.1 %all_to_all.28 = f32[128,1,128]{2,1,0:T(1,128)S(1)} all-to-all(f32[128,1,128]{2,1,0:T(1,128)S(1)} %bitcast.14), channel_id=1, replica_groups={{0,2,4,6,8,10,12,14,16,18,20,22,24,26,28,30,32,34,36,38,40,42,44,46,48,..., dimensions={0} | all-to-all | bytes 131072 | tf_op jit(solution)/shard_map/all_to_all | solution.py:354
  90.7 0.8 finish.1
  (6 shorter events, 0.0 us)
Async XLA Ops:
  0.6 6.8 %collective-permute-start.3 = (f32[3,32,36]{2,1,0:T(8,128)}, f32[3,32,36]{2,1,0:T(8,128)S(1)}, u32[]{:S(2)}, u32[]{:S(2)}) collective-permute-start(f32[3,32,36]{2,1,0:T(8,128)} %bitcast.15), channel_id=1, source_target_pairs={{0,1},{1,0},{2,3},{3,2},{4,5},{5,4},{6,7},{7,6},{8,9},{9,8},{10,11... | collective-permute-start | bytes 41480 | tf_op jit(solution)/shard_map/ppermute | solution.py:346
  4.0 3.4 %collective-permute-start = (f32[3,32]{1,0:T(4,128)}, f32[3,32]{1,0:T(4,128)S(1)}, u32[]{:S(2)}, u32[]{:S(2)}) collective-permute-start(f32[3,32]{1,0:T(4,128)} %param.7), channel_id=1, source_target_pairs={{0,1},{1,0},{2,3},{3,2},{4,5},{5,4},{6,7},{7,6},{8,9},{9,8},{10,11... | collective-permute-start | bytes 1160 | tf_op jit(solution)/shard_map/ppermute | solution.py:346
  4.1 3.3 %collective-permute-start.2 = (f32[3,32]{1,0:T(4,128)}, f32[3,32]{1,0:T(4,128)S(1)}, u32[]{:S(2)}, u32[]{:S(2)}) collective-permute-start(f32[3,32]{1,0:T(4,128)} %param.7), channel_id=1, source_target_pairs={{0,17},{1,16},{2,19},{3,18},{4,21},{5,20},{6,23},{7,22},{8,25},{9,... | collective-permute-start | bytes 1160 | tf_op jit(solution)/shard_map/ppermute | solution.py:346
  4.1 3.3 %collective-permute-start.1 = (f32[3,32]{1,0:T(4,128)}, f32[3,32]{1,0:T(4,128)S(1)}, u32[]{:S(2)}, u32[]{:S(2)}) collective-permute-start(f32[3,32]{1,0:T(4,128)} %param.7), channel_id=1, source_target_pairs={{0,16},{1,17},{2,18},{3,19},{4,20},{5,21},{6,22},{7,23},{8,24},{9,... | collective-permute-start | bytes 1160 | tf_op jit(solution)/shard_map/ppermute | solution.py:346
  8.3 16.6 %all-to-all-start = ((f32[8,64,128]{2,1,0:T(8,128)}), f32[8,64,128]{2,1,0:T(8,128)S(1)}, u32[]{:S(2)}, u32[]{:S(2)}) async-start(f32[8,64,128]{2,1,0:T(8,128)} %get-tuple-element.24), calls=%async_computation | async-start | bytes 524288 | tf_op jit(solution)/shard_map/all_to_all | solution.py:354
  17.7 0.9 %copy-start = (s32[256,256]{1,0:T(8,128)S(1)}, s32[256,256]{1,0:T(8,128)}, u32[]{:S(2)}) copy-start(s32[256,256]{1,0:T(8,128)} %tile_map.1) | copy-start | bytes 786436
  24.9 1.5 %collective-permute-start.4 = (f32[8,64,128]{2,1,0:T(8,128)S(1)}, f32[8,64,128]{2,1,0:T(8,128)S(1)}, u32[]{:S(2)}, u32[]{:S(2)}) collective-permute-start(f32[8,64,128]{2,1,0:T(8,128)S(1)} %all-to-all-done.mine), channel_id=1, source_target_pairs={{0,1},{1,0},{2,3},{3,2},{4,5},{5,4},{6,7},{7,6},{8,9},{9,8},{10,11... | collective-permute-start | bytes 786440 | tf_op jit(solution)/shard_map/ppermute | solution.py:346
  56.6 3.6 %collective-permute-start.5 = (f32[8,32,128]{2,1,0:T(8,128)S(1)}, f32[8,32,128]{2,1,0:T(8,128)S(1)}, u32[]{:S(2)}, u32[]{:S(2)}) collective-permute-start(f32[8,32,128]{2,1,0:T(8,128)S(1)} %all_to_all.26.gathered), channel_id=1, source_target_pairs={{0,1},{1,0},{2,3},{3,2},{4,5},{5,4},{6,7},{7,6},{8,9},{9,8},{10,11... | collective-permute-start | bytes 393224 | tf_op jit(solution)/shard_map/ppermute | solution.py:346
  72.2 2.4 %collective-permute-start.6 = (f32[8,128]{1,0:T(8,128)S(1)}, f32[8,128]{1,0:T(8,128)S(1)}, u32[]{:S(2)}, u32[]{:S(2)}) collective-permute-start(f32[8,128]{1,0:T(8,128)S(1)} %get-tuple-element.42.sums), channel_id=1, source_target_pairs={{0,1},{1,0},{2,3},{3,2},{4,5},{5,4},{6,7},{7,6},{8,9},{9,8},{10,11... | collective-permute-start | bytes 12296 | tf_op jit(solution)/shard_map/ppermute | solution.py:346
